TPU v7x, 256 devices: a whole 4x4x8 slice. The times are simulated.
256 devices in a mesh: phase: 8 (over x, core), seq: 32 (over z, y).
Axes of the slice: x: 4, y: 4, z: 8, core: 2. Of those that a mesh axis runs over, the one named last changes fastest.
Arguments:
- patches: bfloat16 [8192, 1024], P('seq'), may hold values from -6 to 6
- ln_gain: float32 [1024], replicated, may hold values from 0.1 to 1.9
- kv_proj: bfloat16 [1024, 2, 3072], P(None, None, 'phase'), may hold values from -0.1875 to 0.1875
- query: bfloat16 [5120, 3072], P('seq', 'phase'), may hold values from -128 to 128
- text_kv: bfloat16 [2, 5120, 3072], P(None, 'seq', 'phase'), may hold values from -128 to 128
- type_bias: bfloat16 [2, 3072], P(None, 'phase'), may hold values from -3 to 3
- d_out: bfloat16 [5120, 3072], P('seq', 'phase'), may hold values from -6 to 6
- patch_counts: int32 [32], replicated, may hold values from 1 to 64, as said below
- image_offsets: int32 [32], replicated, may hold values from 0 to 5119, as said below
- token_types: int32 [5120], P('seq'), may hold values from 0 to 1
- segment_ids: int32 [5120], replicated, may hold values from 0 to 15, never falling along the last dimension, each value on 1 to 2720 neighbouring positions
Outputs:
- attended: bfloat16 [5120, 3072], P('seq', 'phase')
- d_query: bfloat16 [5120, 3072], P('seq', 'phase')
- d_text_kv: bfloat16 [2, 5120, 3072], P(None, 'seq', 'phase')
- d_kv_proj: float32 [1024, 2, 3072], P('seq', None, 'phase')
- d_patches: bfloat16 [8192, 1024], P('seq')
Inputs may be any that keep to these rules, and one draw needn't show every extreme that they name: `patch_counts`: some image has exactly 64 real rows. Image f takes the positions image_offsets[f] to image_offsets[f] + patch_counts[f] - 1; these runs are disjoint, and each lies within one block of 160 positions starting at a multiple of 160. `segment_ids`: ids never fall along the sequence; each episode is a run of at most 2720 positions.
All inputs are finite; a program needn't handle non-finite values.
Results may differ from a plain program's by a relative error of at most 0.03.
The roundings to bfloat16 on the way count: a program that leaves them out, or rounds other values in their place, can miss the bound.
Values may be sent and summed in bfloat16 or wider, within the bound.
No kernel may reach another device: no remote copies, remote signals or barrier semaphores. Data moves between devices by JAX's collectives and lax.ppermute only.
A program may use at most 128 MiB of HBM per device.

v0:
```python
import math

import jax
import jax.numpy as jnp
from jax import lax
from jax.sharding import PartitionSpec as P

HD = 128
PAD = 256
PATCH_MOST = 64


EPSILON = 1e-05
NEGATIVE = -1e30


def normalize_rows(patches):
    row_values = patches.astype(jnp.float32)
    center = row_values - jnp.mean(row_values, axis=-1, keepdims=True)
    inverse = lax.rsqrt(jnp.mean(center * center, axis=-1, keepdims=True) + EPSILON)
    return (center * inverse, inverse)


def shards(
    patches,
    ln_gain,
    kv_proj,
    query,
    text_kv,
    type_bias,
    d_out,
    patch_counts,
    image_offsets,
    token_types,
    segment_ids,
):
    tok_rows = query.shape[0]
    head_cols = query.shape[1]
    head_count = head_cols // HD
    enc_width = patches.shape[1]
    frames_here = patches.shape[0] // PAD
    seq_index = lax.axis_index("seq")
    score_scale_factor = 1.0 / math.sqrt(HD)
    used_rows = patches.reshape(frames_here, PAD, enc_width)[:, :PATCH_MOST].reshape(
        frames_here * PATCH_MOST, enc_width
    )
    scaled, inverse = normalize_rows(used_rows)
    normed = (scaled * ln_gain).astype(jnp.bfloat16)
    proj_matrix = kv_proj.reshape(enc_width, 2 * head_cols)
    positions = seq_index * tok_rows + jnp.arange(tok_rows, dtype=jnp.int32)
    frame_ids = jnp.arange(patch_counts.shape[0], dtype=jnp.int32)
    inside = (positions[:, None] >= image_offsets[None, :]) & (
        positions[:, None] < image_offsets[None, :] + patch_counts[None, :]
    )
    is_image = jnp.any(inside, axis=1)
    frame_of = jnp.sum(jnp.where(inside, frame_ids[None, :], 0), axis=1)
    row_of = positions - jnp.sum(jnp.where(inside, image_offsets[None, :], 0), axis=1)
    source = frame_of * PATCH_MOST + row_of
    image_kv = jnp.dot(normed, proj_matrix, preferred_element_type=jnp.float32).astype(jnp.bfloat16)
    shard_piece = lax.all_gather(image_kv, "seq", axis=0, tiled=True)
    local_ids = source
    column_ids = jnp.arange(shard_piece.shape[0], dtype=jnp.int32)
    one_hot = ((local_ids[:, None] == column_ids[None, :]) & is_image[:, None]).astype(jnp.bfloat16)
    routed = jnp.dot(one_hot, shard_piece, preferred_element_type=jnp.float32).astype(jnp.bfloat16)
    bias_rows = jnp.where(
        token_types[:, None] == 1,
        type_bias[1].astype(jnp.float32)[None, :],
        type_bias[0].astype(jnp.float32)[None, :],
    )
    text_keys = (text_kv[0].astype(jnp.float32) + bias_rows).astype(jnp.bfloat16)
    keys_here = jnp.where(is_image[:, None], routed[:, :head_cols], text_keys)
    values_here = jnp.where(is_image[:, None], routed[:, head_cols:], text_kv[1])
    key_all, value_all = (
        lax.all_gather(keys_here, "seq", axis=0, tiled=True),
        lax.all_gather(values_here, "seq", axis=0, tiled=True),
    )
    key_count = key_all.shape[0]
    key_pos = jnp.arange(key_count, dtype=jnp.int32)
    key_segs = jnp.take(segment_ids, jnp.clip(key_pos, 0, segment_ids.shape[0] - 1))
    query_segs = jnp.take(segment_ids, positions)
    allowed = (
        (query_segs[:, None] == key_segs[None, :])
        & (key_pos[None, :] <= positions[:, None])
        & (key_pos[None, :] >= 0)
    )
    query_heads = query.reshape(tok_rows, head_count, HD)
    key_heads = key_all.reshape(key_count, head_count, HD)
    value_heads = value_all.reshape(key_count, head_count, HD)
    score = (
        jnp.einsum("qhd,khd->hqk", query_heads, key_heads, preferred_element_type=jnp.float32)
        * score_scale_factor
    )
    score = jnp.where(allowed[None, :, :], score, NEGATIVE)
    row_max = jnp.max(score, axis=2, keepdims=True)
    weights = jnp.exp(score - row_max)
    prob_full = weights / jnp.sum(weights, axis=2, keepdims=True)
    prob_low = prob_full.astype(jnp.bfloat16)
    attended = jnp.einsum(
        "hqk,khd->qhd", prob_low, value_heads, preferred_element_type=jnp.float32
    ).astype(jnp.bfloat16)
    grad_heads = d_out.reshape(tok_rows, head_count, HD)
    d_prob = jnp.einsum("qhd,khd->hqk", grad_heads, value_heads, preferred_element_type=jnp.float32)
    delta = jnp.sum(grad_heads.astype(jnp.float32) * attended.astype(jnp.float32), axis=2)
    d_score = (prob_full * (d_prob - jnp.transpose(delta)[:, :, None])).astype(jnp.bfloat16)
    d_query = (
        jnp.einsum("hqk,khd->qhd", d_score, key_heads, preferred_element_type=jnp.float32)
        * score_scale_factor
    ).astype(jnp.bfloat16)
    grad_keys = (
        jnp.einsum("hqk,qhd->khd", d_score, query_heads, preferred_element_type=jnp.float32)
        * score_scale_factor
    )
    grad_values = jnp.einsum(
        "hqk,qhd->khd", prob_low, grad_heads, preferred_element_type=jnp.float32
    )
    summed = lax.psum_scatter(
        jnp.concatenate(
            [
                grad_keys.reshape(lax.axis_size("seq") * tok_rows, head_cols),
                grad_values.reshape(lax.axis_size("seq") * tok_rows, head_cols),
            ],
            axis=1,
        ).astype(jnp.bfloat16),
        "seq",
        scatter_dimension=0,
        tiled=True,
    )
    zero_rows = jnp.zeros_like(summed)
    text_grads = jnp.where(is_image[:, None], zero_rows, summed)
    d_text_kv = jnp.stack([text_grads[:, :head_cols], text_grads[:, head_cols:]], axis=0)
    image_terms = jnp.where(is_image[:, None], summed, zero_rows)
    my_starts = lax.dynamic_slice_in_dim(image_offsets, seq_index * frames_here, frames_here)
    my_counts = lax.dynamic_slice_in_dim(patch_counts, seq_index * frames_here, frames_here)
    row_ids = jnp.arange(PATCH_MOST, dtype=jnp.int32)
    target = (my_starts[:, None] + row_ids[None, :]).reshape(-1)
    live_rows = (row_ids[None, :] < my_counts[:, None]).reshape(-1)
    shard_piece = lax.all_gather(image_terms, "seq", axis=0, tiled=True)
    local_ids = target
    column_ids = jnp.arange(shard_piece.shape[0], dtype=jnp.int32)
    one_hot = ((local_ids[:, None] == column_ids[None, :]) & live_rows[:, None]).astype(
        jnp.bfloat16
    )
    d_image = jnp.dot(one_hot, shard_piece, preferred_element_type=jnp.float32).astype(jnp.bfloat16)
    d_kv_proj = (
        lax.psum_scatter(
            lax.dot_general(
                normed, d_image, (((0,), (0,)), ((), ())), preferred_element_type=jnp.float32
            ).astype(jnp.bfloat16),
            "seq",
            scatter_dimension=0,
            tiled=True,
        )
        .astype(jnp.float32)
        .reshape(-1, 2, head_cols)
    )
    partial_grad = lax.dot_general(
        d_image, proj_matrix, (((1,), (1,)), ((), ())), preferred_element_type=jnp.float32
    )
    d_normed = lax.psum(partial_grad.astype(jnp.bfloat16), "phase").astype(jnp.float32)
    scaled_grad = d_normed * ln_gain
    d_rows = (
        scaled_grad
        - jnp.mean(scaled_grad, axis=-1, keepdims=True)
        - scaled * jnp.mean(scaled_grad * scaled, axis=-1, keepdims=True)
    ) * inverse
    padded_rows = jnp.pad(
        d_rows.reshape(frames_here, PATCH_MOST, enc_width), ((0, 0), (0, PAD - PATCH_MOST), (0, 0))
    )
    d_patches = padded_rows.reshape(frames_here * PAD, enc_width).astype(jnp.bfloat16)
    return (
        attended.reshape(tok_rows, head_cols),
        d_query.reshape(tok_rows, head_cols),
        d_text_kv,
        d_kv_proj,
        d_patches,
    )


def solution(mesh):
    placed = (
        P("seq", None),
        P(),
        P(None, None, "phase"),
        P("seq", "phase"),
        P(None, "seq", "phase"),
        P(None, "phase"),
        P("seq", "phase"),
        P(),
        P(),
        P("seq"),
        P(),
    )
    return jax.shard_map(
        shards,
        mesh=mesh,
        in_specs=placed,
        out_specs=(
            P("seq", "phase"),
            P("seq", "phase"),
            P(None, "seq", "phase"),
            P("seq", None, "phase"),
            P("seq", None),
        ),
        check_vma=False,
    )
```

profile of v0, /device:TPU:1, one launch (start us, length us, event | category | flops | bytes accessed | tf_op | source)
XLA Modules:
  0.0 916.0 jit_solution(14521765599714900002)
XLA Ops:
  9.6 1.7 copy.62
  11.3 2.0 convolution_convert_fusion.4
  13.7 79.6 %all-gather.5.cloned.1.call-done = bf16[2048,768]{1,0:T(8,128)(2,1)} async-done(((bf16[64,768]{1,0:T(8,128)(2,1)}), bf16[2048,768]{1,0:T(8,128)(2,1)}) %all-gather.5.cloned.1.call-update) | async-done | bytes 3145744 | tf_op jit(solution)/shard_map/all_gather | solution.py:60
  93.3 2.7 fusion.14
  97.6 1.4 gather_fusion
  99.1 28.7 %gather_fusion.1 = s32[5120]{0:T(1024)S(1)} fusion(s32[5120]{0:T(1024)S(1)} %copy-done.2, s32[5120]{0:T(1024)S(1)} %broadcast_clamp_fusion), kind=kCustom, calls=%fused_computation.1 | custom fusion | bytes 61440 | tf_op jit(solution)/shard_map/jit(_take)/gather | solution.py:79
  128.6 47.5 %all-gather.9.cloned.1.call-done = bf16[5120,384]{1,0:T(8,128)(2,1)} async-done(((bf16[160,384]{1,0:T(8,128)(2,1)}), bf16[5120,384]{1,0:T(8,128)(2,1)}) %all-gather.9.cloned.1.call-update) | async-done | bytes 3932176 | tf_op jit(solution)/shard_map/all_gather | solution.py:74
  176.1 6.2 copy.40
  182.3 3.5 fusion.57
  185.8 3.6 fusion.72
  189.5 1.6 fusion.6
  191.0 2.2 copy-done.4
  193.3 2.3 copy-done.3
  195.6 3.2 convolution_convert_fusion
  198.7 58.8 %all-gather.7.cloned.1.call-done = bf16[5120,384]{1,0:T(8,128)(2,1)} async-done(((bf16[160,384]{1,0:T(8,128)(2,1)}), bf16[5120,384]{1,0:T(8,128)(2,1)}) %all-gather.7.cloned.1.call-update) | async-done | bytes 3932176 | tf_op jit(solution)/shard_map/all_gather | solution.py:75
  257.6 6.2 copy.39
  263.7 5.3 multiply_reduce_fusion
  270.1 5.8 fusion.1
  275.9 5.5 multiply_convert_fusion
  281.4 6.3 copy.52
  287.7 6.3 copy.53
  294.0 7.0 pad_maximum_fusion
  301.1 223.5 %reduce-scatter.3.cloned.1.call-done = bf16[160,768]{1,0:T(8,128)(2,1)} async-done(((bf16[5120,768]{1,0:T(8,128)(2,1)}), bf16[160,768]{1,0:T(8,128)(2,1)}) %reduce-scatter.3.cloned.1.call-update) | async-done | bytes 245776 | tf_op jit(solution)/shard_map/reduce_scatter | solution.py:116
  524.6 1.7 broadcast_select_fusion
  528.9 96.4 %all-gather.11.cloned.1.call-done = bf16[5120,768]{1,0:T(8,128)(2,1)} async-done(((bf16[160,768]{1,0:T(8,128)(2,1)}), bf16[5120,768]{1,0:T(8,128)(2,1)}) %all-gather.11.cloned.1.call-update) | async-done | bytes 7864336 | tf_op jit(solution)/shard_map/all_gather | solution.py:137
  625.3 4.8 fusion.18
  630.1 1.3 convolution_convert_fusion.2
  631.5 1.9 convolution_convert_fusion.1
  633.4 5.1 fusion.21
  639.9 51.4 %all-reduce.3.cloned.1.call-done = bf16[64,1024]{1,0:T(8,128)(2,1)} async-done(((bf16[64,1024]{1,0:T(8,128)(2,1)}), bf16[64,1024]{1,0:T(8,128)(2,1)}) %all-reduce.3.cloned.1.call-update) | async-done | bytes 131088 | tf_op jit(solution)/shard_map/psum | solution.py:159
  694.3 213.4 %reduce-scatter.5.cloned.1.call-done = bf16[32,768]{1,0:T(8,128)(2,1)} async-done(((bf16[1024,768]{1,0:T(8,128)(2,1)}), bf16[32,768]{1,0:T(8,128)(2,1)}) %reduce-scatter.5.cloned.1.call-update) | async-done | bytes 49168 | tf_op jit(solution)/shard_map/reduce_scatter | solution.py:145
  907.7 1.5 reshape.268
  (70 shorter events, 13.3 us)
Async XLA Ops:
  7.2 188.4 %copy-start = (bf16[160,384]{1,0:T(8,128)(2,1)S(1)}, bf16[160,384]{1,0:T(8,128)(2,1)}, u32[]{:S(2)}) copy-start(bf16[160,384]{1,0:T(8,128)(2,1)} %param.17) | copy-start | bytes 368644
  7.2 6.2 copy-start.13
  7.2 6.2 copy-start.11
  7.2 6.2 copy-start.10
  7.2 6.4 copy-start.12
  7.2 88.7 %copy-start.8 = (bf16[2,160,384]{2,1,0:T(8,128)(2,1)S(1)}, bf16[2,160,384]{2,1,0:T(8,128)(2,1)}, u32[]{:S(2)}) copy-start(bf16[2,160,384]{2,1,0:T(8,128)(2,1)} %param.15) | copy-start | bytes 737284
  7.2 86.0 %all-gather.5.cloned.1.call-start = ((), (), s32[]{:S(2)}) async-start(), calls=%async_computation.2 | async-start | bytes 3244032 | tf_op jit(solution)/shard_map/all_gather | solution.py:60
  9.6 88.1 %copy-start.2 = (s32[5120]{0:T(1024)S(1)}, s32[5120]{0:T(1024)}, u32[]{:S(2)}) copy-start(s32[5120]{0:T(1024)} %param.21) | copy-start | bytes 61444
  13.3 162.7 %all-gather.9.cloned.1.call-start = ((), (), s32[]{:S(2)}) async-start(), calls=%async_computation.4 | async-start | bytes 4055040 | tf_op jit(solution)/shard_map/all_gather | solution.py:74
  96.8 160.7 %all-gather.7.cloned.1.call-start = ((), (), s32[]{:S(2)}) async-start(), calls=%async_computation.3 | async-start | bytes 4055040 | tf_op jit(solution)/shard_map/all_gather | solution.py:75
  97.6 427.1 %reduce-scatter.3.cloned.1.call-start = ((), (), s32[]{:S(2)}) async-start(), calls=%async_computation.5 | async-start | bytes 8110080 | tf_op jit(solution)/shard_map/reduce_scatter | solution.py:116
  127.8 54.5 %copy-start.7 = (bf16[160,384]{1,0:T(8,128)(2,1)S(1)}, bf16[160,384]{1,0:T(8,128)(2,1)}, u32[]{:S(2)}) copy-start(bf16[160,384]{1,0:T(8,128)(2,1)} %param.14) | copy-start | bytes 368644
  189.4 3.8 copy-start.4
  193.3 2.3 copy-start.3
  263.7 6.4 copy-start.5
  301.1 324.3 %all-gather.11.cloned.1.call-start = ((), (), s32[]{:S(2)}) async-start(), calls=%async_computation.6 | async-start | bytes 8110080 | tf_op jit(solution)/shard_map/all_gather | solution.py:137
  526.4 164.9 %all-reduce.3.cloned.1.call-start = ((), (), s32[]{:S(2)}) async-start(), calls=%async_computation.8 | async-start | bytes 262144 | tf_op jit(solution)/shard_map/psum | solution.py:159
  528.9 102.5 %copy-start.6 = (bf16[256,1024]{1,0:T(8,128)(2,1)S(1)}, bf16[256,1024]{1,0:T(8,128)(2,1)}, u32[]{:S(2)}) copy-start(bf16[256,1024]{1,0:T(8,128)(2,1)} %param.11) | copy-start | bytes 1572868
  528.9 102.5 %copy-start.9 = (f32[1024]{0:T(1024)S(1)}, f32[1024]{0:T(1024)}, u32[]{:S(2)}) copy-start(f32[1024]{0:T(1024)} %param.12) | copy-start | bytes 12292
  631.4 276.3 %reduce-scatter.5.cloned.1.call-start = ((), (), s32[]{:S(2)}) async-start(), calls=%async_computation.7 | async-start | bytes 1622016 | tf_op jit(solution)/shard_map/reduce_scatter | solution.py:145
  633.3 275.9 %copy-start.1 = (bf16[160,384]{1,0:T(8,128)(2,1)S(1)}, bf16[160,384]{1,0:T(8,128)(2,1)}, u32[]{:S(2)}) copy-start(bf16[160,384]{1,0:T(8,128)(2,1)} %param.17) | copy-start | bytes 368644
Sparse Core Ops, SparseCore 0:
  13.5 79.7 all-gather.4
  96.9 79.0 all-gather.8
  179.2 78.2 all-gather.6
  301.2 223.3 reduce-scatter.2
  528.0 97.3 all-gather.10
  631.5 59.6 all-reduce.2
  695.1 212.5 reduce-scatter.4
where the time goes:
time: 921 us; the launch traced here: 916 us
  waiting for transfers between devices  771 us (84%)
  local copies, waits for them, and re-layouts  66.8 us (7%)
  matrix products  40.9 us (4%)
  other arithmetic  22.2 us (2%)
  between operations  14.5 us (2%)
    reduce_scatter x1, waiting for transfers between devices, shards(): lax.psum_scatter(jnp.concatenate([grad_keys.reshape(lax.axis_size('seq')...  224 us
    reduce_scatter x1, waiting for transfers between devices, shards(): lax.psum_scatter(lax.dot_general(normed, d_image, (((0,), (0,)), ((), ())...  213 us
    all_gather x1, waiting for transfers between devices, shards(): shard_piece = lax.all_gather(image_terms, 'seq', axis=0, tiled=True)  96.4 us
    all_gather x1, waiting for transfers between devices, shards(): shard_piece = lax.all_gather(image_kv, 'seq', axis=0, tiled=True)  79.6 us
    all_gather x1, waiting for transfers between devices, shards(): lax.all_gather(values_here, 'seq', axis=0, tiled=True)  58.8 us
    psum x1, waiting for transfers between devices, shards(): lax.psum(partial_grad.astype(jnp.bfloat16), 'phase').astype(jnp.float32)  51.4 us
    all_gather x1, waiting for transfers between devices, shards(): lax.all_gather(keys_here, 'seq', axis=0, tiled=True)  47.5 us
    gather x1, local copies, waits for them, and re-layouts, shards(): jnp.take(segment_ids, jnp.clip(key_pos, 0, segment_ids.shape[0] - 1))  28.7 us
  transfers between devices with their start and end apart: 7, of which 7 were waited for; matrix products, arithmetic and copies ran while one was open for 7% of the time, Pallas kernels for 0%

commit v1 on v0

v1 whole, which is shorter than its diff:
```python
import math

import jax
import jax.numpy as jnp
from jax import lax
from jax.experimental import pallas as pl
from jax.experimental.pallas import tpu as pltpu
from jax.sharding import Mesh
from jax.sharding import PartitionSpec as P

HD = 128
PAD = 256
PATCH_MOST = 64
EPISODES = 16
EPISODE_MOST = 2720
EPSILON = 1e-05
NEGATIVE = -1e30
CHUNK = 256

F32 = jnp.float32
BF16 = jnp.bfloat16


def dot_nt(a, b):
    return lax.dot_general(a, b, (((1,), (1,)), ((), ())), preferred_element_type=F32)


def dot_tn(a, b):
    return lax.dot_general(a, b, (((0,), (0,)), ((), ())), preferred_element_type=F32)


def dot_nn(a, b):
    return jnp.dot(a, b, preferred_element_type=F32)


def normalize_rows(patches):
    row_values = patches.astype(F32)
    center = row_values - jnp.mean(row_values, axis=-1, keepdims=True)
    inverse = lax.rsqrt(jnp.mean(center * center, axis=-1, keepdims=True) + EPSILON)
    return (center * inverse, inverse)


def vmem(limit=48):
    return pltpu.CompilerParams(vmem_limit_bytes=limit * 1024 * 1024)


def pack_kernel(heads, tok, patch_ref, gain_ref, proj_ref, q_ref, kv_ref, bias_ref, do_ref, type_ref,
                out_ref, normed_ref):
    scaled, _ = normalize_rows(patch_ref[...])
    normed = (scaled * gain_ref[...]).astype(BF16)
    normed_ref[...] = normed
    image = dot_nn(normed, proj_ref[...]).astype(BF16)
    cols = heads * HD
    bias = jnp.where(type_ref[...] == 1, bias_ref[1:2].astype(F32), bias_ref[0:1].astype(F32))
    keys = (kv_ref[0].astype(F32) + bias).astype(BF16)
    for h in range(heads):
        span = slice(h * HD, (h + 1) * HD)
        out_ref[h, 0:tok] = keys[:, span]
        out_ref[h, tok : 2 * tok] = kv_ref[1, :, span]
        out_ref[h, 2 * tok : 3 * tok] = q_ref[:, span]
        out_ref[h, 3 * tok : 4 * tok] = do_ref[:, span]
        out_ref[h, 4 * tok : 4 * tok + PATCH_MOST] = image[:, span]
        out_ref[h, 4 * tok + PATCH_MOST :] = image[:, cols + h * HD : cols + (h + 1) * HD]
    for h in range(heads, out_ref.shape[0]):
        out_ref[h] = jnp.zeros_like(out_ref[h])


def place_kernel(frames, meta_ref, rows_ref, out_ref, scratch):
    group = out_ref.shape[0]
    first = meta_ref[2 * frames] * group
    scratch[...] = jnp.zeros_like(scratch)
    row = lax.broadcasted_iota(jnp.int32, (PATCH_MOST, HD), 0)

    def one(f, carry):
        offset = meta_ref[f] - first

        @pl.when((offset >= 0) & (offset < group))
        def _():
            where = pl.ds(offset, PATCH_MOST)
            scratch[where] = jnp.where(
                row < meta_ref[frames + f], rows_ref[f].astype(F32), scratch[where]
            )

        return carry

    lax.fori_loop(0, frames, one, 0)
    out_ref[...] = scratch[0:group].astype(BF16)


def query_kernel(frames, tok, meta_ref, start_ref, g_ref, att_ref, dq_ref, own_ref, stat_ref,
                 kf, vf, kb, vb, qb, dob, s_ref, m_ref, l_ref, acc):
    group = att_ref.shape[0]
    total = kb.shape[0]
    scale = 1.0 / math.sqrt(HD)
    power = scale * math.log2(math.e)
    z = meta_ref[2 * frames]
    first_chunk = meta_ref[2 * frames + 2]
    last_chunk = meta_ref[2 * frames + 3]
    image_row = 4 * tok

    def text(b, carry):
        where = pl.ds(pl.multiple_of(b * tok, 32), tok)
        kf[where] = g_ref[b, 0:tok].astype(F32)
        vf[where] = g_ref[b, tok : 2 * tok].astype(F32)
        return carry

    lax.fori_loop(0, total // tok, text, 0)
    row = lax.broadcasted_iota(jnp.int32, (PATCH_MOST, HD), 0)

    def image(f, carry):
        where = pl.ds(meta_ref[f], PATCH_MOST)
        live = row < meta_ref[frames + f]
        kf[where] = jnp.where(live, g_ref[f, image_row : image_row + PATCH_MOST].astype(F32), kf[where])
        vf[where] = jnp.where(live, g_ref[f, image_row + PATCH_MOST :].astype(F32), vf[where])
        return carry

    lax.fori_loop(0, frames, image, 0)

    def low(c, carry):
        where = pl.ds(pl.multiple_of(c * CHUNK, CHUNK), CHUNK)
        kb[where] = kf[where].astype(BF16)
        vb[where] = vf[where].astype(BF16)
        return carry

    lax.fori_loop(0, total // CHUNK, low, 0)
    per = group // tok
    for i in range(per):
        qb[i * tok : (i + 1) * tok] = g_ref[z * per + i, 2 * tok : 3 * tok]
        dob[i * tok : (i + 1) * tok] = g_ref[z * per + i, 3 * tok : 4 * tok]
    own = pl.ds(pl.multiple_of(z * group, HD), group)
    own_ref[0] = kb[own]
    own_ref[1] = vb[own]

    m_ref[...] = jnp.full_like(m_ref, NEGATIVE)
    l_ref[...] = jnp.zeros_like(l_ref)
    acc[...] = jnp.zeros_like(acc)
    lane = lax.broadcasted_iota(jnp.int32, (group, CHUNK), 1)
    query_pos = z * group + lax.broadcasted_iota(jnp.int32, (group, 1), 0)
    start = start_ref[...]

    def chunk(c):
        return pl.ds(pl.multiple_of(c * CHUNK, CHUNK), CHUNK)

    def scores(c, carry):
        s = dot_nt(qb[...], kb[chunk(c)])
        pos = lane + c * CHUNK
        s = jnp.where((pos >= start) & (pos <= query_pos), s, NEGATIVE)
        s_ref[c - first_chunk] = s
        m_ref[...] = jnp.maximum(m_ref[...], jnp.maximum(s[:, :HD], s[:, HD:]))
        return carry

    lax.fori_loop(first_chunk, last_chunk, scores, 0)
    row_max = jnp.max(m_ref[...], axis=1, keepdims=True)
    m_ref[...] = jnp.broadcast_to(row_max, m_ref.shape)

    def weigh(c, carry):
        top = m_ref[...]
        w = jnp.exp2((s_ref[c - first_chunk] - jnp.concatenate([top, top], axis=1)) * power)
        s_ref[c - first_chunk] = w
        l_ref[...] += w[:, :HD] + w[:, HD:]
        acc[...] += dot_nn(w.astype(BF16), vb[chunk(c)])
        return carry

    lax.fori_loop(first_chunk, last_chunk, weigh, 0)
    inverse_sum = 1.0 / jnp.sum(l_ref[...], axis=1, keepdims=True)
    attended = (acc[...] * inverse_sum).astype(BF16)
    att_ref[...] = attended
    delta = jnp.sum(dob[...].astype(F32) * attended.astype(F32), axis=1, keepdims=True)
    acc[...] = jnp.zeros_like(acc)
    m_ref[...] = jnp.broadcast_to(inverse_sum, m_ref.shape)
    l_ref[...] = jnp.broadcast_to(delta, l_ref.shape)

    def back(c, carry):
        d_prob = dot_nt(dob[...], vb[chunk(c)])
        inv, dlt = m_ref[...], l_ref[...]
        p = s_ref[c - first_chunk] * jnp.concatenate([inv, inv], axis=1)
        d_score = (p * (d_prob - jnp.concatenate([dlt, dlt], axis=1))).astype(BF16)
        acc[...] += dot_nn(d_score, kb[chunk(c)])
        return carry

    lax.fori_loop(first_chunk, last_chunk, back, 0)
    dq_ref[...] = (acc[...] * scale).astype(BF16)
    which = lax.broadcasted_iota(jnp.int32, (group, HD), 1)
    table = jnp.where(which == 0, row_max, jnp.where(which == 1, inverse_sum, delta))
    for i in range(group // HD):
        stat_ref[i] = jnp.transpose(table[i * HD : (i + 1) * HD])[0:8]


def key_kernel(frames, tok, meta_ref, end_ref, g_ref, stat_ref, own_ref, norm_ref, dkv_ref, part_ref,
               qb, dob, dk, dv):
    group = own_ref.shape[1]
    total = qb.shape[0]
    scale = 1.0 / math.sqrt(HD)
    power = scale * math.log2(math.e)
    z = meta_ref[2 * frames]

    def text(b, carry):
        where = pl.ds(pl.multiple_of(b * tok, 32), tok)
        qb[where] = g_ref[b, 2 * tok : 3 * tok]
        dob[where] = g_ref[b, 3 * tok : 4 * tok]
        return carry

    lax.fori_loop(0, total // tok, text, 0)
    dk[...] = jnp.zeros_like(dk)
    dv[...] = jnp.zeros_like(dv)
    lane = lax.broadcasted_iota(jnp.int32, (group, CHUNK), 1)
    key_pos = z * group + lax.broadcasted_iota(jnp.int32, (group, 1), 0)
    end = end_ref[...]

    def step(c, carry):
        where = pl.ds(pl.multiple_of(c * CHUNK, CHUNK), CHUNK)
        stat = jnp.concatenate([stat_ref[2 * c], stat_ref[2 * c + 1]], axis=1)
        q, do = qb[where], dob[where]
        s = dot_nt(own_ref[0], q)
        pos = lane + c * CHUNK
        p = jnp.exp2((s - stat[0:1]) * power) * stat[1:2]
        p = jnp.where((pos >= key_pos) & (pos < end), p, 0.0)
        dv[...] += dot_nn(p.astype(BF16), do)
        d_prob = dot_nt(own_ref[1], do)
        d_score = (p * (d_prob - stat[2:3])).astype(BF16)
        dk[...] += dot_nn(d_score, q)
        return carry

    lax.fori_loop(meta_ref[2 * frames + 4], meta_ref[2 * frames + 5], step, 0)
    key_grad = (dk[...] * scale).astype(BF16)
    value_grad = dv[...].astype(BF16)
    dkv_ref[0] = key_grad
    dkv_ref[1] = value_grad
    both = jnp.concatenate([key_grad, value_grad], axis=1)
    for i in range(norm_ref.shape[0]):
        part_ref[i] = dot_tn(norm_ref[i], both).astype(BF16)


def unpack_kernel(heads, tok, r_ref, image_ref, proj_ref, att_ref, dq_ref, dtext_ref, dproj_ref, dn_ref):
    cols = heads * HD
    is_image = image_ref[...] == 1
    parts = [None] * (2 * heads)
    rows = dproj_ref.shape[0]
    for h in range(heads):
        span = slice(h * HD, (h + 1) * HD)
        att_ref[:, span] = r_ref[h, 0:tok]
        dq_ref[:, span] = r_ref[h, tok : 2 * tok]
        for c in range(2):
            grad = r_ref[h, (2 + c) * tok : (3 + c) * tok]
            zero = jnp.zeros_like(grad)
            dtext_ref[c, :, span] = jnp.where(is_image, zero, grad)
            parts[c * heads + h] = jnp.where(is_image, grad, zero)
            at = 4 * tok + c * rows
            dproj_ref[:, c * cols + h * HD : c * cols + (h + 1) * HD] = r_ref[h, at : at + rows].astype(F32)
    grads = jnp.concatenate(parts, axis=1)
    for i in range(dn_ref.shape[0]):
        dn_ref[i] = dot_nt(grads, proj_ref[i * HD : (i + 1) * HD]).astype(BF16)


def route_kernel(frames, tok, meta_ref, dn_ref, out_ref, scratch):
    first = meta_ref[2 * frames + 1] * tok
    total = dn_ref[0].astype(F32)
    for i in range(1, dn_ref.shape[0]):
        total = total + dn_ref[i].astype(F32)
    scratch[...] = jnp.zeros_like(scratch)
    scratch[0:tok] = total
    row = lax.broadcasted_iota(jnp.int32, (PATCH_MOST, HD), 0)

    def one(f, carry):
        offset = meta_ref[f] - first
        here = (offset >= 0) & (offset < tok)
        live = jnp.where(here, meta_ref[frames + f], 0)
        rows = scratch[pl.ds(jnp.where(here, offset, 0), PATCH_MOST)]
        out_ref[f] = jnp.where(row < live, rows, 0.0).astype(BF16)
        return carry

    lax.fori_loop(0, frames, one, 0)


def norm_grad_kernel(patch_ref, gain_ref, dn_ref, out_ref):
    scaled, inverse = normalize_rows(patch_ref[...])
    d_normed = jnp.concatenate([dn_ref[i] for i in range(dn_ref.shape[0])], axis=1).astype(F32)
    scaled_grad = d_normed * gain_ref[...]
    d_rows = (
        scaled_grad
        - jnp.mean(scaled_grad, axis=-1, keepdims=True)
        - scaled * jnp.mean(scaled_grad * scaled, axis=-1, keepdims=True)
    ) * inverse
    out_ref[0:PATCH_MOST] = d_rows.astype(BF16)
    out_ref[PATCH_MOST:] = jnp.zeros((out_ref.shape[0] - PATCH_MOST, out_ref.shape[1]), BF16)


def shards(patches, ln_gain, kv_proj, query, text_kv, type_bias, d_out, patch_counts, image_offsets,
           token_types, segment_ids):
    tok, cols = query.shape
    heads = cols // HD
    width = patches.shape[1]
    groups, per, sections = lax.axis_size("z"), lax.axis_size("y"), lax.axis_size("phase")
    frames = patch_counts.shape[0]
    blocks = groups * per
    group = per * tok
    total = blocks * tok
    z, y, section = lax.axis_index("z"), lax.axis_index("y"), lax.axis_index("phase")
    block = z * per + y
    smem = pl.BlockSpec(memory_space=pltpu.SMEM)
    whole = pl.BlockSpec(memory_space=pltpu.VMEM)

    def shape(dims, kind=BF16):
        return jax.ShapeDtypeStruct(dims, kind)

    ids = jnp.arange(EPISODES, dtype=jnp.int32)
    seg_first = jnp.sum((segment_ids[None, :] < ids[:, None]).astype(jnp.int32), axis=1)
    seg_end = jnp.sum((segment_ids[None, :] <= ids[:, None]).astype(jnp.int32), axis=1)
    own_seg = lax.dynamic_slice_in_dim(segment_ids, z * group, group)
    same = own_seg[:, None] == ids[None, :]
    start = jnp.sum(jnp.where(same, seg_first[None, :], 0), axis=1, keepdims=True)
    end = jnp.sum(jnp.where(same, seg_end[None, :], 0), axis=1, keepdims=True)
    scalars = jnp.stack([
        z,
        block,
        start[0, 0] // CHUNK,
        ((z + 1) * group + CHUNK - 1) // CHUNK,
        (z * group) // CHUNK,
        (end[group - 1, 0] + CHUNK - 1) // CHUNK,
    ]).astype(jnp.int32)
    meta = jnp.concatenate([image_offsets, patch_counts, scalars])
    positions = block * tok + jnp.arange(tok, dtype=jnp.int32)
    is_image = jnp.any(
        (positions[:, None] >= image_offsets[None, :])
        & (positions[:, None] < image_offsets[None, :] + patch_counts[None, :]),
        axis=1, keepdims=True,
    ).astype(jnp.int32)

    gain = ln_gain.reshape(1, width)
    proj = kv_proj.reshape(width, 2 * cols)
    used = patches[:PATCH_MOST]
    rows_each = 4 * tok + 2 * PATCH_MOST
    packed, normed = pl.pallas_call(
        lambda *refs: pack_kernel(heads, tok, *refs),
        out_shape=(shape((per, rows_each, HD)), shape((PATCH_MOST, width))),
        in_specs=[whole] * 8,
        out_specs=(whole, whole),
        compiler_params=vmem(),
        name="pack",
    )(used, gain, proj, query, text_kv, type_bias, d_out, token_types.reshape(tok, 1))
    by_head = lax.all_to_all(packed, "y", 0, 0, tiled=True)
    gathered = lax.all_gather(by_head, "z", axis=0, tiled=True)

    mine = lax.dynamic_slice_in_dim(normed, section * HD, HD, axis=1)
    all_frames = lax.all_to_all(
        jnp.broadcast_to(mine[None], (blocks, PATCH_MOST, HD)), ("z", "y"), 0, 0, tiled=True
    )
    placed = pl.pallas_call(
        lambda *refs: place_kernel(frames, *refs),
        out_shape=shape((group, HD)),
        in_specs=[smem, whole],
        out_specs=whole,
        scratch_shapes=[pltpu.VMEM((group + PATCH_MOST, HD), F32)],
        compiler_params=vmem(),
        name="place",
    )(meta, all_frames)
    norm_pos = lax.all_gather(placed, "phase", axis=0, tiled=False)

    most_chunks = (EPISODE_MOST + group + CHUNK - 2) // CHUNK + 1
    attended, d_query, own_kv, stats = pl.pallas_call(
        lambda *refs: query_kernel(frames, tok, *refs),
        out_shape=(
            shape((group, HD)),
            shape((group, HD)),
            shape((2, group, HD)),
            shape((group // HD, 8, HD), F32),
        ),
        in_specs=[smem, whole, whole],
        out_specs=(whole, whole, whole, whole),
        scratch_shapes=[
            pltpu.VMEM((total + PATCH_MOST, HD), F32),
            pltpu.VMEM((total + PATCH_MOST, HD), F32),
            pltpu.VMEM((total, HD), BF16),
            pltpu.VMEM((total, HD), BF16),
            pltpu.VMEM((group, HD), BF16),
            pltpu.VMEM((group, HD), BF16),
            pltpu.VMEM((most_chunks, group, CHUNK), F32),
            pltpu.VMEM((group, HD), F32),
            pltpu.VMEM((group, HD), F32),
            pltpu.VMEM((group, HD), F32),
        ],
        compiler_params=vmem(),
        name="queries",
    )(meta, start, gathered)
    all_stats = lax.all_to_all(
        jnp.broadcast_to(stats[None], (groups,) + stats.shape), "z", 0, 0, tiled=True
    ).reshape(total // HD, 8, HD)

    d_kv, part = pl.pallas_call(
        lambda *refs: key_kernel(frames, tok, *refs),
        out_shape=(shape((2, group, HD)), shape((sections, HD, 2 * HD))),
        in_specs=[smem, whole, whole, whole, whole, whole],
        out_specs=(whole, whole),
        scratch_shapes=[
            pltpu.VMEM((total, HD), BF16),
            pltpu.VMEM((total, HD), BF16),
            pltpu.VMEM((group, HD), F32),
            pltpu.VMEM((group, HD), F32),
        ],
        compiler_params=vmem(),
        name="keys",
    )(meta, end, gathered, all_stats, own_kv, norm_pos)
    proj_terms = lax.all_to_all(part.reshape(groups, width // groups, 2 * HD), "z", 0, 0, tiled=True)
    proj_rows = width // blocks
    proj_sum = (
        jnp.sum(proj_terms.astype(F32), axis=0)
        .astype(BF16)
        .reshape(per, proj_rows, 2, HD)
        .transpose(0, 2, 1, 3)
        .reshape(per, 2 * proj_rows, HD)
    )
    answers = jnp.concatenate(
        [
            attended.reshape(per, tok, HD),
            d_query.reshape(per, tok, HD),
            d_kv[0].reshape(per, tok, HD),
            d_kv[1].reshape(per, tok, HD),
            proj_sum,
        ],
        axis=1,
    )
    returned = lax.all_to_all(answers, "y", 0, 0, tiled=True)
    att_here, dq_here, d_text_kv, d_proj, terms = pl.pallas_call(
        lambda *refs: unpack_kernel(heads, tok, *refs),
        out_shape=(
            shape((tok, cols)),
            shape((tok, cols)),
            shape((2, tok, cols)),
            shape((proj_rows, 2 * cols), F32),
            shape((sections, tok, width // sections)),
        ),
        in_specs=[whole] * 3,
        out_specs=(whole,) * 5,
        compiler_params=vmem(),
        name="unpack",
    )(returned, is_image, proj)

    summed = lax.all_to_all(terms, "phase", 0, 0, tiled=True)
    routed = pl.pallas_call(
        lambda *refs: route_kernel(frames, tok, *refs),
        out_shape=shape((frames, PATCH_MOST, HD)),
        in_specs=[smem, whole],
        out_specs=whole,
        scratch_shapes=[pltpu.VMEM((tok + PATCH_MOST, HD), F32)],
        compiler_params=vmem(),
        name="route",
    )(meta, summed)
    from_blocks = lax.all_to_all(routed, ("z", "y"), 0, 0, tiled=True)
    source = lax.dynamic_index_in_dim(image_offsets, block, keepdims=False) // tok
    d_slice = lax.dynamic_index_in_dim(from_blocks, source, keepdims=False)
    d_normed = lax.all_gather(d_slice, "phase", axis=0, tiled=False)
    d_patches = pl.pallas_call(
        norm_grad_kernel,
        out_shape=shape(patches.shape),
        in_specs=[whole] * 3,
        out_specs=whole,
        compiler_params=vmem(),
        name="norm_grad",
    )(used, gain, d_normed)
    return (
        att_here,
        dq_here,
        d_text_kv,
        d_proj.reshape(proj_rows, 2, cols),
        d_patches,
    )


def solution(mesh):
    sections, seq = mesh.devices.shape
    per = 4
    inner = Mesh(mesh.devices.reshape(sections, seq // per, per), ("phase", "z", "y"))
    seq = ("z", "y")
    return jax.shard_map(
        shards,
        mesh=inner,
        in_specs=(
            P(seq, None),
            P(),
            P(None, None, "phase"),
            P(seq, "phase"),
            P(None, seq, "phase"),
            P(None, "phase"),
            P(seq, "phase"),
            P(),
            P(),
            P(seq),
            P(),
        ),
        out_specs=(
            P(seq, "phase"),
            P(seq, "phase"),
            P(None, seq, "phase"),
            P(seq, None, "phase"),
            P(seq, None),
        ),
        check_vma=False,
    )
```

time: 921 us -> 252 us (0.27)
  waiting for transfers between devices: 771 us -> 109 us
  local copies, waits for them, and re-layouts: 66.8 us -> 12.3 us
  blocking collectives: 0 us -> 46.2 us
  matrix products: 40.9 us -> 0 us
  starting transfers between devices: 0.29 us -> 36.6 us
  Pallas kernels: 0 us -> 25.6 us
  other arithmetic: 22.2 us -> 1.51 us
    reduce_scatter x2 -> x0, waiting for transfers between devices: 437 us -> none  [the longest x1 224 us: shards(): lax.psum_scatter(jnp.concatenate([grad_keys.reshape(lax.axis_size('seq')...]
    all_gather x4 -> x2, waiting for transfers between devices: 282 us -> 61.6 us  [the longest x1 56.2 us: shards(): gathered = lax.all_gather(by_head, 'z', axis=0, tiled=True)]
    psum x1 -> x0, waiting for transfers between devices: 51.4 us -> none  [shards(): lax.psum(partial_grad.astype(jnp.bfloat16), 'phase').astype(jnp.float32)]
    all_to_all x0 -> x5, waiting for transfers between devices: none -> 47.8 us  [the longest x1 13.1 us: shards(): from_blocks = lax.all_to_all(routed, ('z', 'y'), 0, 0, tiled=True)]
    dot_general x11 -> x0, matrix products: 40.9 us -> none  [the longest x2 7.43 us: shards(): jnp.dot(one_hot, shard_piece, preferred_element_type=jnp.float32)]
    all_to_all x0 -> x5, starting transfers between devices: none -> 36.5 us  [the longest x1 14.2 us: shards(): lax.all_to_all(jnp.broadcast_to(stats[None], (groups,) + stats.shape), 'z...]
    all_to_all x0 -> x2, blocking collectives: none -> 31.4 us  [the longest x1 15.9 us: shards(): summed = lax.all_to_all(terms, 'phase', 0, 0, tiled=True)]
    gather x2 -> x0, local copies, waits for them, and re-layouts: 30.1 us -> none  [the longest x1 28.7 us: shards(): jnp.take(segment_ids, jnp.clip(key_pos, 0, segment_ids.shape[0] - 1))]
  transfers between devices with their start and end apart: 7 -> 7, of which waited for: 7 -> 7; matrix products, arithmetic and copies ran while one was open for 7% -> 3% of each run, Pallas kernels for 0% -> 4%
where the time goes in v1:
time: 252 us; the launch traced here: 251 us
  waiting for transfers between devices  109 us (43%)
  blocking collectives  46.2 us (18%)
  starting transfers between devices  36.6 us (15%)
  Pallas kernels  25.6 us (10%)
  between operations  19.6 us (8%)
  local copies, waits for them, and re-layouts  12.3 us (5%)
    all_gather x1, waiting for transfers between devices, shards(): gathered = lax.all_gather(by_head, 'z', axis=0, tiled=True)  56.2 us
    all_to_all x1, blocking collectives, shards(): summed = lax.all_to_all(terms, 'phase', 0, 0, tiled=True)  15.9 us
    all_to_all x1, blocking collectives, shards(): by_head = lax.all_to_all(packed, 'y', 0, 0, tiled=True)  15.5 us
    all_gather x1, blocking collectives, shards(): d_normed = lax.all_gather(d_slice, 'phase', axis=0, tiled=False)  14.8 us
    all_to_all x1, starting transfers between devices, shards(): lax.all_to_all(jnp.broadcast_to(stats[None], (groups,) + stats.shape), 'z...  14.2 us
    all_to_all x1, waiting for transfers between devices, shards(): from_blocks = lax.all_to_all(routed, ('z', 'y'), 0, 0, tiled=True)  13.1 us
    all_to_all x1, waiting for transfers between devices, shards(): lax.all_to_all(part.reshape(groups, width // groups, 2 * HD), 'z', 0, 0,...  12.3 us
    all_to_all x1, waiting for transfers between devices, shards(): lax.all_to_all(jnp.broadcast_to(mine[None], (blocks, PATCH_MOST, HD)), ('...  11.6 us
  transfers between devices with their start and end apart: 7, of which 7 were waited for; matrix products, arithmetic and copies ran while one was open for 3% of the time, Pallas kernels for 4%

profile of v1, /device:TPU:1, one launch (start us, length us, event | category | flops | bytes accessed | tf_op | source)
XLA Modules:
  0.0 251.1 jit_solution(17553306098661281418)
XLA Ops:
  7.3 1.8 copy.31
  9.1 0.9 slice.19.refs_0_.patch_ref
  10.7 15.5 %all_to_all.35 = bf16[4,768,128]{2,1,0:T(8,128)(2,1)} all-to-all(bf16[4,768,128]{2,1,0:T(8,128)(2,1)S(1)} %get-tuple-element.18), channel_id=1, replica_groups=mesh['phase'=8,'z'=8,'y'=4] {'y'}, dimensions={0} | all-to-all | bytes 1572864 | tf_op jit(solution)/shard_map/all_to_all | solution.py:341
  26.3 0.9 broadcast_in_dim.56
  27.2 10.0 %all-to-all-start.2 = ((bf16[32,64,128]{2,1,0:T(8,128)(2,1)}), bf16[32,64,128]{2,1,0:T(8,128)(2,1)S(1)}, u32[]{:S(2)}, u32[]{:S(2)}) async-start(bf16[32,64,128]{2,1,0:T(8,128)(2,1)} %broadcast_in_dim.56), calls=%async_computation.2 | async-start | bytes 1048576 | tf_op jit(solution)/shard_map/all_to_all | solution.py:345
  42.1 11.6 %all-to-all-done.2.refs_1_ = bf16[32,64,128]{2,1,0:T(8,128)(2,1)S(1)} async-done(((bf16[32,64,128]{2,1,0:T(8,128)(2,1)}), bf16[32,64,128]{2,1,0:T(8,128)(2,1)S(1)}, u32[]{:S(2)}, u32[]{:S(2)}) %all-to-all-start.2) | async-done | bytes 524320 | tf_op jit(solution)/shard_map/all_to_all | solution.py:345
  53.7 1.7 place.1
  55.6 56.2 %all-gather.4.cloned.1.call-done.refs_2_ = bf16[32,768,128]{2,1,0:T(8,128)(2,1)} async-done(((bf16[4,768,128]{2,1,0:T(8,128)(2,1)}), bf16[32,768,128]{2,1,0:T(8,128)(2,1)}) %all-gather.4.cloned.1.call-update) | async-done | bytes 6291472 | tf_op jit(solution)/shard_map/all_gather | solution.py:342
  111.8 7.6 %queries.1 = (bf16[640,128]{1,0:T(8,128)(2,1)S(1)}, bf16[640,128]{1,0:T(8,128)(2,1)S(1)}, bf16[2,640,128]{2,1,0:T(8,128)(2,1)S(1)}, f32[5,8,128]{2,1,0:T(8,128)S(1)}) custom-call(s32[70]{0:T(128)S(1)} %concatenate.6.refs_0_, s32[640,1]{1,0:T(8,128)S(1)} %broadcast_in_dim.57.refs_1_, bf16[32,768,128]{2,1,0:T(8,128)(2,1)} %all-gather.4.cloned.1.call-done.refs_2_), custom_call_target="tpu_custom_call" | custom-call | tf_op jit(solution)/shard_map/queries/pallas_call | solution.py:360
  119.4 0.7 broadcast_in_dim.31
  120.1 14.2 %all-to-all-start.1 = ((f32[8,5,8,128]{3,2,1,0:T(8,128)}), f32[8,5,8,128]{3,2,1,0:T(8,128)S(1)}, u32[]{:S(2)}, u32[]{:S(2)}) async-start(f32[8,5,8,128]{3,2,1,0:T(8,128)} %broadcast_in_dim.31), calls=%async_computation.1 | async-start | bytes 327680 | tf_op jit(solution)/shard_map/all_to_all | solution.py:385
  134.4 5.4 %all-gather.6.cloned.1.call-done = bf16[5120,128]{1,0:T(8,128)(2,1)} async-done(((bf16[640,128]{1,0:T(8,128)(2,1)}), bf16[5120,128]{1,0:T(8,128)(2,1)}) %all-gather.6.cloned.1.call-update) | async-done | bytes 1310736 | tf_op jit(solution)/shard_map/all_gather | solution.py:357
  139.8 2.9 %all-to-all-done.1 = f32[8,5,8,128]{3,2,1,0:T(8,128)S(1)} async-done(((f32[8,5,8,128]{3,2,1,0:T(8,128)}), f32[8,5,8,128]{3,2,1,0:T(8,128)S(1)}, u32[]{:S(2)}, u32[]{:S(2)}) %all-to-all-start.1) | async-done | bytes 163872 | tf_op jit(solution)/shard_map/all_to_all | solution.py:385
  142.7 1.3 copy-done
  144.0 11.5 %keys.1 = (bf16[2,640,128]{2,1,0:T(8,128)(2,1)S(1)}, bf16[8,128,256]{2,1,0:T(8,128)(2,1)}) custom-call(s32[70]{0:T(128)S(1)} %concatenate.6.refs_0_, s32[640,1]{1,0:T(8,128)S(1)} %broadcast_in_dim.58.refs_1_, bf16[32,768,128]{2,1,0:T(8,128)(2,1)} %all-gather.4.cloned.1.call-done.refs_2_, f32[40,8,128]{2,1,0:T(8,128)S(1)} %bitcast.26, ...), custom_call_target="tpu_custom_call" | custom-call | tf_op jit(solution)/shard_map/keys/pallas_call | solution.py:389
  155.5 4.2 %all-to-all-start.3 = ((bf16[8,128,256]{2,1,0:T(8,128)(2,1)}), bf16[8,128,256]{2,1,0:T(8,128)(2,1)}, u32[]{:S(2)}, u32[]{:S(2)}) async-start(bf16[8,128,256]{2,1,0:T(8,128)(2,1)} %get-tuple-element.25), calls=%async_computation.3 | async-start | bytes 1048576 | tf_op jit(solution)/shard_map/all_to_all | solution.py:403
  159.7 0.7 constant_dynamic-update-slice_fusion.4
  160.4 0.7 constant_dynamic-update-slice_fusion.3
  161.1 0.7 constant_dynamic-update-slice_fusion.2
  161.8 0.7 constant_dynamic-update-slice_fusion.1
  162.5 12.3 %all-to-all-done.3 = bf16[8,128,256]{2,1,0:T(8,128)(2,1)} async-done(((bf16[8,128,256]{2,1,0:T(8,128)(2,1)}), bf16[8,128,256]{2,1,0:T(8,128)(2,1)}, u32[]{:S(2)}, u32[]{:S(2)}) %all-to-all-start.3) | async-done | bytes 524320 | tf_op jit(solution)/shard_map/all_to_all | solution.py:403
  174.8 1.1 reduce_sum.52
  176.7 4.3 %all-to-all-start.4 = ((bf16[4,704,128]{2,1,0:T(8,128)(2,1)}), bf16[4,704,128]{2,1,0:T(8,128)(2,1)S(1)}, u32[]{:S(2)}, u32[]{:S(2)}) async-start(bf16[4,704,128]{2,1,0:T(8,128)(2,1)} %constant_dynamic-update-slice_fusion), calls=%async_computation.4 | async-start | bytes 1441792 | tf_op jit(solution)/shard_map/all_to_all | solution.py:422
  181.2 7.8 %all-to-all-done.4.refs_0_ = bf16[4,704,128]{2,1,0:T(8,128)(2,1)S(1)} async-done(((bf16[4,704,128]{2,1,0:T(8,128)(2,1)}), bf16[4,704,128]{2,1,0:T(8,128)(2,1)S(1)}, u32[]{:S(2)}, u32[]{:S(2)}) %all-to-all-start.4) | async-done | bytes 720928 | tf_op jit(solution)/shard_map/all_to_all | solution.py:422
  189.0 1.4 unpack.1
  190.4 15.9 %all_to_all.36.refs_1_ = bf16[8,160,128]{2,1,0:T(8,128)(2,1)S(1)} all-to-all(bf16[8,160,128]{2,1,0:T(8,128)(2,1)S(1)} %get-tuple-element.30), channel_id=1, replica_groups=mesh['phase'=8,'z'=8,'y'=4] {'phase'}, dimensions={0} | all-to-all | bytes 655360 | tf_op jit(solution)/shard_map/all_to_all | solution.py:438
  206.3 1.7 route.1
  208.1 3.9 %all-to-all-start.6 = ((bf16[32,64,128]{2,1,0:T(8,128)(2,1)}), bf16[32,64,128]{2,1,0:T(8,128)(2,1)S(1)}, u32[]{:S(2)}, u32[]{:S(2)}) async-start(bf16[32,64,128]{2,1,0:T(8,128)(2,1)} %route.1), calls=%async_computation.6 | async-start | bytes 1048576 | tf_op jit(solution)/shard_map/all_to_all | solution.py:448
  214.5 0.7 reshape.84
  215.2 13.1 %all-to-all-done.6 = bf16[32,64,128]{2,1,0:T(8,128)(2,1)S(1)} async-done(((bf16[32,64,128]{2,1,0:T(8,128)(2,1)}), bf16[32,64,128]{2,1,0:T(8,128)(2,1)S(1)}, u32[]{:S(2)}, u32[]{:S(2)}) %all-to-all-start.6) | async-done | bytes 524320 | tf_op jit(solution)/shard_map/all_to_all | solution.py:448
  228.4 14.8 %all_gather.16.dn_ref = bf16[8,64,128]{2,1,0:T(8,128)(2,1)S(1)} all-gather(bf16[1,64,128]{2,1,0:T(8,128)(2,1)S(1)} %constant_dynamic-slice_fusion.1), channel_id=1, replica_groups=mesh['phase'=8,'z'=8,'y'=4] {'phase'}, dimensions={0}, use_global_device_ids=true | all-gather | bytes 147456 | tf_op jit(solution)/shard_map/all_gather | solution.py:451
  243.2 1.1 norm_grad.1
  (45 shorter events, 4.2 us)
Async XLA Ops:
  7.2 104.6 %all-gather.4.cloned.1.call-start = ((), (), s32[]{:S(2)}) async-start(), calls=%async_computation.7 | async-start | bytes 7077888 | tf_op jit(solution)/shard_map/all_gather | solution.py:342
  7.2 2.8 %copy-start.8 = (s32[160]{0:T(256)S(1)}, s32[160]{0:T(256)}, u32[]{:S(2)}) copy-start(s32[160]{0:T(256)} %param.20) | copy-start | bytes 1924
  7.2 2.9 %copy-start.1 = (bf16[2,160,384]{2,1,0:T(8,128)(2,1)S(1)}, bf16[2,160,384]{2,1,0:T(8,128)(2,1)}, u32[]{:S(2)}) copy-start(bf16[2,160,384]{2,1,0:T(8,128)(2,1)} %refs_4_.1) | copy-start | bytes 737284
  7.2 2.9 %copy-start.2 = (bf16[160,384]{1,0:T(8,128)(2,1)S(1)}, bf16[160,384]{1,0:T(8,128)(2,1)}, u32[]{:S(2)}) copy-start(bf16[160,384]{1,0:T(8,128)(2,1)} %refs_3_.1) | copy-start | bytes 368644
  7.2 2.9 %copy-start.3 = (bf16[160,384]{1,0:T(8,128)(2,1)S(1)}, bf16[160,384]{1,0:T(8,128)(2,1)}, u32[]{:S(2)}) copy-start(bf16[160,384]{1,0:T(8,128)(2,1)} %refs_6_.1) | copy-start | bytes 368644
  7.3 2.9 %copy-start.4 = (f32[1024]{0:T(1024)S(1)}, f32[1024]{0:T(1024)}, u32[]{:S(2)}) copy-start(f32[1024]{0:T(1024)} %param.12) | copy-start | bytes 12292
  7.3 2.9 %copy-start.5 = (bf16[2,384]{1,0:T(2,128)(2,1)S(1)}, bf16[2,384]{1,0:T(2,128)(2,1)}, u32[]{:S(2)}) copy-start(bf16[2,384]{1,0:T(2,128)(2,1)} %refs_5_.1) | copy-start | bytes 4612
  26.2 11.0 %copy-start.6 = (s32[5120]{0:T(1024)S(1)}, s32[5120]{0:T(1024)}, u32[]{:S(2)}) copy-start(s32[5120]{0:T(1024)} %param.21) | copy-start | bytes 61444
  26.2 15.8 %copy-start.7 = (s32[32]{0:T(128)S(1)}, s32[32]{0:T(128)}, u32[]{:S(2)}) copy-start(s32[32]{0:T(128)} %param.19) | copy-start | bytes 388
  26.2 15.8 %copy-start.9 = (s32[32]{0:T(128)S(1)}, s32[32]{0:T(128)}, u32[]{:S(2)}) copy-start(s32[32]{0:T(128)} %param.18) | copy-start | bytes 388
  27.2 26.5 %all-to-all-start.2 = ((bf16[32,64,128]{2,1,0:T(8,128)(2,1)}), bf16[32,64,128]{2,1,0:T(8,128)(2,1)S(1)}, u32[]{:S(2)}, u32[]{:S(2)}) async-start(bf16[32,64,128]{2,1,0:T(8,128)(2,1)} %broadcast_in_dim.56), calls=%async_computation.2 | async-start | bytes 1048576 | tf_op jit(solution)/shard_map/all_to_all | solution.py:345
  37.2 102.6 %all-gather.6.cloned.1.call-start = ((), (), s32[]{:S(2)}) async-start(), calls=%async_computation.8 | async-start | bytes 1474560 | tf_op jit(solution)/shard_map/all_gather | solution.py:357
  120.1 22.6 %all-to-all-start.1 = ((f32[8,5,8,128]{3,2,1,0:T(8,128)}), f32[8,5,8,128]{3,2,1,0:T(8,128)S(1)}, u32[]{:S(2)}, u32[]{:S(2)}) async-start(f32[8,5,8,128]{3,2,1,0:T(8,128)} %broadcast_in_dim.31), calls=%async_computation.1 | async-start | bytes 327680 | tf_op jit(solution)/shard_map/all_to_all | solution.py:385
  142.7 1.3 copy-start
  155.5 19.3 %all-to-all-start.3 = ((bf16[8,128,256]{2,1,0:T(8,128)(2,1)}), bf16[8,128,256]{2,1,0:T(8,128)(2,1)}, u32[]{:S(2)}, u32[]{:S(2)}) async-start(bf16[8,128,256]{2,1,0:T(8,128)(2,1)} %get-tuple-element.25), calls=%async_computation.3 | async-start | bytes 1048576 | tf_op jit(solution)/shard_map/all_to_all | solution.py:403
  176.7 12.4 %all-to-all-start.4 = ((bf16[4,704,128]{2,1,0:T(8,128)(2,1)}), bf16[4,704,128]{2,1,0:T(8,128)(2,1)S(1)}, u32[]{:S(2)}, u32[]{:S(2)}) async-start(bf16[4,704,128]{2,1,0:T(8,128)(2,1)} %constant_dynamic-update-slice_fusion), calls=%async_computation.4 | async-start | bytes 1441792 | tf_op jit(solution)/shard_map/all_to_all | solution.py:422
  208.1 20.3 %all-to-all-start.6 = ((bf16[32,64,128]{2,1,0:T(8,128)(2,1)}), bf16[32,64,128]{2,1,0:T(8,128)(2,1)S(1)}, u32[]{:S(2)}, u32[]{:S(2)}) async-start(bf16[32,64,128]{2,1,0:T(8,128)(2,1)} %route.1), calls=%async_computation.6 | async-start | bytes 1048576 | tf_op jit(solution)/shard_map/all_to_all | solution.py:448
Sparse Core Ops, SparseCore 0:
  26.4 85.3 all-gather.3
  114.2 25.5 all-gather.5

commit v2 on v1

--- a/solution.py
+++ b/solution.py
@@ -45,7 +45,7 @@
 
 
 def pack_kernel(heads, tok, patch_ref, gain_ref, proj_ref, q_ref, kv_ref, bias_ref, do_ref, type_ref,
-                out_ref, normed_ref):
+                kv_out, q_out, normed_ref):
     scaled, _ = normalize_rows(patch_ref[...])
     normed = (scaled * gain_ref[...]).astype(BF16)
     normed_ref[...] = normed
@@ -55,48 +55,48 @@
     keys = (kv_ref[0].astype(F32) + bias).astype(BF16)
     for h in range(heads):
         span = slice(h * HD, (h + 1) * HD)
-        out_ref[h, 0:tok] = keys[:, span]
-        out_ref[h, tok : 2 * tok] = kv_ref[1, :, span]
-        out_ref[h, 2 * tok : 3 * tok] = q_ref[:, span]
-        out_ref[h, 3 * tok : 4 * tok] = do_ref[:, span]
-        out_ref[h, 4 * tok : 4 * tok + PATCH_MOST] = image[:, span]
-        out_ref[h, 4 * tok + PATCH_MOST :] = image[:, cols + h * HD : cols + (h + 1) * HD]
-    for h in range(heads, out_ref.shape[0]):
-        out_ref[h] = jnp.zeros_like(out_ref[h])
+        kv_out[h, 0:tok] = keys[:, span]
+        kv_out[h, tok : 2 * tok] = kv_ref[1, :, span]
+        kv_out[h, 2 * tok : 2 * tok + PATCH_MOST] = image[:, span]
+        kv_out[h, 2 * tok + PATCH_MOST :] = image[:, cols + h * HD : cols + (h + 1) * HD]
+        q_out[h, 0:tok] = q_ref[:, span]
+        q_out[h, tok:] = do_ref[:, span]
+    for h in range(heads, kv_out.shape[0]):
+        kv_out[h] = jnp.zeros_like(kv_out[h])
+        q_out[h] = jnp.zeros_like(q_out[h])
 
 
 def place_kernel(frames, meta_ref, rows_ref, out_ref, scratch):
-    group = out_ref.shape[0]
-    first = meta_ref[2 * frames] * group
+    total = out_ref.shape[0]
     scratch[...] = jnp.zeros_like(scratch)
     row = lax.broadcasted_iota(jnp.int32, (PATCH_MOST, HD), 0)
 
     def one(f, carry):
-        offset = meta_ref[f] - first
-
-        @pl.when((offset >= 0) & (offset < group))
-        def _():
-            where = pl.ds(offset, PATCH_MOST)
-            scratch[where] = jnp.where(
-                row < meta_ref[frames + f], rows_ref[f].astype(F32), scratch[where]
-            )
-
+        where = pl.ds(meta_ref[f], PATCH_MOST)
+        live = row < meta_ref[frames + f]
+        scratch[where] = jnp.where(live, rows_ref[f].astype(F32), scratch[where])
         return carry
 
     lax.fori_loop(0, frames, one, 0)
-    out_ref[...] = scratch[0:group].astype(BF16)
-
-
-def query_kernel(frames, tok, meta_ref, start_ref, g_ref, att_ref, dq_ref, own_ref, stat_ref,
+
+    def low(c, carry):
+        where = pl.ds(pl.multiple_of(c * CHUNK, CHUNK), CHUNK)
+        out_ref[where] = scratch[where].astype(BF16)
+        return carry
+
+    lax.fori_loop(0, total // CHUNK, low, 0)
+
+
+def query_kernel(frames, tok, meta_ref, start_ref, g_ref, mine_ref, out_ref, own_ref, stat_ref,
                  kf, vf, kb, vb, qb, dob, s_ref, m_ref, l_ref, acc):
-    group = att_ref.shape[0]
+    group = own_ref.shape[1]
     total = kb.shape[0]
     scale = 1.0 / math.sqrt(HD)
     power = scale * math.log2(math.e)
     z = meta_ref[2 * frames]
     first_chunk = meta_ref[2 * frames + 2]
     last_chunk = meta_ref[2 * frames + 3]
-    image_row = 4 * tok
+    image_row = 2 * tok
 
     def text(b, carry):
         where = pl.ds(pl.multiple_of(b * tok, 32), tok)
@@ -125,8 +125,8 @@
     lax.fori_loop(0, total // CHUNK, low, 0)
     per = group // tok
     for i in range(per):
-        qb[i * tok : (i + 1) * tok] = g_ref[z * per + i, 2 * tok : 3 * tok]
-        dob[i * tok : (i + 1) * tok] = g_ref[z * per + i, 3 * tok : 4 * tok]
+        qb[i * tok : (i + 1) * tok] = mine_ref[i, 0:tok]
+        dob[i * tok : (i + 1) * tok] = mine_ref[i, tok:]
     own = pl.ds(pl.multiple_of(z * group, HD), group)
     own_ref[0] = kb[own]
     own_ref[1] = vb[own]
@@ -164,7 +164,8 @@
     lax.fori_loop(first_chunk, last_chunk, weigh, 0)
     inverse_sum = 1.0 / jnp.sum(l_ref[...], axis=1, keepdims=True)
     attended = (acc[...] * inverse_sum).astype(BF16)
-    att_ref[...] = attended
+    for i in range(per):
+        out_ref[i, 0:tok] = attended[i * tok : (i + 1) * tok]
     delta = jnp.sum(dob[...].astype(F32) * attended.astype(F32), axis=1, keepdims=True)
     acc[...] = jnp.zeros_like(acc)
     m_ref[...] = jnp.broadcast_to(inverse_sum, m_ref.shape)
@@ -179,14 +180,16 @@
         return carry
 
     lax.fori_loop(first_chunk, last_chunk, back, 0)
-    dq_ref[...] = (acc[...] * scale).astype(BF16)
+    d_query = (acc[...] * scale).astype(BF16)
+    for i in range(per):
+        out_ref[i, tok:] = d_query[i * tok : (i + 1) * tok]
     which = lax.broadcasted_iota(jnp.int32, (group, HD), 1)
     table = jnp.where(which == 0, row_max, jnp.where(which == 1, inverse_sum, delta))
     for i in range(group // HD):
         stat_ref[i] = jnp.transpose(table[i * HD : (i + 1) * HD])[0:8]
 
 
-def key_kernel(frames, tok, meta_ref, end_ref, g_ref, stat_ref, own_ref, norm_ref, dkv_ref, part_ref,
+def key_kernel(frames, tok, meta_ref, end_ref, g_ref, stat_ref, own_ref, dkv_ref, out_ref,
                qb, dob, dk, dv):
     group = own_ref.shape[1]
     total = qb.shape[0]
@@ -196,8 +199,8 @@
 
     def text(b, carry):
         where = pl.ds(pl.multiple_of(b * tok, 32), tok)
-        qb[where] = g_ref[b, 2 * tok : 3 * tok]
-        dob[where] = g_ref[b, 3 * tok : 4 * tok]
+        qb[where] = g_ref[b, 0:tok]
+        dob[where] = g_ref[b, tok:]
         return carry
 
     lax.fori_loop(0, total // tok, text, 0)
@@ -224,29 +227,39 @@
     lax.fori_loop(meta_ref[2 * frames + 4], meta_ref[2 * frames + 5], step, 0)
     key_grad = (dk[...] * scale).astype(BF16)
     value_grad = dv[...].astype(BF16)
-    dkv_ref[0] = key_grad
-    dkv_ref[1] = value_grad
-    both = jnp.concatenate([key_grad, value_grad], axis=1)
-    for i in range(norm_ref.shape[0]):
-        part_ref[i] = dot_tn(norm_ref[i], both).astype(BF16)
-
-
-def unpack_kernel(heads, tok, r_ref, image_ref, proj_ref, att_ref, dq_ref, dtext_ref, dproj_ref, dn_ref):
-    cols = heads * HD
-    is_image = image_ref[...] == 1
-    parts = [None] * (2 * heads)
-    rows = dproj_ref.shape[0]
+    dkv_ref[:, 0:HD] = key_grad
+    dkv_ref[:, HD:] = value_grad
+    for i in range(group // tok):
+        rows = slice(i * tok, (i + 1) * tok)
+        out_ref[i, 0:tok] = key_grad[rows]
+        out_ref[i, tok:] = value_grad[rows]
+
+
+def proj_kernel(norm_ref, grad_ref, out_ref):
+    low = dot_tn(norm_ref[...], grad_ref[...]).astype(BF16)
+    rows = out_ref.shape[1] // 2
+    for i in range(out_ref.shape[0]):
+        out_ref[i, 0:rows] = low[i * rows : (i + 1) * rows, 0:HD]
+        out_ref[i, rows:] = low[i * rows : (i + 1) * rows, HD:]
+
+
+def unpack_queries_kernel(heads, tok, r_ref, att_ref, dq_ref):
     for h in range(heads):
         span = slice(h * HD, (h + 1) * HD)
         att_ref[:, span] = r_ref[h, 0:tok]
-        dq_ref[:, span] = r_ref[h, tok : 2 * tok]
+        dq_ref[:, span] = r_ref[h, tok:]
+
+
+def unpack_kernel(heads, tok, r_ref, image_ref, proj_ref, dtext_ref, dn_ref):
+    is_image = image_ref[...] == 1
+    parts = [None] * (2 * heads)
+    for h in range(heads):
+        span = slice(h * HD, (h + 1) * HD)
         for c in range(2):
-            grad = r_ref[h, (2 + c) * tok : (3 + c) * tok]
+            grad = r_ref[h, c * tok : (c + 1) * tok]
             zero = jnp.zeros_like(grad)
             dtext_ref[c, :, span] = jnp.where(is_image, zero, grad)
             parts[c * heads + h] = jnp.where(is_image, grad, zero)
-            at = 4 * tok + c * rows
-            dproj_ref[:, c * cols + h * HD : c * cols + (h + 1) * HD] = r_ref[h, at : at + rows].astype(F32)
     grads = jnp.concatenate(parts, axis=1)
     for i in range(dn_ref.shape[0]):
         dn_ref[i] = dot_nt(grads, proj_ref[i * HD : (i + 1) * HD]).astype(BF16)
@@ -329,44 +342,51 @@
     gain = ln_gain.reshape(1, width)
     proj = kv_proj.reshape(width, 2 * cols)
     used = patches[:PATCH_MOST]
-    rows_each = 4 * tok + 2 * PATCH_MOST
-    packed, normed = pl.pallas_call(
+    packed, questions, normed = pl.pallas_call(
         lambda *refs: pack_kernel(heads, tok, *refs),
-        out_shape=(shape((per, rows_each, HD)), shape((PATCH_MOST, width))),
+        out_shape=(
+            shape((per, 2 * tok + 2 * PATCH_MOST, HD)),
+            shape((per, 2 * tok, HD)),
+            shape((PATCH_MOST, width)),
+        ),
         in_specs=[whole] * 8,
-        out_specs=(whole, whole),
+        out_specs=(whole, whole, whole),
         compiler_params=vmem(),
         name="pack",
     )(used, gain, proj, query, text_kv, type_bias, d_out, token_types.reshape(tok, 1))
-    by_head = lax.all_to_all(packed, "y", 0, 0, tiled=True)
-    gathered = lax.all_gather(by_head, "z", axis=0, tiled=True)
-
-    mine = lax.dynamic_slice_in_dim(normed, section * HD, HD, axis=1)
+    kv_mine = lax.all_to_all(packed, "y", 0, 0, tiled=True)
+    kv_all = lax.all_gather(kv_mine, "z", axis=0, tiled=True)
+    questions, _ = lax.optimization_barrier((questions, kv_mine))
+    q_mine = lax.all_to_all(questions, "y", 0, 0, tiled=True)
+    q_all = lax.all_gather(q_mine, "z", axis=0, tiled=True)
+
+    normed, _ = lax.optimization_barrier((normed, q_mine))
+    slices = normed.reshape(PATCH_MOST, groups, 1, HD).transpose(1, 2, 0, 3)
     all_frames = lax.all_to_all(
-        jnp.broadcast_to(mine[None], (blocks, PATCH_MOST, HD)), ("z", "y"), 0, 0, tiled=True
+        jnp.broadcast_to(slices, (groups, per, PATCH_MOST, HD)).reshape(blocks, PATCH_MOST, HD),
+        ("z", "y"), 0, 0, tiled=True,
     )
-    placed = pl.pallas_call(
+    norm_pos = pl.pallas_call(
         lambda *refs: place_kernel(frames, *refs),
-        out_shape=shape((group, HD)),
+        out_shape=shape((total, HD)),
         in_specs=[smem, whole],
         out_specs=whole,
-        scratch_shapes=[pltpu.VMEM((group + PATCH_MOST, HD), F32)],
+        scratch_shapes=[pltpu.VMEM((total + PATCH_MOST, HD), F32)],
         compiler_params=vmem(),
         name="place",
     )(meta, all_frames)
-    norm_pos = lax.all_gather(placed, "phase", axis=0, tiled=False)
+    kv_all, norm_pos = lax.optimization_barrier((kv_all, norm_pos))
 
     most_chunks = (EPISODE_MOST + group + CHUNK - 2) // CHUNK + 1
-    attended, d_query, own_kv, stats = pl.pallas_call(
+    answers, own_kv, stats = pl.pallas_call(
         lambda *refs: query_kernel(frames, tok, *refs),
         out_shape=(
-            shape((group, HD)),
-            shape((group, HD)),
+            shape((per, 2 * tok, HD)),
             shape((2, group, HD)),
             shape((group // HD, 8, HD), F32),
         ),
-        in_specs=[smem, whole, whole],
-        out_specs=(whole, whole, whole, whole),
+        in_specs=[smem, whole, whole, whole],
+        out_specs=(whole, whole, whole),
         scratch_shapes=[
             pltpu.VMEM((total + PATCH_MOST, HD), F32),
             pltpu.VMEM((total + PATCH_MOST, HD), F32),
@@ -381,15 +401,26 @@
         ],
         compiler_params=vmem(),
         name="queries",
-    )(meta, start, gathered)
+    )(meta, start, kv_all, q_mine)
     all_stats = lax.all_to_all(
         jnp.broadcast_to(stats[None], (groups,) + stats.shape), "z", 0, 0, tiled=True
     ).reshape(total // HD, 8, HD)
-
-    d_kv, part = pl.pallas_call(
+    answers, all_stats = lax.optimization_barrier((answers, all_stats))
+    returned = lax.all_to_all(answers, "y", 0, 0, tiled=True)
+    att_here, dq_here = pl.pallas_call(
+        lambda *refs: unpack_queries_kernel(heads, tok, *refs),
+        out_shape=(shape((tok, cols)), shape((tok, cols))),
+        in_specs=[whole],
+        out_specs=(whole, whole),
+        compiler_params=vmem(),
+        name="unpack_queries",
+    )(returned)
+    q_all, returned = lax.optimization_barrier((q_all, returned))
+
+    d_kv, key_grads = pl.pallas_call(
         lambda *refs: key_kernel(frames, tok, *refs),
-        out_shape=(shape((2, group, HD)), shape((sections, HD, 2 * HD))),
-        in_specs=[smem, whole, whole, whole, whole, whole],
+        out_shape=(shape((group, 2 * HD)), shape((per, 2 * tok, HD))),
+        in_specs=[smem] + [whole] * 4,
         out_specs=(whole, whole),
         scratch_shapes=[
             pltpu.VMEM((total, HD), BF16),
@@ -399,41 +430,17 @@
         ],
         compiler_params=vmem(),
         name="keys",
-    )(meta, end, gathered, all_stats, own_kv, norm_pos)
-    proj_terms = lax.all_to_all(part.reshape(groups, width // groups, 2 * HD), "z", 0, 0, tiled=True)
-    proj_rows = width // blocks
-    proj_sum = (
-        jnp.sum(proj_terms.astype(F32), axis=0)
-        .astype(BF16)
-        .reshape(per, proj_rows, 2, HD)
-        .transpose(0, 2, 1, 3)
-        .reshape(per, 2 * proj_rows, HD)
-    )
-    answers = jnp.concatenate(
-        [
-            attended.reshape(per, tok, HD),
-            d_query.reshape(per, tok, HD),
-            d_kv[0].reshape(per, tok, HD),
-            d_kv[1].reshape(per, tok, HD),
-            proj_sum,
-        ],
-        axis=1,
-    )
-    returned = lax.all_to_all(answers, "y", 0, 0, tiled=True)
-    att_here, dq_here, d_text_kv, d_proj, terms = pl.pallas_call(
+    )(meta, end, q_all, all_stats, own_kv)
+    d_kv_all = lax.all_gather(d_kv, "z", axis=0, tiled=True)
+    keys_back = lax.all_to_all(key_grads, "y", 0, 0, tiled=True)
+    d_text_kv, terms = pl.pallas_call(
         lambda *refs: unpack_kernel(heads, tok, *refs),
-        out_shape=(
-            shape((tok, cols)),
-            shape((tok, cols)),
-            shape((2, tok, cols)),
-            shape((proj_rows, 2 * cols), F32),
-            shape((sections, tok, width // sections)),
-        ),
+        out_shape=(shape((2, tok, cols)), shape((sections, tok, width // sections))),
         in_specs=[whole] * 3,
-        out_specs=(whole,) * 5,
+        out_specs=(whole,) * 2,
         compiler_params=vmem(),
         name="unpack",
-    )(returned, is_image, proj)
+    )(keys_back, is_image, proj)
 
     summed = lax.all_to_all(terms, "phase", 0, 0, tiled=True)
     routed = pl.pallas_call(
@@ -448,7 +455,25 @@
     from_blocks = lax.all_to_all(routed, ("z", "y"), 0, 0, tiled=True)
     source = lax.dynamic_index_in_dim(image_offsets, block, keepdims=False) // tok
     d_slice = lax.dynamic_index_in_dim(from_blocks, source, keepdims=False)
-    d_normed = lax.all_gather(d_slice, "phase", axis=0, tiled=False)
+    d_normed = lax.all_to_all(
+        jnp.broadcast_to(d_slice[None], (sections,) + d_slice.shape), "phase", 0, 0, tiled=True
+    )
+    proj_rows = width // blocks
+    proj_head = pl.pallas_call(
+        proj_kernel,
+        out_shape=shape((per, 2 * proj_rows, HD)),
+        in_specs=[whole] * 2,
+        out_specs=whole,
+        compiler_params=vmem(),
+        name="proj_grad",
+    )(norm_pos, d_kv_all)
+    proj_back = lax.all_to_all(proj_head, "y", 0, 0, tiled=True)
+    d_proj = (
+        proj_back[:heads].astype(F32)
+        .reshape(heads, 2, proj_rows, HD)
+        .transpose(2, 1, 0, 3)
+        .reshape(proj_rows, 2, cols)
+    )
     d_patches = pl.pallas_call(
         norm_grad_kernel,
         out_shape=shape(patches.shape),
@@ -461,7 +486,7 @@
         att_here,
         dq_here,
         d_text_kv,
-        d_proj.reshape(proj_rows, 2, cols),
+        d_proj,
         d_patches,
     )
 

time: 252 us -> 226 us (0.90)
  waiting for transfers between devices: 109 us -> 70.3 us
  blocking collectives: 46.2 us -> 60.3 us
  Pallas kernels: 25.6 us -> 16.1 us
  local copies, waits for them, and re-layouts: 12.3 us -> 20.6 us
    all_gather x2 -> x3, waiting for transfers between devices: 61.6 us -> 28.9 us  [the longest x1 20.3 us: shards(): kv_all = lax.all_gather(kv_mine, 'z', axis=0, tiled=True)]
    all_to_all x1 -> x3, blocking collectives: 15.5 us -> 44.1 us  [the longest x1 22.8 us: shards(): lax.all_to_all(jnp.broadcast_to(stats[None], (groups,) + stats.shape), 'z...]
    all_gather x1 -> x0, blocking collectives: 14.8 us -> none  [shards(): d_normed = lax.all_gather(d_slice, 'phase', axis=0, tiled=False)]
    unnamed x25 -> x51, local copies, waits for them, and re-layouts: 5.96 us -> 15 us
    pallas_call x1, Pallas kernels: 11.5 us -> 3.48 us  [shards(): pl.pallas_call(lambda *refs: key_kernel(frames, tok, *refs), out_shape=(s...]
    all_to_all x1, waiting for transfers between devices: 7.81 us -> 0.01 us  [shards(): returned = lax.all_to_all(answers, 'y', 0, 0, tiled=True)]
    all_to_all x3 -> x4, starting transfers between devices: 28.3 us -> 22.6 us  [the longest x1 9.37 us: shards(): lax.all_to_all(jnp.broadcast_to(slices, (groups, per, PATCH_MOST, HD)).re...]
    all_to_all x1, starting transfers between devices: 3.89 us -> 9.33 us  [shards(): from_blocks = lax.all_to_all(routed, ('z', 'y'), 0, 0, tiled=True)]
  transfers between devices with their start and end apart: 7 -> 9, of which waited for: 7 -> 7; matrix products, arithmetic and copies ran while one was open for 3% -> 3% of each run, Pallas kernels for 4% -> 5%
where the time goes in v2:
time: 226 us; the launch traced here: 225 us
  waiting for transfers between devices  70.3 us (31%)
  blocking collectives  60.3 us (27%)
  starting transfers between devices  36 us (16%)
  local copies, waits for them, and re-layouts  20.6 us (9%)
  between operations  19.4 us (9%)
  Pallas kernels  16.1 us (7%)
    all_to_all x1, blocking collectives, shards(): lax.all_to_all(jnp.broadcast_to(stats[None], (groups,) + stats.shape), 'z...  22.8 us
    all_gather x1, waiting for transfers between devices, shards(): kv_all = lax.all_gather(kv_mine, 'z', axis=0, tiled=True)  20.3 us
    all_to_all x1, waiting for transfers between devices, shards(): from_blocks = lax.all_to_all(routed, ('z', 'y'), 0, 0, tiled=True)  17 us
    all_to_all x1, blocking collectives, shards(): summed = lax.all_to_all(terms, 'phase', 0, 0, tiled=True)  16.2 us
    all_to_all x1, waiting for transfers between devices, shards(): lax.all_to_all(jnp.broadcast_to(slices, (groups, per, PATCH_MOST, HD)).re...  16.2 us
    unnamed x51, local copies, waits for them, and re-layouts  15 us
    all_to_all x1, blocking collectives, shards(): kv_mine = lax.all_to_all(packed, 'y', 0, 0, tiled=True)  12.4 us
    all_to_all x1, starting transfers between devices, shards(): lax.all_to_all(jnp.broadcast_to(slices, (groups, per, PATCH_MOST, HD)).re...  9.37 us
  transfers between devices with their start and end apart: 9, of which 7 were waited for; matrix products, arithmetic and copies ran while one was open for 3% of the time, Pallas kernels for 5%

profile of v2, /device:TPU:1, one launch (start us, length us, event | category | flops | bytes accessed | tf_op | source)
XLA Modules:
  0.0 225.0 jit_solution(8889886115310675780)
XLA Ops:
  7.3 1.9 copy.39
  9.1 0.9 slice.16.refs_0_.patch_ref
  10.8 12.4 %all_to_all.50 = bf16[4,448,128]{2,1,0:T(8,128)(2,1)} all-to-all(bf16[4,448,128]{2,1,0:T(8,128)(2,1)S(1)} %get-tuple-element.24), channel_id=1, replica_groups=mesh['phase'=8,'z'=8,'y'=4] {'y'}, dimensions={0} | all-to-all | bytes 917504 | tf_op jit(solution)/shard_map/all_to_all | solution.py:357
  23.4 9.0 %all_to_all.51.refs_3_ = bf16[4,320,128]{2,1,0:T(8,128)(2,1)} all-to-all(bf16[4,320,128]{2,1,0:T(8,128)(2,1)S(1)} %get-tuple-element.27), channel_id=1, replica_groups=mesh['phase'=8,'z'=8,'y'=4] {'y'}, dimensions={0} | all-to-all | bytes 655360 | tf_op jit(solution)/shard_map/all_to_all | solution.py:360
  33.3 9.4 %all-to-all-start.2 = ((bf16[32,64,128]{2,1,0:T(8,128)(2,1)}), bf16[32,64,128]{2,1,0:T(8,128)(2,1)S(1)}, u32[]{:S(2)}, u32[]{:S(2)}) async-start(bf16[32,64,128]{2,1,0:T(8,128)(2,1)} %bitcast.12), calls=%async_computation.2 | async-start | bytes 1048576 | tf_op jit(solution)/shard_map/all_to_all | solution.py:365
  47.8 16.2 %all-to-all-done.2.refs_1_ = bf16[32,64,128]{2,1,0:T(8,128)(2,1)S(1)} async-done(((bf16[32,64,128]{2,1,0:T(8,128)(2,1)}), bf16[32,64,128]{2,1,0:T(8,128)(2,1)S(1)}, u32[]{:S(2)}, u32[]{:S(2)}) %all-to-all-start.2) | async-done | bytes 524320 | tf_op jit(solution)/shard_map/all_to_all | solution.py:365
  64.7 1.0 copy-done.5
  65.8 1.2 place.1.norm_ref
  66.9 20.3 %all-gather.4.cloned.1.call-done.refs_2_ = bf16[32,448,128]{2,1,0:T(8,128)(2,1)} async-done(((bf16[4,448,128]{2,1,0:T(8,128)(2,1)}), bf16[32,448,128]{2,1,0:T(8,128)(2,1)}) %all-gather.4.cloned.1.call-update) | async-done | bytes 3670032 | tf_op jit(solution)/shard_map/all_gather | solution.py:358
  87.2 2.0 copy-done
  89.3 5.3 %queries.1 = (bf16[4,320,128]{2,1,0:T(8,128)(2,1)S(1)}, bf16[2,640,128]{2,1,0:T(8,128)(2,1)S(1)}, f32[5,8,128]{2,1,0:T(8,128)S(1)}) custom-call(s32[70]{0:T(128)S(1)} %concatenate.3.refs_0_, s32[640,1]{1,0:T(8,128)S(1)} %broadcast_in_dim.69.refs_1_, bf16[32,448,128]{2,1,0:T(8,128)(2,1)S(1)} %copy-done, bf16[4,320,128]{2,1,0:T(8,128)(2,1)S(1)} %copy-done.1), custom_call_target="tpu_custom_call" | custom-call | tf_op jit(solution)/shard_map/queries/pallas_call | solution.py:381
  95.3 22.8 %all_to_all.52 = f32[8,5,8,128]{3,2,1,0:T(8,128)} all-to-all(f32[8,5,8,128]{3,2,1,0:T(8,128)S(1)} %broadcast_in_dim.65), channel_id=1, replica_groups=mesh['phase'=8,'z'=8,'y'=4] {'z'}, dimensions={0} | all-to-all | bytes 327680 | tf_op jit(solution)/shard_map/all_to_all | solution.py:405
  118.1 4.0 %all-to-all-start.4 = ((bf16[4,320,128]{2,1,0:T(8,128)(2,1)}), bf16[4,320,128]{2,1,0:T(8,128)(2,1)S(1)}, u32[]{:S(2)}, u32[]{:S(2)}) async-start(bf16[4,320,128]{2,1,0:T(8,128)(2,1)} %copy-done.12), calls=%async_computation.4 | async-start | bytes 655360 | tf_op jit(solution)/shard_map/all_to_all | solution.py:409
  122.2 8.6 %all-gather.6.cloned.1.call-done.refs_2_ = bf16[32,320,128]{2,1,0:T(8,128)(2,1)} async-done(((bf16[4,320,128]{2,1,0:T(8,128)(2,1)}), bf16[32,320,128]{2,1,0:T(8,128)(2,1)}) %all-gather.6.cloned.1.call-update) | async-done | bytes 2621456 | tf_op jit(solution)/shard_map/all_gather | solution.py:361
  130.9 1.7 copy-done.2
  132.6 0.9 copy-done.8
  133.5 1.0 copy-done.14
  134.5 3.5 %keys.1 = (bf16[640,256]{1,0:T(8,128)(2,1)S(1)}, bf16[4,320,128]{2,1,0:T(8,128)(2,1)S(1)}) custom-call(s32[70]{0:T(128)S(1)} %concatenate.3.refs_0_, s32[640,1]{1,0:T(8,128)S(1)} %broadcast_in_dim.70.refs_1_, bf16[32,320,128]{2,1,0:T(8,128)(2,1)S(1)} %copy-done.2, f32[40,8,128]{2,1,0:T(8,128)S(1)} %bitcast.36, bf16[2,640,128]{2,1,0:T(8,128)(2,1)S(1)} %copy-done.14), custom_call_target="tpu_custom_call" | custom-call | tf_op jit(solution)/shard_map/keys/pallas_call | solution.py:420
  139.4 4.0 %all-to-all-start.5 = ((bf16[4,320,128]{2,1,0:T(8,128)(2,1)}), bf16[4,320,128]{2,1,0:T(8,128)(2,1)S(1)}, u32[]{:S(2)}, u32[]{:S(2)}) async-start(bf16[4,320,128]{2,1,0:T(8,128)(2,1)} %copy-done.11), calls=%async_computation.5 | async-start | bytes 655360 | tf_op jit(solution)/shard_map/all_to_all | solution.py:435
  143.5 1.2 add.50
  146.1 3.2 %all-to-all-done.5.refs_0_ = bf16[4,320,128]{2,1,0:T(8,128)(2,1)S(1)} async-done(((bf16[4,320,128]{2,1,0:T(8,128)(2,1)}), bf16[4,320,128]{2,1,0:T(8,128)(2,1)S(1)}, u32[]{:S(2)}, u32[]{:S(2)}) %all-to-all-start.5) | async-done | bytes 327712 | tf_op jit(solution)/shard_map/all_to_all | solution.py:435
  151.1 16.2 %all_to_all.53.refs_1_ = bf16[8,160,128]{2,1,0:T(8,128)(2,1)S(1)} all-to-all(bf16[8,160,128]{2,1,0:T(8,128)(2,1)S(1)} %get-tuple-element.42), channel_id=1, replica_groups=mesh['phase'=8,'z'=8,'y'=4] {'phase'}, dimensions={0} | all-to-all | bytes 655360 | tf_op jit(solution)/shard_map/all_to_all | solution.py:445
  167.3 1.7 route.1
  169.0 9.3 %all-to-all-start.8 = ((bf16[32,64,128]{2,1,0:T(8,128)(2,1)}), bf16[32,64,128]{2,1,0:T(8,128)(2,1)S(1)}, u32[]{:S(2)}, u32[]{:S(2)}) async-start(bf16[32,64,128]{2,1,0:T(8,128)(2,1)} %route.1), calls=%async_computation.8 | async-start | bytes 1048576 | tf_op jit(solution)/shard_map/all_to_all | solution.py:455
  180.9 17.0 %all-to-all-done.8 = bf16[32,64,128]{2,1,0:T(8,128)(2,1)S(1)} async-done(((bf16[32,64,128]{2,1,0:T(8,128)(2,1)}), bf16[32,64,128]{2,1,0:T(8,128)(2,1)S(1)}, u32[]{:S(2)}, u32[]{:S(2)}) %all-to-all-start.8) | async-done | bytes 524320 | tf_op jit(solution)/shard_map/all_to_all | solution.py:455
  198.6 5.9 %all-to-all-start.9 = ((bf16[8,64,128]{2,1,0:T(8,128)(2,1)}), bf16[8,64,128]{2,1,0:T(8,128)(2,1)S(1)}, u32[]{:S(2)}, u32[]{:S(2)}) async-start(bf16[8,64,128]{2,1,0:T(8,128)(2,1)} %broadcast_in_dim.68), calls=%async_computation.9 | async-start | bytes 262144 | tf_op jit(solution)/shard_map/all_to_all | solution.py:458
  204.6 1.7 copy-done.3
  206.3 1.2 proj_grad.1
  207.5 2.3 %all-to-all-done.9.dn_ref = bf16[8,64,128]{2,1,0:T(8,128)(2,1)S(1)} async-done(((bf16[8,64,128]{2,1,0:T(8,128)(2,1)}), bf16[8,64,128]{2,1,0:T(8,128)(2,1)S(1)}, u32[]{:S(2)}, u32[]{:S(2)}) %all-to-all-start.9) | async-done | bytes 131104 | tf_op jit(solution)/shard_map/all_to_all | solution.py:458
  209.9 3.3 %all-to-all-start.6 = ((bf16[4,64,128]{2,1,0:T(8,128)(2,1)}), bf16[4,64,128]{2,1,0:T(8,128)(2,1)S(1)}, u32[]{:S(2)}, u32[]{:S(2)}) async-start(bf16[4,64,128]{2,1,0:T(8,128)(2,1)} %proj_grad.1), calls=%async_computation.6 | async-start | bytes 131072 | tf_op jit(solution)/shard_map/all_to_all | solution.py:470
  213.9 1.1 norm_grad.1
  215.0 2.6 %all-to-all-done.6 = bf16[4,64,128]{2,1,0:T(8,128)(2,1)S(1)} async-done(((bf16[4,64,128]{2,1,0:T(8,128)(2,1)}), bf16[4,64,128]{2,1,0:T(8,128)(2,1)S(1)}, u32[]{:S(2)}, u32[]{:S(2)}) %all-to-all-start.6) | async-done | bytes 65568 | tf_op jit(solution)/shard_map/all_to_all | solution.py:470
  (77 shorter events, 12.7 us)
Async XLA Ops:
  7.2 2.9 %copy-start.22 = (s32[160]{0:T(256)S(1)}, s32[160]{0:T(256)}, u32[]{:S(2)}) copy-start(s32[160]{0:T(256)} %param.20) | copy-start | bytes 1924
  7.2 3.0 %copy-start.18 = (f32[1024]{0:T(1024)S(1)}, f32[1024]{0:T(1024)}, u32[]{:S(2)}) copy-start(f32[1024]{0:T(1024)} %param.12) | copy-start | bytes 12292
  7.2 3.0 %copy-start.16 = (bf16[160,384]{1,0:T(8,128)(2,1)S(1)}, bf16[160,384]{1,0:T(8,128)(2,1)}, u32[]{:S(2)}) copy-start(bf16[160,384]{1,0:T(8,128)(2,1)} %refs_3_.1) | copy-start | bytes 368644
  7.2 3.0 %copy-start.15 = (bf16[2,160,384]{2,1,0:T(8,128)(2,1)S(1)}, bf16[2,160,384]{2,1,0:T(8,128)(2,1)}, u32[]{:S(2)}) copy-start(bf16[2,160,384]{2,1,0:T(8,128)(2,1)} %refs_4_.1) | copy-start | bytes 737284
  7.2 3.0 %copy-start.19 = (bf16[2,384]{1,0:T(2,128)(2,1)S(1)}, bf16[2,384]{1,0:T(2,128)(2,1)}, u32[]{:S(2)}) copy-start(bf16[2,384]{1,0:T(2,128)(2,1)} %refs_5_.1) | copy-start | bytes 4612
  7.2 3.0 %copy-start.17 = (bf16[160,384]{1,0:T(8,128)(2,1)S(1)}, bf16[160,384]{1,0:T(8,128)(2,1)}, u32[]{:S(2)}) copy-start(bf16[160,384]{1,0:T(8,128)(2,1)} %refs_6_.1) | copy-start | bytes 368644
  7.2 80.0 %all-gather.4.cloned.1.call-start = ((), (), s32[]{:S(2)}) async-start(), calls=%async_computation.10 | async-start | bytes 4128768 | tf_op jit(solution)/shard_map/all_gather | solution.py:358
  10.1 22.3 %copy-start.6 = (bf16[64,1024]{1,0:T(8,128)(2,1)}, bf16[64,1024]{1,0:T(8,128)(2,1)S(1)}, u32[]{:S(2)}) copy-start(bf16[64,1024]{1,0:T(8,128)(2,1)S(1)} %slice.16.refs_0_.patch_ref) | copy-start | bytes 393220
  10.8 31.9 %copy-start.20 = (s32[5120]{0:T(1024)S(1)}, s32[5120]{0:T(1024)}, u32[]{:S(2)}) copy-start(s32[5120]{0:T(1024)} %param.21) | copy-start | bytes 61444
  10.8 36.8 %copy-start.21 = (s32[32]{0:T(128)S(1)}, s32[32]{0:T(128)}, u32[]{:S(2)}) copy-start(s32[32]{0:T(128)} %param.19) | copy-start | bytes 388
  10.8 36.8 %copy-start.23 = (s32[32]{0:T(128)S(1)}, s32[32]{0:T(128)}, u32[]{:S(2)}) copy-start(s32[32]{0:T(128)} %param.18) | copy-start | bytes 388
  23.3 107.5 %all-gather.6.cloned.1.call-start = ((), (), s32[]{:S(2)}) async-start(), calls=%async_computation.11 | async-start | bytes 2949120 | tf_op jit(solution)/shard_map/all_gather | solution.py:361
  32.3 54.9 %copy-start.1 = (bf16[4,320,128]{2,1,0:T(8,128)(2,1)S(1)}, bf16[4,320,128]{2,1,0:T(8,128)(2,1)}, u32[]{:S(2)}) copy-start(bf16[4,320,128]{2,1,0:T(8,128)(2,1)} %all_to_all.51.refs_3_) | copy-start | bytes 983044
  33.3 30.6 %all-to-all-start.2 = ((bf16[32,64,128]{2,1,0:T(8,128)(2,1)}), bf16[32,64,128]{2,1,0:T(8,128)(2,1)S(1)}, u32[]{:S(2)}, u32[]{:S(2)}) async-start(bf16[32,64,128]{2,1,0:T(8,128)(2,1)} %bitcast.12), calls=%async_computation.2 | async-start | bytes 1048576 | tf_op jit(solution)/shard_map/all_to_all | solution.py:365
  63.9 0.8 copy-start.4
  64.7 1.0 copy-start.5
  87.2 2.0 copy-start
  94.6 0.7 copy-start.13
  95.3 22.8 %copy-start.12 = (bf16[4,320,128]{2,1,0:T(8,128)(2,1)}, bf16[4,320,128]{2,1,0:T(8,128)(2,1)S(1)}, u32[]{:S(2)}) copy-start(bf16[4,320,128]{2,1,0:T(8,128)(2,1)S(1)} %get-tuple-element.32) | copy-start | bytes 983044
  118.1 12.8 %all-to-all-start.4 = ((bf16[4,320,128]{2,1,0:T(8,128)(2,1)}), bf16[4,320,128]{2,1,0:T(8,128)(2,1)S(1)}, u32[]{:S(2)}, u32[]{:S(2)}) async-start(bf16[4,320,128]{2,1,0:T(8,128)(2,1)} %copy-done.12), calls=%async_computation.4 | async-start | bytes 655360 | tf_op jit(solution)/shard_map/all_to_all | solution.py:409
  122.1 82.5 %all-gather.8.cloned.1.call-start = ((), (), s32[]{:S(2)}) async-start(), calls=%async_computation.12 | async-start | bytes 2949120 | tf_op jit(solution)/shard_map/all_gather | solution.py:434
  130.9 1.7 copy-start.2
  132.6 0.9 copy-start.8
  133.5 1.0 copy-start.14
  138.0 0.7 copy-start.10
  139.4 9.9 %all-to-all-start.5 = ((bf16[4,320,128]{2,1,0:T(8,128)(2,1)}), bf16[4,320,128]{2,1,0:T(8,128)(2,1)S(1)}, u32[]{:S(2)}, u32[]{:S(2)}) async-start(bf16[4,320,128]{2,1,0:T(8,128)(2,1)} %copy-done.11), calls=%async_computation.5 | async-start | bytes 655360 | tf_op jit(solution)/shard_map/all_to_all | solution.py:435
  149.3 0.9 copy-start.9
  169.0 28.9 %all-to-all-start.8 = ((bf16[32,64,128]{2,1,0:T(8,128)(2,1)}), bf16[32,64,128]{2,1,0:T(8,128)(2,1)S(1)}, u32[]{:S(2)}, u32[]{:S(2)}) async-start(bf16[32,64,128]{2,1,0:T(8,128)(2,1)} %route.1), calls=%async_computation.8 | async-start | bytes 1048576 | tf_op jit(solution)/shard_map/all_to_all | solution.py:455
  178.4 35.5 %copy-start.7 = (bf16[64,1024]{1,0:T(8,128)(2,1)S(1)}, bf16[64,1024]{1,0:T(8,128)(2,1)}, u32[]{:S(2)}) copy-start(bf16[64,1024]{1,0:T(8,128)(2,1)} %copy-done.6) | copy-start | bytes 393220
  198.6 11.2 %all-to-all-start.9 = ((bf16[8,64,128]{2,1,0:T(8,128)(2,1)}), bf16[8,64,128]{2,1,0:T(8,128)(2,1)S(1)}, u32[]{:S(2)}, u32[]{:S(2)}) async-start(bf16[8,64,128]{2,1,0:T(8,128)(2,1)} %broadcast_in_dim.68), calls=%async_computation.9 | async-start | bytes 262144 | tf_op jit(solution)/shard_map/all_to_all | solution.py:458
  204.6 1.7 copy-start.3
  209.9 7.8 %all-to-all-start.6 = ((bf16[4,64,128]{2,1,0:T(8,128)(2,1)}), bf16[4,64,128]{2,1,0:T(8,128)(2,1)S(1)}, u32[]{:S(2)}, u32[]{:S(2)}) async-start(bf16[4,64,128]{2,1,0:T(8,128)(2,1)} %proj_grad.1), calls=%async_computation.6 | async-start | bytes 131072 | tf_op jit(solution)/shard_map/all_to_all | solution.py:470
  (1 other events, 0.7 us)
Sparse Core Ops, SparseCore 0:
  23.4 63.7 all-gather.3
  89.0 41.8 all-gather.5
  139.6 50.7 all-gather.7

commit v3 on v2

--- a/solution.py
+++ b/solution.py
@@ -16,6 +16,7 @@
 EPSILON = 1e-05
 NEGATIVE = -1e30
 CHUNK = 256
+STAT_ROWS = 16
 
 F32 = jnp.float32
 BF16 = jnp.bfloat16
@@ -46,9 +47,10 @@
 
 def pack_kernel(heads, tok, patch_ref, gain_ref, proj_ref, q_ref, kv_ref, bias_ref, do_ref, type_ref,
                 kv_out, q_out, normed_ref):
-    scaled, _ = normalize_rows(patch_ref[...])
+    scaled, _ = normalize_rows(patch_ref[0:PATCH_MOST])
     normed = (scaled * gain_ref[...]).astype(BF16)
-    normed_ref[...] = normed
+    for i in range(normed_ref.shape[0]):
+        normed_ref[i] = normed[:, i * HD : (i + 1) * HD]
     image = dot_nn(normed, proj_ref[...]).astype(BF16)
     cols = heads * HD
     bias = jnp.where(type_ref[...] == 1, bias_ref[1:2].astype(F32), bias_ref[0:1].astype(F32))
@@ -68,13 +70,15 @@
 
 def place_kernel(frames, meta_ref, rows_ref, out_ref, scratch):
     total = out_ref.shape[0]
+    per = rows_ref.shape[0]
     scratch[...] = jnp.zeros_like(scratch)
     row = lax.broadcasted_iota(jnp.int32, (PATCH_MOST, HD), 0)
 
     def one(f, carry):
         where = pl.ds(meta_ref[f], PATCH_MOST)
         live = row < meta_ref[frames + f]
-        scratch[where] = jnp.where(live, rows_ref[f].astype(F32), scratch[where])
+        rows = rows_ref[lax.rem(f, per), lax.div(f, per)].astype(F32)
+        scratch[where] = jnp.where(live, rows, scratch[where])
         return carry
 
     lax.fori_loop(0, frames, one, 0)
@@ -87,8 +91,8 @@
     lax.fori_loop(0, total // CHUNK, low, 0)
 
 
-def query_kernel(frames, tok, meta_ref, start_ref, g_ref, mine_ref, out_ref, own_ref, stat_ref,
-                 kf, vf, kb, vb, qb, dob, s_ref, m_ref, l_ref, acc):
+def query_kernel(frames, tok, meta_ref, start_ref, g_ref, mine_ref, out_hbm, own_hbm, stat_hbm,
+                 out_ref, own_ref, stat_ref, out_sem, kf, vf, kb, vb, qb, dob, s_ref, m_ref, l_ref, acc):
     group = own_ref.shape[1]
     total = kb.shape[0]
     scale = 1.0 / math.sqrt(HD)
@@ -130,6 +134,8 @@
     own = pl.ds(pl.multiple_of(z * group, HD), group)
     own_ref[0] = kb[own]
     own_ref[1] = vb[own]
+    own_copy = pltpu.make_async_copy(own_ref, own_hbm, out_sem.at[0])
+    own_copy.start()
 
     m_ref[...] = jnp.full_like(m_ref, NEGATIVE)
     l_ref[...] = jnp.zeros_like(l_ref)
@@ -185,54 +191,105 @@
         out_ref[i, tok:] = d_query[i * tok : (i + 1) * tok]
     which = lax.broadcasted_iota(jnp.int32, (group, HD), 1)
     table = jnp.where(which == 0, row_max, jnp.where(which == 1, inverse_sum, delta))
-    for i in range(group // HD):
-        stat_ref[i] = jnp.transpose(table[i * HD : (i + 1) * HD])[0:8]
-
-
-def key_kernel(frames, tok, meta_ref, end_ref, g_ref, stat_ref, own_ref, dkv_ref, out_ref,
-               qb, dob, dk, dv):
+    tiles = [jnp.transpose(table[i * HD : (i + 1) * HD])[0:8] for i in range(group // HD)]
+    stat = jnp.concatenate([t[k : k + 1] for k in range(3) for t in tiles], axis=0)
+    stat = jnp.concatenate([stat, stat[0:1]], axis=0)
+    for i in range(stat_ref.shape[0]):
+        stat_ref[i] = stat
+    stat_copy = pltpu.make_async_copy(stat_ref, stat_hbm, out_sem.at[1])
+    out_copy = pltpu.make_async_copy(out_ref, out_hbm, out_sem.at[2])
+    stat_copy.start()
+    out_copy.start()
+    own_copy.wait()
+    stat_copy.wait()
+    out_copy.wait()
+
+
+def key_kernel(frames, tok, meta_ref, end_ref, g_hbm, stat_hbm, own_hbm, dkv_hbm, out_hbm,
+               qb, dob, stat_ref, own_ref, dk, dv, rows_ref, out_ref, q_sem, do_sem, in_sem, out_sem):
     group = own_ref.shape[1]
-    total = qb.shape[0]
+    per = group // tok
     scale = 1.0 / math.sqrt(HD)
     power = scale * math.log2(math.e)
     z = meta_ref[2 * frames]
-
-    def text(b, carry):
-        where = pl.ds(pl.multiple_of(b * tok, 32), tok)
-        qb[where] = g_ref[b, 0:tok]
-        dob[where] = g_ref[b, tok:]
-        return carry
-
-    lax.fori_loop(0, total // tok, text, 0)
+    count = meta_ref[2 * frames + 5]
+    last_tile = stat_ref.shape[0] * (group // HD) - 1
+
+    def fetch(i):
+        where = pl.ds(pl.multiple_of(i * tok, 32), tok)
+        b = z * per + i
+        return (
+            pltpu.make_async_copy(g_hbm.at[b, 0:tok], qb.at[where], q_sem.at[i]),
+            pltpu.make_async_copy(g_hbm.at[b, tok : 2 * tok], dob.at[where], do_sem.at[i]),
+        )
+
+    own_copy = pltpu.make_async_copy(own_hbm, own_ref, in_sem.at[0])
+    stat_copy = pltpu.make_async_copy(stat_hbm, stat_ref, in_sem.at[1])
+    own_copy.start()
+    stat_copy.start()
+
+    def begin(i, carry):
+        for copy in fetch(i):
+            copy.start()
+        return carry
+
+    def finish(i, carry):
+        for copy in fetch(i):
+            copy.wait()
+        return carry
+
+    lax.fori_loop(0, count, begin, 0)
     dk[...] = jnp.zeros_like(dk)
     dv[...] = jnp.zeros_like(dv)
+    tail = pl.ds(pl.multiple_of(count * tok, 32), CHUNK)
+    qb[tail] = jnp.zeros((CHUNK, HD), BF16)
+    dob[tail] = jnp.zeros((CHUNK, HD), BF16)
     lane = lax.broadcasted_iota(jnp.int32, (group, CHUNK), 1)
-    key_pos = z * group + lax.broadcasted_iota(jnp.int32, (group, 1), 0)
-    end = end_ref[...]
+    key_pos = lax.broadcasted_iota(jnp.int32, (group, 1), 0)
+    end = end_ref[...] - z * group
+    own_copy.wait()
+    stat_copy.wait()
+
+    def statistics(c, kind):
+        parts = []
+        for half in range(2):
+            tile = jnp.minimum(z * (group // HD) + 2 * c + half, last_tile)
+            at = lax.div(tile, group // HD)
+            row = kind * (group // HD) + lax.rem(tile, group // HD)
+            parts.append(stat_ref[at, pl.ds(row, 1)])
+        return jnp.concatenate(parts, axis=1)
 
     def step(c, carry):
         where = pl.ds(pl.multiple_of(c * CHUNK, CHUNK), CHUNK)
-        stat = jnp.concatenate([stat_ref[2 * c], stat_ref[2 * c + 1]], axis=1)
+        arrived = lax.div(c * CHUNK + tok - 1, tok)
+        needed = jnp.minimum(lax.div((c + 1) * CHUNK + tok - 1, tok), count)
+        lax.fori_loop(arrived, needed, finish, 0)
         q, do = qb[where], dob[where]
         s = dot_nt(own_ref[0], q)
         pos = lane + c * CHUNK
-        p = jnp.exp2((s - stat[0:1]) * power) * stat[1:2]
+        p = jnp.exp2((s - statistics(c, 0)) * power) * statistics(c, 1)
         p = jnp.where((pos >= key_pos) & (pos < end), p, 0.0)
         dv[...] += dot_nn(p.astype(BF16), do)
         d_prob = dot_nt(own_ref[1], do)
-        d_score = (p * (d_prob - stat[2:3])).astype(BF16)
+        d_score = (p * (d_prob - statistics(c, 2))).astype(BF16)
         dk[...] += dot_nn(d_score, q)
         return carry
 
-    lax.fori_loop(meta_ref[2 * frames + 4], meta_ref[2 * frames + 5], step, 0)
+    lax.fori_loop(0, meta_ref[2 * frames + 4], step, 0)
     key_grad = (dk[...] * scale).astype(BF16)
     value_grad = dv[...].astype(BF16)
-    dkv_ref[:, 0:HD] = key_grad
-    dkv_ref[:, HD:] = value_grad
-    for i in range(group // tok):
+    rows_ref[:, 0:HD] = key_grad
+    rows_ref[:, HD:] = value_grad
+    rows_copy = pltpu.make_async_copy(rows_ref, dkv_hbm, out_sem.at[0])
+    rows_copy.start()
+    for i in range(per):
         rows = slice(i * tok, (i + 1) * tok)
         out_ref[i, 0:tok] = key_grad[rows]
         out_ref[i, tok:] = value_grad[rows]
+    out_copy = pltpu.make_async_copy(out_ref, out_hbm, out_sem.at[1])
+    out_copy.start()
+    rows_copy.wait()
+    out_copy.wait()
 
 
 def proj_kernel(norm_ref, grad_ref, out_ref):
@@ -250,8 +307,12 @@
         dq_ref[:, span] = r_ref[h, tok:]
 
 
-def unpack_kernel(heads, tok, r_ref, image_ref, proj_ref, dtext_ref, dn_ref):
-    is_image = image_ref[...] == 1
+def unpack_kernel(heads, tok, meta_ref, offset_ref, count_ref, r_ref, proj_ref, dtext_ref, dn_ref):
+    frames = offset_ref.shape[1]
+    pos = meta_ref[2 * frames + 1] * tok + lax.broadcasted_iota(jnp.int32, (tok, frames), 0)
+    begin = offset_ref[...]
+    inside = (pos >= begin) & (pos < begin + count_ref[...])
+    is_image = jnp.max(inside.astype(F32), axis=1, keepdims=True) > 0.5
     parts = [None] * (2 * heads)
     for h in range(heads):
         span = slice(h * HD, (h + 1) * HD)
@@ -286,7 +347,7 @@
 
 
 def norm_grad_kernel(patch_ref, gain_ref, dn_ref, out_ref):
-    scaled, inverse = normalize_rows(patch_ref[...])
+    scaled, inverse = normalize_rows(patch_ref[0:PATCH_MOST])
     d_normed = jnp.concatenate([dn_ref[i] for i in range(dn_ref.shape[0])], axis=1).astype(F32)
     scaled_grad = d_normed * gain_ref[...]
     d_rows = (
@@ -312,6 +373,7 @@
     block = z * per + y
     smem = pl.BlockSpec(memory_space=pltpu.SMEM)
     whole = pl.BlockSpec(memory_space=pltpu.VMEM)
+    hbm = pl.BlockSpec(memory_space=pltpu.HBM)
 
     def shape(dims, kind=BF16):
         return jax.ShapeDtypeStruct(dims, kind)
@@ -328,32 +390,24 @@
         block,
         start[0, 0] // CHUNK,
         ((z + 1) * group + CHUNK - 1) // CHUNK,
-        (z * group) // CHUNK,
-        (end[group - 1, 0] + CHUNK - 1) // CHUNK,
+        (end[group - 1, 0] - z * group + CHUNK - 1) // CHUNK,
+        (end[group - 1, 0] - z * group + tok - 1) // tok,
     ]).astype(jnp.int32)
     meta = jnp.concatenate([image_offsets, patch_counts, scalars])
-    positions = block * tok + jnp.arange(tok, dtype=jnp.int32)
-    is_image = jnp.any(
-        (positions[:, None] >= image_offsets[None, :])
-        & (positions[:, None] < image_offsets[None, :] + patch_counts[None, :]),
-        axis=1, keepdims=True,
-    ).astype(jnp.int32)
-
     gain = ln_gain.reshape(1, width)
     proj = kv_proj.reshape(width, 2 * cols)
-    used = patches[:PATCH_MOST]
     packed, questions, normed = pl.pallas_call(
         lambda *refs: pack_kernel(heads, tok, *refs),
         out_shape=(
             shape((per, 2 * tok + 2 * PATCH_MOST, HD)),
             shape((per, 2 * tok, HD)),
-            shape((PATCH_MOST, width)),
+            shape((groups, PATCH_MOST, HD)),
         ),
         in_specs=[whole] * 8,
         out_specs=(whole, whole, whole),
         compiler_params=vmem(),
         name="pack",
-    )(used, gain, proj, query, text_kv, type_bias, d_out, token_types.reshape(tok, 1))
+    )(patches, gain, proj, query, text_kv, type_bias, d_out, token_types.reshape(tok, 1))
     kv_mine = lax.all_to_all(packed, "y", 0, 0, tiled=True)
     kv_all = lax.all_gather(kv_mine, "z", axis=0, tiled=True)
     questions, _ = lax.optimization_barrier((questions, kv_mine))
@@ -361,11 +415,8 @@
     q_all = lax.all_gather(q_mine, "z", axis=0, tiled=True)
 
     normed, _ = lax.optimization_barrier((normed, q_mine))
-    slices = normed.reshape(PATCH_MOST, groups, 1, HD).transpose(1, 2, 0, 3)
-    all_frames = lax.all_to_all(
-        jnp.broadcast_to(slices, (groups, per, PATCH_MOST, HD)).reshape(blocks, PATCH_MOST, HD),
-        ("z", "y"), 0, 0, tiled=True,
-    )
+    some_frames = lax.all_to_all(normed, "z", 0, 0, tiled=True)
+    all_frames = lax.all_gather(some_frames, "y", axis=0, tiled=False)
     norm_pos = pl.pallas_call(
         lambda *refs: place_kernel(frames, *refs),
         out_shape=shape((total, HD)),
@@ -377,17 +428,22 @@
     )(meta, all_frames)
     kv_all, norm_pos = lax.optimization_barrier((kv_all, norm_pos))
 
+    most_blocks = (group - 1 + EPISODE_MOST + tok - 1) // tok
     most_chunks = (EPISODE_MOST + group + CHUNK - 2) // CHUNK + 1
     answers, own_kv, stats = pl.pallas_call(
         lambda *refs: query_kernel(frames, tok, *refs),
         out_shape=(
             shape((per, 2 * tok, HD)),
             shape((2, group, HD)),
-            shape((group // HD, 8, HD), F32),
+            shape((groups, STAT_ROWS, HD), F32),
         ),
         in_specs=[smem, whole, whole, whole],
-        out_specs=(whole, whole, whole),
+        out_specs=(hbm, hbm, hbm),
         scratch_shapes=[
+            pltpu.VMEM((per, 2 * tok, HD), BF16),
+            pltpu.VMEM((2, group, HD), BF16),
+            pltpu.VMEM((groups, STAT_ROWS, HD), F32),
+            pltpu.SemaphoreType.DMA((3,)),
             pltpu.VMEM((total + PATCH_MOST, HD), F32),
             pltpu.VMEM((total + PATCH_MOST, HD), F32),
             pltpu.VMEM((total, HD), BF16),
@@ -399,12 +455,10 @@
             pltpu.VMEM((group, HD), F32),
             pltpu.VMEM((group, HD), F32),
         ],
-        compiler_params=vmem(),
+        compiler_params=vmem(62),
         name="queries",
     )(meta, start, kv_all, q_mine)
-    all_stats = lax.all_to_all(
-        jnp.broadcast_to(stats[None], (groups,) + stats.shape), "z", 0, 0, tiled=True
-    ).reshape(total // HD, 8, HD)
+    all_stats = lax.all_to_all(stats, "z", 0, 0, tiled=True)
     answers, all_stats = lax.optimization_barrier((answers, all_stats))
     returned = lax.all_to_all(answers, "y", 0, 0, tiled=True)
     att_here, dq_here = pl.pallas_call(
@@ -420,15 +474,23 @@
     d_kv, key_grads = pl.pallas_call(
         lambda *refs: key_kernel(frames, tok, *refs),
         out_shape=(shape((group, 2 * HD)), shape((per, 2 * tok, HD))),
-        in_specs=[smem] + [whole] * 4,
-        out_specs=(whole, whole),
+        in_specs=[smem, whole, hbm, hbm, hbm],
+        out_specs=(hbm, hbm),
         scratch_shapes=[
-            pltpu.VMEM((total, HD), BF16),
-            pltpu.VMEM((total, HD), BF16),
+            pltpu.VMEM((most_blocks * tok + CHUNK, HD), BF16),
+            pltpu.VMEM((most_blocks * tok + CHUNK, HD), BF16),
+            pltpu.VMEM((groups, STAT_ROWS, HD), F32),
+            pltpu.VMEM((2, group, HD), BF16),
             pltpu.VMEM((group, HD), F32),
             pltpu.VMEM((group, HD), F32),
+            pltpu.VMEM((group, 2 * HD), BF16),
+            pltpu.VMEM((per, 2 * tok, HD), BF16),
+            pltpu.SemaphoreType.DMA((most_blocks,)),
+            pltpu.SemaphoreType.DMA((most_blocks,)),
+            pltpu.SemaphoreType.DMA((2,)),
+            pltpu.SemaphoreType.DMA((2,)),
         ],
-        compiler_params=vmem(),
+        compiler_params=vmem(62),
         name="keys",
     )(meta, end, q_all, all_stats, own_kv)
     d_kv_all = lax.all_gather(d_kv, "z", axis=0, tiled=True)
@@ -436,11 +498,11 @@
     d_text_kv, terms = pl.pallas_call(
         lambda *refs: unpack_kernel(heads, tok, *refs),
         out_shape=(shape((2, tok, cols)), shape((sections, tok, width // sections))),
-        in_specs=[whole] * 3,
+        in_specs=[smem] + [whole] * 4,
         out_specs=(whole,) * 2,
         compiler_params=vmem(),
         name="unpack",
-    )(keys_back, is_image, proj)
+    )(meta, image_offsets.reshape(1, frames), patch_counts.reshape(1, frames), keys_back, proj)
 
     summed = lax.all_to_all(terms, "phase", 0, 0, tiled=True)
     routed = pl.pallas_call(
@@ -481,7 +543,7 @@
         out_specs=whole,
         compiler_params=vmem(),
         name="norm_grad",
-    )(used, gain, d_normed)
+    )(patches, gain, d_normed)
     return (
         att_here,
         dq_here,

time: 226 us -> 213 us (0.942)
  waiting for transfers between devices: 70.3 us -> 50.8 us
  blocking collectives: 60.3 us -> 77.8 us
  local copies, waits for them, and re-layouts: 20.6 us -> 9.87 us
  Pallas kernels: 16.1 us -> 21.7 us
  starting transfers between devices: 36 us -> 32.5 us
    all_to_all x2 -> x1, waiting for transfers between devices: 19.4 us -> 3.68 us  [shards(): some_frames = lax.all_to_all(normed, 'z', 0, 0, tiled=True)]
    all_gather x0 -> x1, blocking collectives: none -> 11.3 us  [shards(): all_frames = lax.all_gather(some_frames, 'y', axis=0, tiled=False)]
    unnamed x51 -> x34, local copies, waits for them, and re-layouts: 15 us -> 5.39 us
    all_to_all x1 -> x2, blocking collectives: 22.8 us -> 29.1 us  [the longest x1 19.2 us: shards(): all_stats = lax.all_to_all(stats, 'z', 0, 0, tiled=True)]
    all_gather x1, waiting for transfers between devices: 20.3 us -> 15.1 us  [shards(): kv_all = lax.all_gather(kv_mine, 'z', axis=0, tiled=True)]
    all_to_all x2 -> x1, starting transfers between devices: 13.4 us -> 8.37 us  [shards(): some_frames = lax.all_to_all(normed, 'z', 0, 0, tiled=True)]
    pallas_call x1, Pallas kernels: 5.33 us -> 7.77 us  [shards(): pl.pallas_call(lambda *refs: query_kernel(frames, tok, *refs), out_shape=...]
  transfers between devices with their start and end apart: 9 -> 8, of which waited for: 7 -> 6; matrix products, arithmetic and copies ran while one was open for 3% -> 2% of each run, Pallas kernels for 5% -> 7%
where the time goes in v3:
time: 213 us; the launch traced here: 212 us
  blocking collectives  77.8 us (37%)
  waiting for transfers between devices  50.8 us (24%)
  starting transfers between devices  32.5 us (15%)
  Pallas kernels  21.7 us (10%)
  between operations  19.2 us (9%)
  local copies, waits for them, and re-layouts  9.87 us (5%)
    all_to_all x1, blocking collectives, shards(): all_stats = lax.all_to_all(stats, 'z', 0, 0, tiled=True)  19.2 us
    all_to_all x1, waiting for transfers between devices, shards(): from_blocks = lax.all_to_all(routed, ('z', 'y'), 0, 0, tiled=True)  17.6 us
    all_to_all x1, blocking collectives, shards(): summed = lax.all_to_all(terms, 'phase', 0, 0, tiled=True)  16.2 us
    all_gather x1, waiting for transfers between devices, shards(): kv_all = lax.all_gather(kv_mine, 'z', axis=0, tiled=True)  15.1 us
    all_to_all x1, blocking collectives, shards(): kv_mine = lax.all_to_all(packed, 'y', 0, 0, tiled=True)  12.3 us
    all_gather x1, blocking collectives, shards(): all_frames = lax.all_gather(some_frames, 'y', axis=0, tiled=False)  11.3 us
    all_to_all x1, starting transfers between devices, shards(): from_blocks = lax.all_to_all(routed, ('z', 'y'), 0, 0, tiled=True)  11 us
    all_to_all x1, blocking collectives, shards(): keys_back = lax.all_to_all(key_grads, 'y', 0, 0, tiled=True)  9.9 us
  transfers between devices with their start and end apart: 8, of which 6 were waited for; matrix products, arithmetic and copies ran while one was open for 2% of the time, Pallas kernels for 7%

profile of v3, /device:TPU:1, one launch (start us, length us, event | category | flops | bytes accessed | tf_op | source)
XLA Modules:
  0.0 212.1 jit_solution(13247214843550703926)
XLA Ops:
  7.3 1.8 copy.32
  9.3 1.2 pack.1
  10.5 12.3 %all_to_all.50 = bf16[4,448,128]{2,1,0:T(8,128)(2,1)} all-to-all(bf16[4,448,128]{2,1,0:T(8,128)(2,1)S(1)} %get-tuple-element.24), channel_id=1, replica_groups=mesh['phase'=8,'z'=8,'y'=4] {'y'}, dimensions={0} | all-to-all | bytes 917504 | tf_op jit(solution)/shard_map/all_to_all | solution.py:411
  22.9 8.9 %all_to_all.51.refs_3_ = bf16[4,320,128]{2,1,0:T(8,128)(2,1)} all-to-all(bf16[4,320,128]{2,1,0:T(8,128)(2,1)S(1)} %get-tuple-element.27), channel_id=1, replica_groups=mesh['phase'=8,'z'=8,'y'=4] {'y'}, dimensions={0} | all-to-all | bytes 655360 | tf_op jit(solution)/shard_map/all_to_all | solution.py:414
  31.9 8.4 %all-to-all-start.2 = ((bf16[8,64,128]{2,1,0:T(8,128)(2,1)}), bf16[8,64,128]{2,1,0:T(8,128)(2,1)S(1)}, u32[]{:S(2)}, u32[]{:S(2)}) async-start(bf16[8,64,128]{2,1,0:T(8,128)(2,1)} %get-tuple-element.28), calls=%async_computation.2 | async-start | bytes 262144 | tf_op jit(solution)/shard_map/all_to_all | solution.py:418
  45.0 0.9 broadcast_in_dim.47.refs_1_
  46.0 3.7 %all-to-all-done.2 = bf16[8,64,128]{2,1,0:T(8,128)(2,1)S(1)} async-done(((bf16[8,64,128]{2,1,0:T(8,128)(2,1)}), bf16[8,64,128]{2,1,0:T(8,128)(2,1)S(1)}, u32[]{:S(2)}, u32[]{:S(2)}) %all-to-all-start.2) | async-done | bytes 131104 | tf_op jit(solution)/shard_map/all_to_all | solution.py:418
  49.6 11.3 %all-gather = bf16[32,64,128]{2,1,0:T(8,128)(2,1)S(1)} all-gather(bf16[8,64,128]{2,1,0:T(8,128)(2,1)S(1)} %all-to-all-done.2), channel_id=2, replica_groups=mesh['phase'=8,'z'=8,'y'=4] {'y'}, dimensions={0}, use_global_device_ids=true | all-gather | bytes 655360 | tf_op jit(solution)/shard_map/all_gather | solution.py:419
  60.9 1.2 place.1.norm_ref
  62.2 1.1 copy-done
  63.2 15.1 %all-gather.5.cloned.1.call-done.refs_2_ = bf16[32,448,128]{2,1,0:T(8,128)(2,1)} async-done(((bf16[4,448,128]{2,1,0:T(8,128)(2,1)}), bf16[32,448,128]{2,1,0:T(8,128)(2,1)}) %all-gather.5.cloned.1.call-update) | async-done | bytes 3670032 | tf_op jit(solution)/shard_map/all_gather | solution.py:412
  78.3 7.8 %queries.1 = (bf16[4,320,128]{2,1,0:T(8,128)(2,1)}, bf16[2,640,128]{2,1,0:T(8,128)(2,1)}, f32[8,16,128]{2,1,0:T(8,128)}) custom-call(s32[70]{0:T(128)} %copy-done.8, s32[640,1]{1,0:T(8,128)} %broadcast_in_dim.47.refs_1_, bf16[32,448,128]{2,1,0:T(8,128)(2,1)} %all-gather.5.cloned.1.call-done.refs_2_, bf16[4,320,128]{2,1,0:T(8,128)(2,1)} %all_to_all.51.refs_3_), custom_call_target="tpu_custom_call" | custom-call | tf_op jit(solution)/shard_map/queries/pallas_call | solution.py:433
  86.1 19.2 %all_to_all.52.refs_3_ = f32[8,16,128]{2,1,0:T(8,128)} all-to-all(f32[8,16,128]{2,1,0:T(8,128)} %get-tuple-element.31), channel_id=1, replica_groups=mesh['phase'=8,'z'=8,'y'=4] {'z'}, dimensions={0} | all-to-all | bytes 131072 | tf_op jit(solution)/shard_map/all_to_all | solution.py:461
  105.3 4.1 %all-to-all-start.4 = ((bf16[4,320,128]{2,1,0:T(8,128)(2,1)}), bf16[4,320,128]{2,1,0:T(8,128)(2,1)S(1)}, u32[]{:S(2)}, u32[]{:S(2)}) async-start(bf16[4,320,128]{2,1,0:T(8,128)(2,1)} %get-tuple-element.32), calls=%async_computation.4 | async-start | bytes 655360 | tf_op jit(solution)/shard_map/all_to_all | solution.py:463
  109.4 0.9 broadcast_in_dim.48.refs_1_
  110.3 9.4 %all-gather.7.cloned.1.call-done.refs_2_ = bf16[32,320,128]{2,1,0:T(8,128)(2,1)} async-done(((bf16[4,320,128]{2,1,0:T(8,128)(2,1)}), bf16[32,320,128]{2,1,0:T(8,128)(2,1)}) %all-gather.7.cloned.1.call-update) | async-done | bytes 2621456 | tf_op jit(solution)/shard_map/all_gather | solution.py:415
  119.7 5.3 %keys.1 = (bf16[640,256]{1,0:T(8,128)(2,1)}, bf16[4,320,128]{2,1,0:T(8,128)(2,1)}) custom-call(s32[70]{0:T(128)} %copy-done.8, s32[640,1]{1,0:T(8,128)} %broadcast_in_dim.48.refs_1_, bf16[32,320,128]{2,1,0:T(8,128)(2,1)} %all-gather.7.cloned.1.call-done.refs_2_, f32[8,16,128]{2,1,0:T(8,128)} %all_to_all.52.refs_3_, ...), custom_call_target="tpu_custom_call" | custom-call | tf_op jit(solution)/shard_map/keys/pallas_call | solution.py:474
  125.1 9.9 %all_to_all.53.refs_3_ = bf16[4,320,128]{2,1,0:T(8,128)(2,1)S(1)} all-to-all(bf16[4,320,128]{2,1,0:T(8,128)(2,1)} %get-tuple-element.38), channel_id=1, replica_groups=mesh['phase'=8,'z'=8,'y'=4] {'y'}, dimensions={0} | all-to-all | bytes 655360 | tf_op jit(solution)/shard_map/all_to_all | solution.py:497
  135.0 1.4 unpack.1
  136.4 16.2 %all_to_all.54.refs_1_ = bf16[8,160,128]{2,1,0:T(8,128)(2,1)S(1)} all-to-all(bf16[8,160,128]{2,1,0:T(8,128)(2,1)S(1)} %get-tuple-element.42), channel_id=1, replica_groups=mesh['phase'=8,'z'=8,'y'=4] {'phase'}, dimensions={0} | all-to-all | bytes 655360 | tf_op jit(solution)/shard_map/all_to_all | solution.py:507
  152.6 1.7 route.1
  154.3 11.0 %all-to-all-start.8 = ((bf16[32,64,128]{2,1,0:T(8,128)(2,1)}), bf16[32,64,128]{2,1,0:T(8,128)(2,1)S(1)}, u32[]{:S(2)}, u32[]{:S(2)}) async-start(bf16[32,64,128]{2,1,0:T(8,128)(2,1)} %route.1), calls=%async_computation.8 | async-start | bytes 1048576 | tf_op jit(solution)/shard_map/all_to_all | solution.py:517
  167.9 17.6 %all-to-all-done.8 = bf16[32,64,128]{2,1,0:T(8,128)(2,1)S(1)} async-done(((bf16[32,64,128]{2,1,0:T(8,128)(2,1)}), bf16[32,64,128]{2,1,0:T(8,128)(2,1)S(1)}, u32[]{:S(2)}, u32[]{:S(2)}) %all-to-all-start.8) | async-done | bytes 524320 | tf_op jit(solution)/shard_map/all_to_all | solution.py:517
  186.2 5.5 %all-to-all-start.9 = ((bf16[8,64,128]{2,1,0:T(8,128)(2,1)}), bf16[8,64,128]{2,1,0:T(8,128)(2,1)S(1)}, u32[]{:S(2)}, u32[]{:S(2)}) async-start(bf16[8,64,128]{2,1,0:T(8,128)(2,1)} %broadcast_in_dim.46), calls=%async_computation.9 | async-start | bytes 262144 | tf_op jit(solution)/shard_map/all_to_all | solution.py:520
  191.7 1.7 copy-done.2
  193.4 1.2 proj_grad.1
  194.6 2.3 %all-to-all-done.9.dn_ref = bf16[8,64,128]{2,1,0:T(8,128)(2,1)S(1)} async-done(((bf16[8,64,128]{2,1,0:T(8,128)(2,1)}), bf16[8,64,128]{2,1,0:T(8,128)(2,1)S(1)}, u32[]{:S(2)}, u32[]{:S(2)}) %all-to-all-start.9) | async-done | bytes 131104 | tf_op jit(solution)/shard_map/all_to_all | solution.py:520
  197.0 3.3 %all-to-all-start.6 = ((bf16[4,64,128]{2,1,0:T(8,128)(2,1)}), bf16[4,64,128]{2,1,0:T(8,128)(2,1)S(1)}, u32[]{:S(2)}, u32[]{:S(2)}) async-start(bf16[4,64,128]{2,1,0:T(8,128)(2,1)} %proj_grad.1), calls=%async_computation.6 | async-start | bytes 131072 | tf_op jit(solution)/shard_map/all_to_all | solution.py:532
  200.3 0.7 unpack_queries.1
  201.0 1.1 norm_grad.1
  202.1 2.6 %all-to-all-done.6 = bf16[4,64,128]{2,1,0:T(8,128)(2,1)S(1)} async-done(((bf16[4,64,128]{2,1,0:T(8,128)(2,1)}), bf16[4,64,128]{2,1,0:T(8,128)(2,1)S(1)}, u32[]{:S(2)}, u32[]{:S(2)}) %all-to-all-start.6) | async-done | bytes 65568 | tf_op jit(solution)/shard_map/all_to_all | solution.py:532
  204.9 0.7 copy.31
  (51 shorter events, 3.2 us)
Async XLA Ops:
  7.2 1.9 copy-start.15
  7.2 2.0 copy-start.10
  7.2 2.0 copy-start.3
  7.2 2.0 copy-start.6
  7.2 2.0 copy-start.5
  7.2 2.0 copy-start.13
  7.2 2.0 copy-start.7
  7.2 71.1 %all-gather.5.cloned.1.call-start = ((), (), s32[]{:S(2)}) async-start(), calls=%async_computation.10 | async-start | bytes 4128768 | tf_op jit(solution)/shard_map/all_gather | solution.py:412
  9.1 22.8 %copy-start.14 = (s32[5120]{0:T(1024)S(1)}, s32[5120]{0:T(1024)}, u32[]{:S(2)}) copy-start(s32[5120]{0:T(1024)} %param.21) | copy-start | bytes 61444
  9.3 36.6 %copy-start.11 = (s32[32]{0:T(128)S(1)}, s32[32]{0:T(128)}, u32[]{:S(2)}) copy-start(s32[32]{0:T(128)} %param.18) | copy-start | bytes 388
  9.3 36.6 %copy-start.12 = (s32[32]{0:T(128)S(1)}, s32[32]{0:T(128)}, u32[]{:S(2)}) copy-start(s32[32]{0:T(128)} %param.19) | copy-start | bytes 388
  22.8 96.9 %all-gather.7.cloned.1.call-start = ((), (), s32[]{:S(2)}) async-start(), calls=%async_computation.11 | async-start | bytes 2949120 | tf_op jit(solution)/shard_map/all_gather | solution.py:415
  31.9 17.7 %all-to-all-start.2 = ((bf16[8,64,128]{2,1,0:T(8,128)(2,1)}), bf16[8,64,128]{2,1,0:T(8,128)(2,1)S(1)}, u32[]{:S(2)}, u32[]{:S(2)}) async-start(bf16[8,64,128]{2,1,0:T(8,128)(2,1)} %get-tuple-element.28), calls=%async_computation.2 | async-start | bytes 262144 | tf_op jit(solution)/shard_map/all_to_all | solution.py:418
  46.0 32.4 %copy-start.8 = (s32[70]{0:T(128)}, s32[70]{0:T(128)S(1)}, u32[]{:S(2)}) copy-start(s32[70]{0:T(128)S(1)} %concatenate.3.refs_0_) | copy-start | bytes 844
  62.2 1.1 copy-start
  105.3 29.7 %copy-start.9 = (s32[70]{0:T(128)S(1)}, s32[70]{0:T(128)}, u32[]{:S(2)}) copy-start(s32[70]{0:T(128)} %copy-done.8) | copy-start | bytes 844
  105.3 14.5 %all-to-all-start.4 = ((bf16[4,320,128]{2,1,0:T(8,128)(2,1)}), bf16[4,320,128]{2,1,0:T(8,128)(2,1)S(1)}, u32[]{:S(2)}, u32[]{:S(2)}) async-start(bf16[4,320,128]{2,1,0:T(8,128)(2,1)} %get-tuple-element.32), calls=%async_computation.4 | async-start | bytes 655360 | tf_op jit(solution)/shard_map/all_to_all | solution.py:463
  109.4 82.3 %all-gather.9.cloned.1.call-start = ((), (), s32[]{:S(2)}) async-start(), calls=%async_computation.12 | async-start | bytes 2949120 | tf_op jit(solution)/shard_map/all_gather | solution.py:496
  135.0 56.7 %copy-start.1 = (bf16[5120,128]{1,0:T(8,128)(2,1)S(1)}, bf16[5120,128]{1,0:T(8,128)(2,1)}, u32[]{:S(2)}) copy-start(bf16[5120,128]{1,0:T(8,128)(2,1)} %copy-done) | copy-start | bytes 3932164
  154.3 46.7 %copy-start.4 = (bf16[256,1024]{1,0:T(8,128)(2,1)S(1)}, bf16[256,1024]{1,0:T(8,128)(2,1)}, u32[]{:S(2)}) copy-start(bf16[256,1024]{1,0:T(8,128)(2,1)} %patch_ref.1) | copy-start | bytes 1572868
  154.3 31.2 %all-to-all-start.8 = ((bf16[32,64,128]{2,1,0:T(8,128)(2,1)}), bf16[32,64,128]{2,1,0:T(8,128)(2,1)S(1)}, u32[]{:S(2)}, u32[]{:S(2)}) async-start(bf16[32,64,128]{2,1,0:T(8,128)(2,1)} %route.1), calls=%async_computation.8 | async-start | bytes 1048576 | tf_op jit(solution)/shard_map/all_to_all | solution.py:517
  186.2 10.8 %all-to-all-start.9 = ((bf16[8,64,128]{2,1,0:T(8,128)(2,1)}), bf16[8,64,128]{2,1,0:T(8,128)(2,1)S(1)}, u32[]{:S(2)}, u32[]{:S(2)}) async-start(bf16[8,64,128]{2,1,0:T(8,128)(2,1)} %broadcast_in_dim.46), calls=%async_computation.9 | async-start | bytes 262144 | tf_op jit(solution)/shard_map/all_to_all | solution.py:520
  191.7 1.7 copy-start.2
  197.0 7.8 %all-to-all-start.6 = ((bf16[4,64,128]{2,1,0:T(8,128)(2,1)}), bf16[4,64,128]{2,1,0:T(8,128)(2,1)S(1)}, u32[]{:S(2)}, u32[]{:S(2)}) async-start(bf16[4,64,128]{2,1,0:T(8,128)(2,1)} %proj_grad.1), calls=%async_computation.6 | async-start | bytes 131072 | tf_op jit(solution)/shard_map/all_to_all | solution.py:532
Sparse Core Ops, SparseCore 0:
  22.9 55.3 all-gather.4
  80.1 39.5 all-gather.6
  125.2 52.8 all-gather.8

commit v4 on v3

--- a/solution.py
+++ b/solution.py
@@ -1,3 +1,4 @@
+import functools
 import math
 
 import jax
@@ -69,7 +70,7 @@
 
 
 def place_kernel(frames, meta_ref, rows_ref, out_ref, scratch):
-    total = out_ref.shape[0]
+    total = out_ref.shape[1]
     per = rows_ref.shape[0]
     scratch[...] = jnp.zeros_like(scratch)
     row = lax.broadcasted_iota(jnp.int32, (PATCH_MOST, HD), 0)
@@ -85,7 +86,7 @@
 
     def low(c, carry):
         where = pl.ds(pl.multiple_of(c * CHUNK, CHUNK), CHUNK)
-        out_ref[where] = scratch[where].astype(BF16)
+        out_ref[:, where] = jnp.transpose(scratch[where]).astype(BF16)
         return carry
 
     lax.fori_loop(0, total // CHUNK, low, 0)
@@ -259,23 +260,29 @@
             parts.append(stat_ref[at, pl.ds(row, 1)])
         return jnp.concatenate(parts, axis=1)
 
-    def step(c, carry):
+    def step(masked, c, carry):
         where = pl.ds(pl.multiple_of(c * CHUNK, CHUNK), CHUNK)
         arrived = lax.div(c * CHUNK + tok - 1, tok)
         needed = jnp.minimum(lax.div((c + 1) * CHUNK + tok - 1, tok), count)
         lax.fori_loop(arrived, needed, finish, 0)
         q, do = qb[where], dob[where]
         s = dot_nt(own_ref[0], q)
-        pos = lane + c * CHUNK
         p = jnp.exp2((s - statistics(c, 0)) * power) * statistics(c, 1)
-        p = jnp.where((pos >= key_pos) & (pos < end), p, 0.0)
+        if masked:
+            pos = lane + c * CHUNK
+            p = jnp.where((pos >= key_pos) & (pos < end), p, 0.0)
         dv[...] += dot_nn(p.astype(BF16), do)
         d_prob = dot_nt(own_ref[1], do)
         d_score = (p * (d_prob - statistics(c, 2))).astype(BF16)
         dk[...] += dot_nn(d_score, q)
         return carry
 
-    lax.fori_loop(0, meta_ref[2 * frames + 4], step, 0)
+    chunks = meta_ref[2 * frames + 4]
+    after = jnp.minimum((group + CHUNK - 1) // CHUNK, chunks)
+    shared = jnp.maximum(meta_ref[2 * frames + 6], after)
+    lax.fori_loop(0, after, functools.partial(step, True), 0)
+    lax.fori_loop(after, shared, functools.partial(step, False), 0)
+    lax.fori_loop(shared, chunks, functools.partial(step, True), 0)
     key_grad = (dk[...] * scale).astype(BF16)
     value_grad = dv[...].astype(BF16)
     rows_ref[:, 0:HD] = key_grad
@@ -293,7 +300,8 @@
 
 
 def proj_kernel(norm_ref, grad_ref, out_ref):
-    low = dot_tn(norm_ref[...], grad_ref[...]).astype(BF16)
+    total = dot_nn(norm_ref[...], grad_ref[...])
+    low = total.astype(BF16)
     rows = out_ref.shape[1] // 2
     for i in range(out_ref.shape[0]):
         out_ref[i, 0:rows] = low[i * rows : (i + 1) * rows, 0:HD]
@@ -326,24 +334,31 @@
         dn_ref[i] = dot_nt(grads, proj_ref[i * HD : (i + 1) * HD]).astype(BF16)
 
 
-def route_kernel(frames, tok, meta_ref, dn_ref, out_ref, scratch):
-    first = meta_ref[2 * frames + 1] * tok
+def sum_kernel(dn_ref, out_ref):
     total = dn_ref[0].astype(F32)
     for i in range(1, dn_ref.shape[0]):
         total = total + dn_ref[i].astype(F32)
-    scratch[...] = jnp.zeros_like(scratch)
-    scratch[0:tok] = total
+    low = total.astype(BF16)
+    for i in range(out_ref.shape[0]):
+        out_ref[i] = low
+
+
+def route_kernel(frames, meta_ref, rows_ref, out_ref, scratch):
+    per, tok = rows_ref.shape[0], rows_ref.shape[1]
+    group = per * tok
+    z = meta_ref[2 * frames]
+    y = meta_ref[2 * frames + 1] - z * per
+    for i in range(per):
+        scratch[i * tok : (i + 1) * tok] = rows_ref[i].astype(F32)
+    scratch[group:] = jnp.zeros((PATCH_MOST, HD), F32)
     row = lax.broadcasted_iota(jnp.int32, (PATCH_MOST, HD), 0)
-
-    def one(f, carry):
-        offset = meta_ref[f] - first
-        here = (offset >= 0) & (offset < tok)
+    for i in range(out_ref.shape[0]):
+        f = i * per + y
+        offset = meta_ref[f] - z * group
+        here = (offset >= 0) & (offset < group)
         live = jnp.where(here, meta_ref[frames + f], 0)
         rows = scratch[pl.ds(jnp.where(here, offset, 0), PATCH_MOST)]
-        out_ref[f] = jnp.where(row < live, rows, 0.0).astype(BF16)
-        return carry
-
-    lax.fori_loop(0, frames, one, 0)
+        out_ref[i] = jnp.where(row < live, rows, 0.0).astype(BF16)
 
 
 def norm_grad_kernel(patch_ref, gain_ref, dn_ref, out_ref):
@@ -392,6 +407,7 @@
         ((z + 1) * group + CHUNK - 1) // CHUNK,
         (end[group - 1, 0] - z * group + CHUNK - 1) // CHUNK,
         (end[group - 1, 0] - z * group + tok - 1) // tok,
+        (end[0, 0] - z * group) // CHUNK,
     ]).astype(jnp.int32)
     meta = jnp.concatenate([image_offsets, patch_counts, scalars])
     gain = ln_gain.reshape(1, width)
@@ -419,7 +435,7 @@
     all_frames = lax.all_gather(some_frames, "y", axis=0, tiled=False)
     norm_pos = pl.pallas_call(
         lambda *refs: place_kernel(frames, *refs),
-        out_shape=shape((total, HD)),
+        out_shape=shape((HD, total)),
         in_specs=[smem, whole],
         out_specs=whole,
         scratch_shapes=[pltpu.VMEM((total + PATCH_MOST, HD), F32)],
@@ -505,18 +521,27 @@
     )(meta, image_offsets.reshape(1, frames), patch_counts.reshape(1, frames), keys_back, proj)
 
     summed = lax.all_to_all(terms, "phase", 0, 0, tiled=True)
+    here = pl.pallas_call(
+        sum_kernel,
+        out_shape=shape((per, tok, HD)),
+        in_specs=[whole],
+        out_specs=whole,
+        compiler_params=vmem(),
+        name="sum",
+    )(summed)
+    of_group = lax.all_to_all(here, "y", 0, 0, tiled=True)
     routed = pl.pallas_call(
-        lambda *refs: route_kernel(frames, tok, *refs),
-        out_shape=shape((frames, PATCH_MOST, HD)),
+        lambda *refs: route_kernel(frames, *refs),
+        out_shape=shape((groups, PATCH_MOST, HD)),
         in_specs=[smem, whole],
         out_specs=whole,
-        scratch_shapes=[pltpu.VMEM((tok + PATCH_MOST, HD), F32)],
+        scratch_shapes=[pltpu.VMEM((group + PATCH_MOST, HD), F32)],
         compiler_params=vmem(),
         name="route",
-    )(meta, summed)
-    from_blocks = lax.all_to_all(routed, ("z", "y"), 0, 0, tiled=True)
-    source = lax.dynamic_index_in_dim(image_offsets, block, keepdims=False) // tok
-    d_slice = lax.dynamic_index_in_dim(from_blocks, source, keepdims=False)
+    )(meta, of_group)
+    from_groups = lax.all_to_all(routed, "z", 0, 0, tiled=True)
+    source = lax.dynamic_index_in_dim(image_offsets, block, keepdims=False) // group
+    d_slice = lax.dynamic_index_in_dim(from_groups, source, keepdims=False)
     d_normed = lax.all_to_all(
         jnp.broadcast_to(d_slice[None], (sections,) + d_slice.shape), "phase", 0, 0, tiled=True
     )
@@ -524,7 +549,7 @@
     proj_head = pl.pallas_call(
         proj_kernel,
         out_shape=shape((per, 2 * proj_rows, HD)),
-        in_specs=[whole] * 2,
+        in_specs=[whole, whole],
         out_specs=whole,
         compiler_params=vmem(),
         name="proj_grad",

time: 213 us -> 208 us (0.977)
  waiting for transfers between devices: 50.8 us -> 33.4 us
  blocking collectives: 77.8 us -> 88.1 us
  Pallas kernels: 21.7 us -> 29.9 us
  starting transfers between devices: 32.5 us -> 25.6 us
    all_to_all x1, waiting for transfers between devices: 17.6 us -> 5.32 us  [shards(): from_groups = lax.all_to_all(routed, 'z', 0, 0, tiled=True)]
    all_to_all x1, starting transfers between devices: 11 us -> 3.5 us  [shards(): from_groups = lax.all_to_all(routed, 'z', 0, 0, tiled=True)]
    all_to_all x0 -> x1, blocking collectives: none -> 7.36 us  [shards(): of_group = lax.all_to_all(here, 'y', 0, 0, tiled=True)]
    pallas_call x1, Pallas kernels: 5.31 us -> 12.1 us  [shards(): pl.pallas_call(lambda *refs: key_kernel(frames, tok, *refs), out_shape=(s...]
    all_gather x1, waiting for transfers between devices: 9.45 us -> 6.77 us  [shards(): q_all = lax.all_gather(q_mine, 'z', axis=0, tiled=True)]
    all_to_all x1, blocking collectives: 19.2 us -> 21.8 us  [shards(): all_stats = lax.all_to_all(stats, 'z', 0, 0, tiled=True)]
  transfers between devices with their start and end apart: 8 -> 8, of which waited for: 6 -> 6; matrix products, arithmetic and copies ran while one was open for 2% -> 2% of each run, Pallas kernels for 7% -> 8%
where the time goes in v4:
time: 208 us; the launch traced here: 207 us
  blocking collectives  88.1 us (42%)
  waiting for transfers between devices  33.4 us (16%)
  Pallas kernels  29.9 us (14%)
  starting transfers between devices  25.6 us (12%)
  between operations  19.9 us (10%)
  local copies, waits for them, and re-layouts  9.87 us (5%)
    all_to_all x1, blocking collectives, shards(): all_stats = lax.all_to_all(stats, 'z', 0, 0, tiled=True)  21.8 us
    all_to_all x1, blocking collectives, shards(): summed = lax.all_to_all(terms, 'phase', 0, 0, tiled=True)  16.5 us
    all_gather x1, waiting for transfers between devices, shards(): kv_all = lax.all_gather(kv_mine, 'z', axis=0, tiled=True)  13 us
    all_to_all x1, blocking collectives, shards(): kv_mine = lax.all_to_all(packed, 'y', 0, 0, tiled=True)  12.3 us
    pallas_call x1, Pallas kernels, shards(): pl.pallas_call(lambda *refs: key_kernel(frames, tok, *refs), out_shape=(s...  12.1 us
    all_gather x1, blocking collectives, shards(): all_frames = lax.all_gather(some_frames, 'y', axis=0, tiled=False)  11.3 us
    all_to_all x1, blocking collectives, shards(): keys_back = lax.all_to_all(key_grads, 'y', 0, 0, tiled=True)  10 us
    all_to_all x1, blocking collectives, shards(): q_mine = lax.all_to_all(questions, 'y', 0, 0, tiled=True)  8.95 us
  transfers between devices with their start and end apart: 8, of which 6 were waited for; matrix products, arithmetic and copies ran while one was open for 2% of the time, Pallas kernels for 8%

profile of v4, /device:TPU:1, one launch (start us, length us, event | category | flops | bytes accessed | tf_op | source)
XLA Modules:
  0.0 207.1 jit_solution(1492359528863025507)
XLA Ops:
  7.3 1.8 copy.32
  9.3 1.2 pack.1
  10.5 12.3 %all_to_all.55 = bf16[4,448,128]{2,1,0:T(8,128)(2,1)} all-to-all(bf16[4,448,128]{2,1,0:T(8,128)(2,1)S(1)} %get-tuple-element.24), channel_id=1, replica_groups=mesh['phase'=8,'z'=8,'y'=4] {'y'}, dimensions={0} | all-to-all | bytes 917504 | tf_op jit(solution)/shard_map/all_to_all | solution.py:427
  22.9 8.9 %all_to_all.56.refs_3_ = bf16[4,320,128]{2,1,0:T(8,128)(2,1)} all-to-all(bf16[4,320,128]{2,1,0:T(8,128)(2,1)S(1)} %get-tuple-element.27), channel_id=1, replica_groups=mesh['phase'=8,'z'=8,'y'=4] {'y'}, dimensions={0} | all-to-all | bytes 655360 | tf_op jit(solution)/shard_map/all_to_all | solution.py:430
  32.1 8.4 %all-to-all-start.2 = ((bf16[8,64,128]{2,1,0:T(8,128)(2,1)}), bf16[8,64,128]{2,1,0:T(8,128)(2,1)S(1)}, u32[]{:S(2)}, u32[]{:S(2)}) async-start(bf16[8,64,128]{2,1,0:T(8,128)(2,1)} %get-tuple-element.28), calls=%async_computation.2 | async-start | bytes 262144 | tf_op jit(solution)/shard_map/all_to_all | solution.py:434
  45.6 0.9 broadcast_in_dim.47.refs_1_
  46.6 3.2 %all-to-all-done.2 = bf16[8,64,128]{2,1,0:T(8,128)(2,1)S(1)} async-done(((bf16[8,64,128]{2,1,0:T(8,128)(2,1)}), bf16[8,64,128]{2,1,0:T(8,128)(2,1)S(1)}, u32[]{:S(2)}, u32[]{:S(2)}) %all-to-all-start.2) | async-done | bytes 131104 | tf_op jit(solution)/shard_map/all_to_all | solution.py:434
  49.8 11.3 %all-gather = bf16[32,64,128]{2,1,0:T(8,128)(2,1)S(1)} all-gather(bf16[8,64,128]{2,1,0:T(8,128)(2,1)S(1)} %all-to-all-done.2), channel_id=2, replica_groups=mesh['phase'=8,'z'=8,'y'=4] {'y'}, dimensions={0}, use_global_device_ids=true | all-gather | bytes 655360 | tf_op jit(solution)/shard_map/all_gather | solution.py:435
  61.1 3.1 %place.1.norm_ref = bf16[128,5120]{1,0:T(8,128)(2,1)S(1)} custom-call(s32[71]{0:T(128)S(1)} %concatenate.3.refs_0_, bf16[4,8,64,128]{3,2,1,0:T(8,128)(2,1)S(1)} %bitcast.30), custom_call_target="tpu_custom_call" | custom-call | tf_op jit(solution)/shard_map/place/pallas_call | solution.py:436
  64.2 1.1 copy-done
  65.3 13.0 %all-gather.5.cloned.1.call-done.refs_2_ = bf16[32,448,128]{2,1,0:T(8,128)(2,1)} async-done(((bf16[4,448,128]{2,1,0:T(8,128)(2,1)}), bf16[32,448,128]{2,1,0:T(8,128)(2,1)}) %all-gather.5.cloned.1.call-update) | async-done | bytes 3670032 | tf_op jit(solution)/shard_map/all_gather | solution.py:428
  78.3 7.8 %queries.1 = (bf16[4,320,128]{2,1,0:T(8,128)(2,1)}, bf16[2,640,128]{2,1,0:T(8,128)(2,1)}, f32[8,16,128]{2,1,0:T(8,128)}) custom-call(s32[71]{0:T(128)} %copy-done.8, s32[640,1]{1,0:T(8,128)} %broadcast_in_dim.47.refs_1_, bf16[32,448,128]{2,1,0:T(8,128)(2,1)} %all-gather.5.cloned.1.call-done.refs_2_, bf16[4,320,128]{2,1,0:T(8,128)(2,1)} %all_to_all.56.refs_3_), custom_call_target="tpu_custom_call" | custom-call | tf_op jit(solution)/shard_map/queries/pallas_call | solution.py:449
  86.1 21.8 %all_to_all.57.refs_3_ = f32[8,16,128]{2,1,0:T(8,128)} all-to-all(f32[8,16,128]{2,1,0:T(8,128)} %get-tuple-element.31), channel_id=1, replica_groups=mesh['phase'=8,'z'=8,'y'=4] {'z'}, dimensions={0} | all-to-all | bytes 131072 | tf_op jit(solution)/shard_map/all_to_all | solution.py:477
  107.9 4.1 %all-to-all-start.4 = ((bf16[4,320,128]{2,1,0:T(8,128)(2,1)}), bf16[4,320,128]{2,1,0:T(8,128)(2,1)S(1)}, u32[]{:S(2)}, u32[]{:S(2)}) async-start(bf16[4,320,128]{2,1,0:T(8,128)(2,1)} %get-tuple-element.32), calls=%async_computation.4 | async-start | bytes 655360 | tf_op jit(solution)/shard_map/all_to_all | solution.py:479
  112.0 0.9 broadcast_in_dim.48.refs_1_
  112.9 6.8 %all-gather.7.cloned.1.call-done.refs_2_ = bf16[32,320,128]{2,1,0:T(8,128)(2,1)} async-done(((bf16[4,320,128]{2,1,0:T(8,128)(2,1)}), bf16[32,320,128]{2,1,0:T(8,128)(2,1)}) %all-gather.7.cloned.1.call-update) | async-done | bytes 2621456 | tf_op jit(solution)/shard_map/all_gather | solution.py:431
  119.7 12.1 %keys.1 = (bf16[640,256]{1,0:T(8,128)(2,1)}, bf16[4,320,128]{2,1,0:T(8,128)(2,1)}) custom-call(s32[71]{0:T(128)} %copy-done.8, s32[640,1]{1,0:T(8,128)} %broadcast_in_dim.48.refs_1_, bf16[32,320,128]{2,1,0:T(8,128)(2,1)} %all-gather.7.cloned.1.call-done.refs_2_, f32[8,16,128]{2,1,0:T(8,128)} %all_to_all.57.refs_3_, ...), custom_call_target="tpu_custom_call" | custom-call | tf_op jit(solution)/shard_map/keys/pallas_call | solution.py:490
  131.8 10.0 %all_to_all.58.refs_3_ = bf16[4,320,128]{2,1,0:T(8,128)(2,1)S(1)} all-to-all(bf16[4,320,128]{2,1,0:T(8,128)(2,1)} %get-tuple-element.38), channel_id=1, replica_groups=mesh['phase'=8,'z'=8,'y'=4] {'y'}, dimensions={0} | all-to-all | bytes 655360 | tf_op jit(solution)/shard_map/all_to_all | solution.py:513
  141.9 1.4 unpack.1
  143.3 16.5 %all_to_all.59.dn_ref = bf16[8,160,128]{2,1,0:T(8,128)(2,1)S(1)} all-to-all(bf16[8,160,128]{2,1,0:T(8,128)(2,1)S(1)} %get-tuple-element.42), channel_id=1, replica_groups=mesh['phase'=8,'z'=8,'y'=4] {'phase'}, dimensions={0} | all-to-all | bytes 655360 | tf_op jit(solution)/shard_map/all_to_all | solution.py:523
  159.8 7.4 %all_to_all.60.refs_1_ = bf16[4,160,128]{2,1,0:T(8,128)(2,1)S(1)} all-to-all(bf16[4,160,128]{2,1,0:T(8,128)(2,1)S(1)} %sum.1), channel_id=1, replica_groups=mesh['phase'=8,'z'=8,'y'=4] {'y'}, dimensions={0} | all-to-all | bytes 327680 | tf_op jit(solution)/shard_map/all_to_all | solution.py:532
  167.2 1.2 route.1
  168.4 3.5 %all-to-all-start.9 = ((bf16[8,64,128]{2,1,0:T(8,128)(2,1)}), bf16[8,64,128]{2,1,0:T(8,128)(2,1)S(1)}, u32[]{:S(2)}, u32[]{:S(2)}) async-start(bf16[8,64,128]{2,1,0:T(8,128)(2,1)} %route.1), calls=%async_computation.9 | async-start | bytes 262144 | tf_op jit(solution)/shard_map/all_to_all | solution.py:542
  174.5 5.3 %all-to-all-done.9 = bf16[8,64,128]{2,1,0:T(8,128)(2,1)S(1)} async-done(((bf16[8,64,128]{2,1,0:T(8,128)(2,1)}), bf16[8,64,128]{2,1,0:T(8,128)(2,1)S(1)}, u32[]{:S(2)}, u32[]{:S(2)}) %all-to-all-start.9) | async-done | bytes 131104 | tf_op jit(solution)/shard_map/all_to_all | solution.py:542
  180.5 6.3 %all-to-all-start.10 = ((bf16[8,64,128]{2,1,0:T(8,128)(2,1)}), bf16[8,64,128]{2,1,0:T(8,128)(2,1)S(1)}, u32[]{:S(2)}, u32[]{:S(2)}) async-start(bf16[8,64,128]{2,1,0:T(8,128)(2,1)} %broadcast_in_dim.46), calls=%async_computation.10 | async-start | bytes 262144 | tf_op jit(solution)/shard_map/all_to_all | solution.py:545
  186.7 1.7 copy-done.2
  188.5 1.1 proj_grad.1
  189.6 2.4 %all-to-all-done.10.dn_ref = bf16[8,64,128]{2,1,0:T(8,128)(2,1)S(1)} async-done(((bf16[8,64,128]{2,1,0:T(8,128)(2,1)}), bf16[8,64,128]{2,1,0:T(8,128)(2,1)S(1)}, u32[]{:S(2)}, u32[]{:S(2)}) %all-to-all-start.10) | async-done | bytes 131104 | tf_op jit(solution)/shard_map/all_to_all | solution.py:545
  192.0 3.3 %all-to-all-start.6 = ((bf16[4,64,128]{2,1,0:T(8,128)(2,1)}), bf16[4,64,128]{2,1,0:T(8,128)(2,1)S(1)}, u32[]{:S(2)}, u32[]{:S(2)}) async-start(bf16[4,64,128]{2,1,0:T(8,128)(2,1)} %proj_grad.1), calls=%async_computation.6 | async-start | bytes 131072 | tf_op jit(solution)/shard_map/all_to_all | solution.py:557
  195.3 0.7 unpack_queries.1
  196.1 1.1 norm_grad.1
  197.2 2.6 %all-to-all-done.6 = bf16[4,64,128]{2,1,0:T(8,128)(2,1)S(1)} async-done(((bf16[4,64,128]{2,1,0:T(8,128)(2,1)}), bf16[4,64,128]{2,1,0:T(8,128)(2,1)S(1)}, u32[]{:S(2)}, u32[]{:S(2)}) %all-to-all-start.6) | async-done | bytes 65568 | tf_op jit(solution)/shard_map/all_to_all | solution.py:557
  (53 shorter events, 4.0 us)
Async XLA Ops:
  7.2 1.9 copy-start.15
  7.2 2.0 copy-start.10
  7.2 2.0 copy-start.3
  7.2 2.0 copy-start.6
  7.2 2.0 copy-start.5
  7.2 2.0 copy-start.13
  7.2 2.0 copy-start.7
  7.2 71.1 %all-gather.5.cloned.1.call-start = ((), (), s32[]{:S(2)}) async-start(), calls=%async_computation.11 | async-start | bytes 4128768 | tf_op jit(solution)/shard_map/all_gather | solution.py:428
  9.1 22.8 %copy-start.14 = (s32[5120]{0:T(1024)S(1)}, s32[5120]{0:T(1024)}, u32[]{:S(2)}) copy-start(s32[5120]{0:T(1024)} %param.21) | copy-start | bytes 61444
  9.3 37.2 %copy-start.11 = (s32[32]{0:T(128)S(1)}, s32[32]{0:T(128)}, u32[]{:S(2)}) copy-start(s32[32]{0:T(128)} %param.18) | copy-start | bytes 388
  9.3 37.2 %copy-start.12 = (s32[32]{0:T(128)S(1)}, s32[32]{0:T(128)}, u32[]{:S(2)}) copy-start(s32[32]{0:T(128)} %param.19) | copy-start | bytes 388
  22.8 96.8 %all-gather.7.cloned.1.call-start = ((), (), s32[]{:S(2)}) async-start(), calls=%async_computation.12 | async-start | bytes 2949120 | tf_op jit(solution)/shard_map/all_gather | solution.py:431
  32.1 17.7 %all-to-all-start.2 = ((bf16[8,64,128]{2,1,0:T(8,128)(2,1)}), bf16[8,64,128]{2,1,0:T(8,128)(2,1)S(1)}, u32[]{:S(2)}, u32[]{:S(2)}) async-start(bf16[8,64,128]{2,1,0:T(8,128)(2,1)} %get-tuple-element.28), calls=%async_computation.2 | async-start | bytes 262144 | tf_op jit(solution)/shard_map/all_to_all | solution.py:434
  46.6 31.7 %copy-start.8 = (s32[71]{0:T(128)}, s32[71]{0:T(128)S(1)}, u32[]{:S(2)}) copy-start(s32[71]{0:T(128)S(1)} %concatenate.3.refs_0_) | copy-start | bytes 856
  64.2 1.1 copy-start
  107.9 34.0 %copy-start.9 = (s32[71]{0:T(128)S(1)}, s32[71]{0:T(128)}, u32[]{:S(2)}) copy-start(s32[71]{0:T(128)} %copy-done.8) | copy-start | bytes 856
  107.9 11.8 %all-to-all-start.4 = ((bf16[4,320,128]{2,1,0:T(8,128)(2,1)}), bf16[4,320,128]{2,1,0:T(8,128)(2,1)S(1)}, u32[]{:S(2)}, u32[]{:S(2)}) async-start(bf16[4,320,128]{2,1,0:T(8,128)(2,1)} %get-tuple-element.32), calls=%async_computation.4 | async-start | bytes 655360 | tf_op jit(solution)/shard_map/all_to_all | solution.py:479
  112.0 74.7 %all-gather.9.cloned.1.call-start = ((), (), s32[]{:S(2)}) async-start(), calls=%async_computation.13 | async-start | bytes 2949120 | tf_op jit(solution)/shard_map/all_gather | solution.py:512
  131.8 54.9 %copy-start.1 = (bf16[128,5120]{1,0:T(8,128)(2,1)S(1)}, bf16[128,5120]{1,0:T(8,128)(2,1)}, u32[]{:S(2)}) copy-start(bf16[128,5120]{1,0:T(8,128)(2,1)} %copy-done) | copy-start | bytes 3932164
  168.4 27.7 %copy-start.4 = (bf16[256,1024]{1,0:T(8,128)(2,1)S(1)}, bf16[256,1024]{1,0:T(8,128)(2,1)}, u32[]{:S(2)}) copy-start(bf16[256,1024]{1,0:T(8,128)(2,1)} %patch_ref.1) | copy-start | bytes 1572868
  168.4 11.4 %all-to-all-start.9 = ((bf16[8,64,128]{2,1,0:T(8,128)(2,1)}), bf16[8,64,128]{2,1,0:T(8,128)(2,1)S(1)}, u32[]{:S(2)}, u32[]{:S(2)}) async-start(bf16[8,64,128]{2,1,0:T(8,128)(2,1)} %route.1), calls=%async_computation.9 | async-start | bytes 262144 | tf_op jit(solution)/shard_map/all_to_all | solution.py:542
  180.5 11.6 %all-to-all-start.10 = ((bf16[8,64,128]{2,1,0:T(8,128)(2,1)}), bf16[8,64,128]{2,1,0:T(8,128)(2,1)S(1)}, u32[]{:S(2)}, u32[]{:S(2)}) async-start(bf16[8,64,128]{2,1,0:T(8,128)(2,1)} %broadcast_in_dim.46), calls=%async_computation.10 | async-start | bytes 262144 | tf_op jit(solution)/shard_map/all_to_all | solution.py:545
  186.7 1.7 copy-start.2
  192.0 7.7 %all-to-all-start.6 = ((bf16[4,64,128]{2,1,0:T(8,128)(2,1)}), bf16[4,64,128]{2,1,0:T(8,128)(2,1)S(1)}, u32[]{:S(2)}, u32[]{:S(2)}) async-start(bf16[4,64,128]{2,1,0:T(8,128)(2,1)} %proj_grad.1), calls=%async_computation.6 | async-start | bytes 131072 | tf_op jit(solution)/shard_map/all_to_all | solution.py:557
Sparse Core Ops, SparseCore 0:
  22.9 55.3 all-gather.4
  80.1 39.5 all-gather.6
  132.0 38.2 all-gather.8

commit v5 on v4

--- a/solution.py
+++ b/solution.py
@@ -17,6 +17,7 @@
 EPSILON = 1e-05
 NEGATIVE = -1e30
 CHUNK = 256
+KEY_CHUNK = 512
 STAT_ROWS = 16
 
 F32 = jnp.float32
@@ -242,10 +243,10 @@
     lax.fori_loop(0, count, begin, 0)
     dk[...] = jnp.zeros_like(dk)
     dv[...] = jnp.zeros_like(dv)
-    tail = pl.ds(pl.multiple_of(count * tok, 32), CHUNK)
-    qb[tail] = jnp.zeros((CHUNK, HD), BF16)
-    dob[tail] = jnp.zeros((CHUNK, HD), BF16)
-    lane = lax.broadcasted_iota(jnp.int32, (group, CHUNK), 1)
+    tail = pl.ds(pl.multiple_of(count * tok, 32), KEY_CHUNK)
+    qb[tail] = jnp.zeros((KEY_CHUNK, HD), BF16)
+    dob[tail] = jnp.zeros((KEY_CHUNK, HD), BF16)
+    lane = lax.broadcasted_iota(jnp.int32, (group, KEY_CHUNK), 1)
     key_pos = lax.broadcasted_iota(jnp.int32, (group, 1), 0)
     end = end_ref[...] - z * group
     own_copy.wait()
@@ -253,23 +254,23 @@
 
     def statistics(c, kind):
         parts = []
-        for half in range(2):
-            tile = jnp.minimum(z * (group // HD) + 2 * c + half, last_tile)
+        for half in range(KEY_CHUNK // HD):
+            tile = jnp.minimum(z * (group // HD) + (KEY_CHUNK // HD) * c + half, last_tile)
             at = lax.div(tile, group // HD)
             row = kind * (group // HD) + lax.rem(tile, group // HD)
             parts.append(stat_ref[at, pl.ds(row, 1)])
         return jnp.concatenate(parts, axis=1)
 
     def step(masked, c, carry):
-        where = pl.ds(pl.multiple_of(c * CHUNK, CHUNK), CHUNK)
-        arrived = lax.div(c * CHUNK + tok - 1, tok)
-        needed = jnp.minimum(lax.div((c + 1) * CHUNK + tok - 1, tok), count)
+        where = pl.ds(pl.multiple_of(c * KEY_CHUNK, KEY_CHUNK), KEY_CHUNK)
+        arrived = lax.div(c * KEY_CHUNK + tok - 1, tok)
+        needed = jnp.minimum(lax.div((c + 1) * KEY_CHUNK + tok - 1, tok), count)
         lax.fori_loop(arrived, needed, finish, 0)
         q, do = qb[where], dob[where]
         s = dot_nt(own_ref[0], q)
         p = jnp.exp2((s - statistics(c, 0)) * power) * statistics(c, 1)
         if masked:
-            pos = lane + c * CHUNK
+            pos = lane + c * KEY_CHUNK
             p = jnp.where((pos >= key_pos) & (pos < end), p, 0.0)
         dv[...] += dot_nn(p.astype(BF16), do)
         d_prob = dot_nt(own_ref[1], do)
@@ -278,7 +279,7 @@
         return carry
 
     chunks = meta_ref[2 * frames + 4]
-    after = jnp.minimum((group + CHUNK - 1) // CHUNK, chunks)
+    after = jnp.minimum((group + KEY_CHUNK - 1) // KEY_CHUNK, chunks)
     shared = jnp.maximum(meta_ref[2 * frames + 6], after)
     lax.fori_loop(0, after, functools.partial(step, True), 0)
     lax.fori_loop(after, shared, functools.partial(step, False), 0)
@@ -361,6 +362,20 @@
         out_ref[i] = jnp.where(row < live, rows, 0.0).astype(BF16)
 
 
+def pick_kernel(frames, group, meta_ref, rows_ref, out_ref):
+    rows = rows_ref[lax.div(meta_ref[meta_ref[2 * frames + 1]], group)]
+    for i in range(out_ref.shape[0]):
+        out_ref[i] = rows
+
+
+def proj_out_kernel(heads, r_ref, out_ref):
+    rows = out_ref.shape[0]
+    for h in range(heads):
+        for c in range(2):
+            part = r_ref[h, c * rows : (c + 1) * rows].astype(F32)
+            out_ref[:, c, h * HD : (h + 1) * HD] = part
+
+
 def norm_grad_kernel(patch_ref, gain_ref, dn_ref, out_ref):
     scaled, inverse = normalize_rows(patch_ref[0:PATCH_MOST])
     d_normed = jnp.concatenate([dn_ref[i] for i in range(dn_ref.shape[0])], axis=1).astype(F32)
@@ -405,9 +420,9 @@
         block,
         start[0, 0] // CHUNK,
         ((z + 1) * group + CHUNK - 1) // CHUNK,
-        (end[group - 1, 0] - z * group + CHUNK - 1) // CHUNK,
+        (end[group - 1, 0] - z * group + KEY_CHUNK - 1) // KEY_CHUNK,
         (end[group - 1, 0] - z * group + tok - 1) // tok,
-        (end[0, 0] - z * group) // CHUNK,
+        (end[0, 0] - z * group) // KEY_CHUNK,
     ]).astype(jnp.int32)
     meta = jnp.concatenate([image_offsets, patch_counts, scalars])
     gain = ln_gain.reshape(1, width)
@@ -493,8 +508,8 @@
         in_specs=[smem, whole, hbm, hbm, hbm],
         out_specs=(hbm, hbm),
         scratch_shapes=[
-            pltpu.VMEM((most_blocks * tok + CHUNK, HD), BF16),
-            pltpu.VMEM((most_blocks * tok + CHUNK, HD), BF16),
+            pltpu.VMEM((most_blocks * tok + KEY_CHUNK, HD), BF16),
+            pltpu.VMEM((most_blocks * tok + KEY_CHUNK, HD), BF16),
             pltpu.VMEM((groups, STAT_ROWS, HD), F32),
             pltpu.VMEM((2, group, HD), BF16),
             pltpu.VMEM((group, HD), F32),
@@ -540,11 +555,15 @@
         name="route",
     )(meta, of_group)
     from_groups = lax.all_to_all(routed, "z", 0, 0, tiled=True)
-    source = lax.dynamic_index_in_dim(image_offsets, block, keepdims=False) // group
-    d_slice = lax.dynamic_index_in_dim(from_groups, source, keepdims=False)
-    d_normed = lax.all_to_all(
-        jnp.broadcast_to(d_slice[None], (sections,) + d_slice.shape), "phase", 0, 0, tiled=True
-    )
+    d_slice = pl.pallas_call(
+        lambda *refs: pick_kernel(frames, group, *refs),
+        out_shape=shape((sections, PATCH_MOST, HD)),
+        in_specs=[smem, whole],
+        out_specs=whole,
+        compiler_params=vmem(),
+        name="pick",
+    )(meta, from_groups)
+    d_normed = lax.all_to_all(d_slice, "phase", 0, 0, tiled=True)
     proj_rows = width // blocks
     proj_head = pl.pallas_call(
         proj_kernel,
@@ -555,12 +574,14 @@
         name="proj_grad",
     )(norm_pos, d_kv_all)
     proj_back = lax.all_to_all(proj_head, "y", 0, 0, tiled=True)
-    d_proj = (
-        proj_back[:heads].astype(F32)
-        .reshape(heads, 2, proj_rows, HD)
-        .transpose(2, 1, 0, 3)
-        .reshape(proj_rows, 2, cols)
-    )
+    d_proj = pl.pallas_call(
+        lambda *refs: proj_out_kernel(heads, *refs),
+        out_shape=shape((proj_rows, 2, cols), F32),
+        in_specs=[whole],
+        out_specs=whole,
+        compiler_params=vmem(),
+        name="proj_out",
+    )(proj_back)
     d_patches = pl.pallas_call(
         norm_grad_kernel,
         out_shape=shape(patches.shape),

time: 208 us -> 206 us (level)
  blocking collectives: 88.1 us -> 104 us
  Pallas kernels: 29.9 us -> 24.6 us
  waiting for transfers between devices: 33.4 us -> 28.5 us
  starting transfers between devices: 25.6 us -> 22.5 us
  local copies, waits for them, and re-layouts: 9.87 us -> 7.78 us
    all_to_all x0 -> x1, blocking collectives: none -> 16.1 us  [shards(): from_groups = lax.all_to_all(routed, 'z', 0, 0, tiled=True)]
    pallas_call x1, Pallas kernels: 12.1 us -> 5.58 us  [shards(): pl.pallas_call(lambda *refs: key_kernel(frames, tok, *refs), out_shape=(s...]
    all_to_all x2 -> x1, waiting for transfers between devices: 7.73 us -> 2.41 us  [shards(): d_normed = lax.all_to_all(d_slice, 'phase', 0, 0, tiled=True)]
    all_to_all x2 -> x1, starting transfers between devices: 9.76 us -> 6.59 us  [shards(): d_normed = lax.all_to_all(d_slice, 'phase', 0, 0, tiled=True)]
    unnamed x34 -> x33, local copies, waits for them, and re-layouts: 5.38 us -> 4.66 us
  transfers between devices with their start and end apart: 8 -> 7, of which waited for: 6 -> 5; matrix products, arithmetic and copies ran while one was open for 2% -> 2% of each run, Pallas kernels for 8% -> 8%
where the time goes in v5:
time: 206 us; the launch traced here: 205 us
  blocking collectives  104 us (50%)
  waiting for transfers between devices  28.5 us (14%)
  Pallas kernels  24.6 us (12%)
  starting transfers between devices  22.5 us (11%)
  between operations  17.9 us (9%)
  local copies, waits for them, and re-layouts  7.78 us (4%)
    all_to_all x1, blocking collectives, shards(): all_stats = lax.all_to_all(stats, 'z', 0, 0, tiled=True)  21.2 us
    all_to_all x1, blocking collectives, shards(): summed = lax.all_to_all(terms, 'phase', 0, 0, tiled=True)  16.7 us
    all_to_all x1, blocking collectives, shards(): from_groups = lax.all_to_all(routed, 'z', 0, 0, tiled=True)  16.1 us
    all_gather x1, waiting for transfers between devices, shards(): kv_all = lax.all_gather(kv_mine, 'z', axis=0, tiled=True)  13 us
    all_to_all x1, blocking collectives, shards(): kv_mine = lax.all_to_all(packed, 'y', 0, 0, tiled=True)  12.3 us
    all_gather x1, blocking collectives, shards(): all_frames = lax.all_gather(some_frames, 'y', axis=0, tiled=False)  11.3 us
    all_to_all x1, blocking collectives, shards(): keys_back = lax.all_to_all(key_grads, 'y', 0, 0, tiled=True)  10 us
    all_to_all x1, blocking collectives, shards(): q_mine = lax.all_to_all(questions, 'y', 0, 0, tiled=True)  8.94 us
  transfers between devices with their start and end apart: 7, of which 5 were waited for; matrix products, arithmetic and copies ran while one was open for 2% of the time, Pallas kernels for 8%

profile of v5, /device:TPU:1, one launch (start us, length us, event | category | flops | bytes accessed | tf_op | source)
XLA Modules:
  0.0 205.5 jit_solution(5199787563305884046)
XLA Ops:
  7.3 1.8 copy.25
  9.3 1.2 pack.1
  10.5 12.3 %all_to_all.55 = bf16[4,448,128]{2,1,0:T(8,128)(2,1)} all-to-all(bf16[4,448,128]{2,1,0:T(8,128)(2,1)S(1)} %get-tuple-element.24), channel_id=1, replica_groups=mesh['phase'=8,'z'=8,'y'=4] {'y'}, dimensions={0} | all-to-all | bytes 917504 | tf_op jit(solution)/shard_map/all_to_all | solution.py:442
  22.9 8.9 %all_to_all.56.refs_3_ = bf16[4,320,128]{2,1,0:T(8,128)(2,1)} all-to-all(bf16[4,320,128]{2,1,0:T(8,128)(2,1)S(1)} %get-tuple-element.27), channel_id=1, replica_groups=mesh['phase'=8,'z'=8,'y'=4] {'y'}, dimensions={0} | all-to-all | bytes 655360 | tf_op jit(solution)/shard_map/all_to_all | solution.py:445
  32.1 8.4 %all-to-all-start.2 = ((bf16[8,64,128]{2,1,0:T(8,128)(2,1)}), bf16[8,64,128]{2,1,0:T(8,128)(2,1)S(1)}, u32[]{:S(2)}, u32[]{:S(2)}) async-start(bf16[8,64,128]{2,1,0:T(8,128)(2,1)} %get-tuple-element.28), calls=%async_computation.2 | async-start | bytes 262144 | tf_op jit(solution)/shard_map/all_to_all | solution.py:449
  45.6 0.9 broadcast_in_dim.37.refs_1_
  46.6 3.2 %all-to-all-done.2 = bf16[8,64,128]{2,1,0:T(8,128)(2,1)S(1)} async-done(((bf16[8,64,128]{2,1,0:T(8,128)(2,1)}), bf16[8,64,128]{2,1,0:T(8,128)(2,1)S(1)}, u32[]{:S(2)}, u32[]{:S(2)}) %all-to-all-start.2) | async-done | bytes 131104 | tf_op jit(solution)/shard_map/all_to_all | solution.py:449
  49.8 11.3 %all-gather = bf16[32,64,128]{2,1,0:T(8,128)(2,1)S(1)} all-gather(bf16[8,64,128]{2,1,0:T(8,128)(2,1)S(1)} %all-to-all-done.2), channel_id=2, replica_groups=mesh['phase'=8,'z'=8,'y'=4] {'y'}, dimensions={0}, use_global_device_ids=true | all-gather | bytes 655360 | tf_op jit(solution)/shard_map/all_gather | solution.py:450
  61.1 3.1 %place.1.norm_ref = bf16[128,5120]{1,0:T(8,128)(2,1)S(1)} custom-call(s32[71]{0:T(128)S(1)} %concatenate.3.refs_0_, bf16[4,8,64,128]{3,2,1,0:T(8,128)(2,1)S(1)} %bitcast.19), custom_call_target="tpu_custom_call" | custom-call | tf_op jit(solution)/shard_map/place/pallas_call | solution.py:451
  64.2 1.1 copy-done
  65.3 13.0 %all-gather.5.cloned.1.call-done.refs_2_ = bf16[32,448,128]{2,1,0:T(8,128)(2,1)} async-done(((bf16[4,448,128]{2,1,0:T(8,128)(2,1)}), bf16[32,448,128]{2,1,0:T(8,128)(2,1)}) %all-gather.5.cloned.1.call-update) | async-done | bytes 3670032 | tf_op jit(solution)/shard_map/all_gather | solution.py:443
  78.3 7.8 %queries.1 = (bf16[4,320,128]{2,1,0:T(8,128)(2,1)}, bf16[2,640,128]{2,1,0:T(8,128)(2,1)}, f32[8,16,128]{2,1,0:T(8,128)}) custom-call(s32[71]{0:T(128)} %copy-done.8, s32[640,1]{1,0:T(8,128)} %broadcast_in_dim.37.refs_1_, bf16[32,448,128]{2,1,0:T(8,128)(2,1)} %all-gather.5.cloned.1.call-done.refs_2_, bf16[4,320,128]{2,1,0:T(8,128)(2,1)} %all_to_all.56.refs_3_), custom_call_target="tpu_custom_call" | custom-call | tf_op jit(solution)/shard_map/queries/pallas_call | solution.py:464
  86.1 21.2 %all_to_all.57.refs_3_ = f32[8,16,128]{2,1,0:T(8,128)} all-to-all(f32[8,16,128]{2,1,0:T(8,128)} %get-tuple-element.31), channel_id=1, replica_groups=mesh['phase'=8,'z'=8,'y'=4] {'z'}, dimensions={0} | all-to-all | bytes 131072 | tf_op jit(solution)/shard_map/all_to_all | solution.py:492
  107.3 4.1 %all-to-all-start.4 = ((bf16[4,320,128]{2,1,0:T(8,128)(2,1)}), bf16[4,320,128]{2,1,0:T(8,128)(2,1)S(1)}, u32[]{:S(2)}, u32[]{:S(2)}) async-start(bf16[4,320,128]{2,1,0:T(8,128)(2,1)} %get-tuple-element.32), calls=%async_computation.4 | async-start | bytes 655360 | tf_op jit(solution)/shard_map/all_to_all | solution.py:494
  111.4 0.9 broadcast_in_dim.38.refs_1_
  112.3 7.2 %all-gather.7.cloned.1.call-done.refs_2_ = bf16[32,320,128]{2,1,0:T(8,128)(2,1)} async-done(((bf16[4,320,128]{2,1,0:T(8,128)(2,1)}), bf16[32,320,128]{2,1,0:T(8,128)(2,1)}) %all-gather.7.cloned.1.call-update) | async-done | bytes 2621456 | tf_op jit(solution)/shard_map/all_gather | solution.py:446
  119.5 5.6 %keys.1 = (bf16[640,256]{1,0:T(8,128)(2,1)}, bf16[4,320,128]{2,1,0:T(8,128)(2,1)}) custom-call(s32[71]{0:T(128)} %copy-done.8, s32[640,1]{1,0:T(8,128)} %broadcast_in_dim.38.refs_1_, bf16[32,320,128]{2,1,0:T(8,128)(2,1)} %all-gather.7.cloned.1.call-done.refs_2_, f32[8,16,128]{2,1,0:T(8,128)} %all_to_all.57.refs_3_, ...), custom_call_target="tpu_custom_call" | custom-call | tf_op jit(solution)/shard_map/keys/pallas_call | solution.py:505
  125.1 10.0 %all_to_all.58.refs_3_ = bf16[4,320,128]{2,1,0:T(8,128)(2,1)S(1)} all-to-all(bf16[4,320,128]{2,1,0:T(8,128)(2,1)} %get-tuple-element.38), channel_id=1, replica_groups=mesh['phase'=8,'z'=8,'y'=4] {'y'}, dimensions={0} | all-to-all | bytes 655360 | tf_op jit(solution)/shard_map/all_to_all | solution.py:528
  135.2 1.4 unpack.1
  136.6 16.7 %all_to_all.59.dn_ref = bf16[8,160,128]{2,1,0:T(8,128)(2,1)S(1)} all-to-all(bf16[8,160,128]{2,1,0:T(8,128)(2,1)S(1)} %get-tuple-element.42), channel_id=1, replica_groups=mesh['phase'=8,'z'=8,'y'=4] {'phase'}, dimensions={0} | all-to-all | bytes 655360 | tf_op jit(solution)/shard_map/all_to_all | solution.py:538
  153.3 7.4 %all_to_all.60.refs_1_ = bf16[4,160,128]{2,1,0:T(8,128)(2,1)S(1)} all-to-all(bf16[4,160,128]{2,1,0:T(8,128)(2,1)S(1)} %sum.1), channel_id=1, replica_groups=mesh['phase'=8,'z'=8,'y'=4] {'y'}, dimensions={0} | all-to-all | bytes 327680 | tf_op jit(solution)/shard_map/all_to_all | solution.py:547
  161.3 16.1 %all_to_all.61.refs_1_ = bf16[8,64,128]{2,1,0:T(8,128)(2,1)S(1)} all-to-all(bf16[8,64,128]{2,1,0:T(8,128)(2,1)S(1)} %route.1), channel_id=1, replica_groups=mesh['phase'=8,'z'=8,'y'=4] {'z'}, dimensions={0} | all-to-all | bytes 262144 | tf_op jit(solution)/shard_map/all_to_all | solution.py:557
  177.4 1.2 pick.1
  178.7 6.6 %all-to-all-start.10 = ((bf16[8,64,128]{2,1,0:T(8,128)(2,1)}), bf16[8,64,128]{2,1,0:T(8,128)(2,1)S(1)}, u32[]{:S(2)}, u32[]{:S(2)}) async-start(bf16[8,64,128]{2,1,0:T(8,128)(2,1)} %pick.1), calls=%async_computation.10 | async-start | bytes 262144 | tf_op jit(solution)/shard_map/all_to_all | solution.py:566
  185.2 1.7 copy-done.2
  187.0 1.1 proj_grad.1
  188.1 2.4 %all-to-all-done.10.dn_ref = bf16[8,64,128]{2,1,0:T(8,128)(2,1)S(1)} async-done(((bf16[8,64,128]{2,1,0:T(8,128)(2,1)}), bf16[8,64,128]{2,1,0:T(8,128)(2,1)S(1)}, u32[]{:S(2)}, u32[]{:S(2)}) %all-to-all-start.10) | async-done | bytes 131104 | tf_op jit(solution)/shard_map/all_to_all | solution.py:566
  190.5 3.3 %all-to-all-start.6 = ((bf16[4,64,128]{2,1,0:T(8,128)(2,1)}), bf16[4,64,128]{2,1,0:T(8,128)(2,1)S(1)}, u32[]{:S(2)}, u32[]{:S(2)}) async-start(bf16[4,64,128]{2,1,0:T(8,128)(2,1)} %proj_grad.1), calls=%async_computation.6 | async-start | bytes 131072 | tf_op jit(solution)/shard_map/all_to_all | solution.py:576
  193.8 0.7 unpack_queries.1
  194.6 1.1 norm_grad.1
  195.7 2.6 %all-to-all-done.6.refs_0_ = bf16[4,64,128]{2,1,0:T(8,128)(2,1)S(1)} async-done(((bf16[4,64,128]{2,1,0:T(8,128)(2,1)}), bf16[4,64,128]{2,1,0:T(8,128)(2,1)S(1)}, u32[]{:S(2)}, u32[]{:S(2)}) %all-to-all-start.6) | async-done | bytes 65568 | tf_op jit(solution)/shard_map/all_to_all | solution.py:576
  198.3 0.7 proj_out.1
  (47 shorter events, 2.5 us)
Async XLA Ops:
  7.2 1.9 copy-start.15
  7.2 2.0 copy-start.10
  7.2 2.0 copy-start.3
  7.2 2.0 copy-start.6
  7.2 2.0 copy-start.5
  7.2 2.0 copy-start.13
  7.2 2.0 copy-start.7
  7.2 71.1 %all-gather.5.cloned.1.call-start = ((), (), s32[]{:S(2)}) async-start(), calls=%async_computation.11 | async-start | bytes 4128768 | tf_op jit(solution)/shard_map/all_gather | solution.py:443
  9.1 22.8 %copy-start.14 = (s32[5120]{0:T(1024)S(1)}, s32[5120]{0:T(1024)}, u32[]{:S(2)}) copy-start(s32[5120]{0:T(1024)} %param.21) | copy-start | bytes 61444
  9.3 37.2 %copy-start.11 = (s32[32]{0:T(128)S(1)}, s32[32]{0:T(128)}, u32[]{:S(2)}) copy-start(s32[32]{0:T(128)} %param.19) | copy-start | bytes 388
  9.3 37.2 %copy-start.12 = (s32[32]{0:T(128)S(1)}, s32[32]{0:T(128)}, u32[]{:S(2)}) copy-start(s32[32]{0:T(128)} %param.18) | copy-start | bytes 388
  22.8 96.7 %all-gather.7.cloned.1.call-start = ((), (), s32[]{:S(2)}) async-start(), calls=%async_computation.12 | async-start | bytes 2949120 | tf_op jit(solution)/shard_map/all_gather | solution.py:446
  32.1 17.7 %all-to-all-start.2 = ((bf16[8,64,128]{2,1,0:T(8,128)(2,1)}), bf16[8,64,128]{2,1,0:T(8,128)(2,1)S(1)}, u32[]{:S(2)}, u32[]{:S(2)}) async-start(bf16[8,64,128]{2,1,0:T(8,128)(2,1)} %get-tuple-element.28), calls=%async_computation.2 | async-start | bytes 262144 | tf_op jit(solution)/shard_map/all_to_all | solution.py:449
  46.6 31.7 %copy-start.8 = (s32[71]{0:T(128)}, s32[71]{0:T(128)S(1)}, u32[]{:S(2)}) copy-start(s32[71]{0:T(128)S(1)} %concatenate.3.refs_0_) | copy-start | bytes 856
  64.2 1.1 copy-start
  107.3 27.9 %copy-start.9 = (s32[71]{0:T(128)S(1)}, s32[71]{0:T(128)}, u32[]{:S(2)}) copy-start(s32[71]{0:T(128)} %copy-done.8) | copy-start | bytes 856
  107.3 12.2 %all-to-all-start.4 = ((bf16[4,320,128]{2,1,0:T(8,128)(2,1)}), bf16[4,320,128]{2,1,0:T(8,128)(2,1)S(1)}, u32[]{:S(2)}, u32[]{:S(2)}) async-start(bf16[4,320,128]{2,1,0:T(8,128)(2,1)} %get-tuple-element.32), calls=%async_computation.4 | async-start | bytes 655360 | tf_op jit(solution)/shard_map/all_to_all | solution.py:494
  111.4 73.8 %all-gather.9.cloned.1.call-start = ((), (), s32[]{:S(2)}) async-start(), calls=%async_computation.13 | async-start | bytes 2949120 | tf_op jit(solution)/shard_map/all_gather | solution.py:527
  125.1 60.1 %copy-start.1 = (bf16[128,5120]{1,0:T(8,128)(2,1)S(1)}, bf16[128,5120]{1,0:T(8,128)(2,1)}, u32[]{:S(2)}) copy-start(bf16[128,5120]{1,0:T(8,128)(2,1)} %copy-done) | copy-start | bytes 3932164
  161.3 33.3 %copy-start.4 = (bf16[256,1024]{1,0:T(8,128)(2,1)S(1)}, bf16[256,1024]{1,0:T(8,128)(2,1)}, u32[]{:S(2)}) copy-start(bf16[256,1024]{1,0:T(8,128)(2,1)} %patch_ref.1) | copy-start | bytes 1572868
  178.7 11.9 %all-to-all-start.10 = ((bf16[8,64,128]{2,1,0:T(8,128)(2,1)}), bf16[8,64,128]{2,1,0:T(8,128)(2,1)S(1)}, u32[]{:S(2)}, u32[]{:S(2)}) async-start(bf16[8,64,128]{2,1,0:T(8,128)(2,1)} %pick.1), calls=%async_computation.10 | async-start | bytes 262144 | tf_op jit(solution)/shard_map/all_to_all | solution.py:566
  185.2 1.7 copy-start.2
  190.5 7.7 %all-to-all-start.6 = ((bf16[4,64,128]{2,1,0:T(8,128)(2,1)}), bf16[4,64,128]{2,1,0:T(8,128)(2,1)S(1)}, u32[]{:S(2)}, u32[]{:S(2)}) async-start(bf16[4,64,128]{2,1,0:T(8,128)(2,1)} %proj_grad.1), calls=%async_computation.6 | async-start | bytes 131072 | tf_op jit(solution)/shard_map/all_to_all | solution.py:576
Sparse Core Ops, SparseCore 0:
  22.9 55.3 all-gather.4
  80.1 39.3 all-gather.6
  125.2 45.2 all-gather.8

commit v6 on v5

--- a/solution.py
+++ b/solution.py
@@ -331,8 +331,9 @@
             dtext_ref[c, :, span] = jnp.where(is_image, zero, grad)
             parts[c * heads + h] = jnp.where(is_image, grad, zero)
     grads = jnp.concatenate(parts, axis=1)
+    terms = dot_nt(grads, proj_ref[...]).astype(BF16)
     for i in range(dn_ref.shape[0]):
-        dn_ref[i] = dot_nt(grads, proj_ref[i * HD : (i + 1) * HD]).astype(BF16)
+        dn_ref[i] = terms[:, i * HD : (i + 1) * HD]
 
 
 def sum_kernel(dn_ref, out_ref):

time: 206 us -> 205 us (level)
  blocking collectives: 104 us -> 97.1 us
  Pallas kernels: 24.6 us -> 29.6 us
    all_to_all x1, blocking collectives: 16.1 us -> 10.4 us  [shards(): from_groups = lax.all_to_all(routed, 'z', 0, 0, tiled=True)]
    pallas_call x1, Pallas kernels: 5.58 us -> 10.2 us  [shards(): pl.pallas_call(lambda *refs: key_kernel(frames, tok, *refs), out_shape=(s...]
  transfers between devices with their start and end apart: 7 -> 7, of which waited for: 5 -> 5; matrix products, arithmetic and copies ran while one was open for 2% -> 2% of each run, Pallas kernels for 8% -> 9%
where the time goes in v6:
time: 205 us; the launch traced here: 204 us
  blocking collectives  97.1 us (47%)
  Pallas kernels  29.6 us (14%)
  waiting for transfers between devices  29.6 us (14%)
  starting transfers between devices  22.1 us (11%)
  between operations  17.9 us (9%)
  local copies, waits for them, and re-layouts  7.78 us (4%)
    all_to_all x1, blocking collectives, shards(): all_stats = lax.all_to_all(stats, 'z', 0, 0, tiled=True)  20.6 us
    all_to_all x1, blocking collectives, shards(): summed = lax.all_to_all(terms, 'phase', 0, 0, tiled=True)  16.1 us
    all_gather x1, waiting for transfers between devices, shards(): kv_all = lax.all_gather(kv_mine, 'z', axis=0, tiled=True)  13 us
    all_to_all x1, blocking collectives, shards(): kv_mine = lax.all_to_all(packed, 'y', 0, 0, tiled=True)  12.3 us
    all_gather x1, blocking collectives, shards(): all_frames = lax.all_gather(some_frames, 'y', axis=0, tiled=False)  11.3 us
    all_to_all x1, blocking collectives, shards(): from_groups = lax.all_to_all(routed, 'z', 0, 0, tiled=True)  10.4 us
    pallas_call x1, Pallas kernels, shards(): pl.pallas_call(lambda *refs: key_kernel(frames, tok, *refs), out_shape=(s...  10.2 us
    all_to_all x1, blocking collectives, shards(): keys_back = lax.all_to_all(key_grads, 'y', 0, 0, tiled=True)  10 us
  transfers between devices with their start and end apart: 7, of which 5 were waited for; matrix products, arithmetic and copies ran while one was open for 2% of the time, Pallas kernels for 9%

profile of v6, /device:TPU:1, one launch (start us, length us, event | category | flops | bytes accessed | tf_op | source)
XLA Modules:
  0.0 204.4 jit_solution(870370871053364969)
XLA Ops:
  7.3 1.8 copy.25
  9.3 1.2 pack.1
  10.5 12.3 %all_to_all.55 = bf16[4,448,128]{2,1,0:T(8,128)(2,1)} all-to-all(bf16[4,448,128]{2,1,0:T(8,128)(2,1)S(1)} %get-tuple-element.24), channel_id=1, replica_groups=mesh['phase'=8,'z'=8,'y'=4] {'y'}, dimensions={0} | all-to-all | bytes 917504 | tf_op jit(solution)/shard_map/all_to_all | solution.py:443
  22.9 8.9 %all_to_all.56.refs_3_ = bf16[4,320,128]{2,1,0:T(8,128)(2,1)} all-to-all(bf16[4,320,128]{2,1,0:T(8,128)(2,1)S(1)} %get-tuple-element.27), channel_id=1, replica_groups=mesh['phase'=8,'z'=8,'y'=4] {'y'}, dimensions={0} | all-to-all | bytes 655360 | tf_op jit(solution)/shard_map/all_to_all | solution.py:446
  32.1 8.4 %all-to-all-start.2 = ((bf16[8,64,128]{2,1,0:T(8,128)(2,1)}), bf16[8,64,128]{2,1,0:T(8,128)(2,1)S(1)}, u32[]{:S(2)}, u32[]{:S(2)}) async-start(bf16[8,64,128]{2,1,0:T(8,128)(2,1)} %get-tuple-element.28), calls=%async_computation.2 | async-start | bytes 262144 | tf_op jit(solution)/shard_map/all_to_all | solution.py:450
  45.6 0.9 broadcast_in_dim.37.refs_1_
  46.6 3.2 %all-to-all-done.2 = bf16[8,64,128]{2,1,0:T(8,128)(2,1)S(1)} async-done(((bf16[8,64,128]{2,1,0:T(8,128)(2,1)}), bf16[8,64,128]{2,1,0:T(8,128)(2,1)S(1)}, u32[]{:S(2)}, u32[]{:S(2)}) %all-to-all-start.2) | async-done | bytes 131104 | tf_op jit(solution)/shard_map/all_to_all | solution.py:450
  49.8 11.3 %all-gather = bf16[32,64,128]{2,1,0:T(8,128)(2,1)S(1)} all-gather(bf16[8,64,128]{2,1,0:T(8,128)(2,1)S(1)} %all-to-all-done.2), channel_id=2, replica_groups=mesh['phase'=8,'z'=8,'y'=4] {'y'}, dimensions={0}, use_global_device_ids=true | all-gather | bytes 655360 | tf_op jit(solution)/shard_map/all_gather | solution.py:451
  61.1 3.1 %place.1.norm_ref = bf16[128,5120]{1,0:T(8,128)(2,1)S(1)} custom-call(s32[71]{0:T(128)S(1)} %concatenate.3.refs_0_, bf16[4,8,64,128]{3,2,1,0:T(8,128)(2,1)S(1)} %bitcast.19), custom_call_target="tpu_custom_call" | custom-call | tf_op jit(solution)/shard_map/place/pallas_call | solution.py:452
  64.2 1.1 copy-done
  65.3 13.0 %all-gather.5.cloned.1.call-done.refs_2_ = bf16[32,448,128]{2,1,0:T(8,128)(2,1)} async-done(((bf16[4,448,128]{2,1,0:T(8,128)(2,1)}), bf16[32,448,128]{2,1,0:T(8,128)(2,1)}) %all-gather.5.cloned.1.call-update) | async-done | bytes 3670032 | tf_op jit(solution)/shard_map/all_gather | solution.py:444
  78.3 7.8 %queries.1 = (bf16[4,320,128]{2,1,0:T(8,128)(2,1)}, bf16[2,640,128]{2,1,0:T(8,128)(2,1)}, f32[8,16,128]{2,1,0:T(8,128)}) custom-call(s32[71]{0:T(128)} %copy-done.8, s32[640,1]{1,0:T(8,128)} %broadcast_in_dim.37.refs_1_, bf16[32,448,128]{2,1,0:T(8,128)(2,1)} %all-gather.5.cloned.1.call-done.refs_2_, bf16[4,320,128]{2,1,0:T(8,128)(2,1)} %all_to_all.56.refs_3_), custom_call_target="tpu_custom_call" | custom-call | tf_op jit(solution)/shard_map/queries/pallas_call | solution.py:465
  86.1 20.6 %all_to_all.57.refs_3_ = f32[8,16,128]{2,1,0:T(8,128)} all-to-all(f32[8,16,128]{2,1,0:T(8,128)} %get-tuple-element.31), channel_id=1, replica_groups=mesh['phase'=8,'z'=8,'y'=4] {'z'}, dimensions={0} | all-to-all | bytes 131072 | tf_op jit(solution)/shard_map/all_to_all | solution.py:493
  106.7 4.1 %all-to-all-start.4 = ((bf16[4,320,128]{2,1,0:T(8,128)(2,1)}), bf16[4,320,128]{2,1,0:T(8,128)(2,1)S(1)}, u32[]{:S(2)}, u32[]{:S(2)}) async-start(bf16[4,320,128]{2,1,0:T(8,128)(2,1)} %get-tuple-element.32), calls=%async_computation.4 | async-start | bytes 655360 | tf_op jit(solution)/shard_map/all_to_all | solution.py:495
  110.8 0.9 broadcast_in_dim.38.refs_1_
  111.7 8.3 %all-gather.7.cloned.1.call-done.refs_2_ = bf16[32,320,128]{2,1,0:T(8,128)(2,1)} async-done(((bf16[4,320,128]{2,1,0:T(8,128)(2,1)}), bf16[32,320,128]{2,1,0:T(8,128)(2,1)}) %all-gather.7.cloned.1.call-update) | async-done | bytes 2621456 | tf_op jit(solution)/shard_map/all_gather | solution.py:447
  120.0 10.2 %keys.1 = (bf16[640,256]{1,0:T(8,128)(2,1)}, bf16[4,320,128]{2,1,0:T(8,128)(2,1)}) custom-call(s32[71]{0:T(128)} %copy-done.8, s32[640,1]{1,0:T(8,128)} %broadcast_in_dim.38.refs_1_, bf16[32,320,128]{2,1,0:T(8,128)(2,1)} %all-gather.7.cloned.1.call-done.refs_2_, f32[8,16,128]{2,1,0:T(8,128)} %all_to_all.57.refs_3_, ...), custom_call_target="tpu_custom_call" | custom-call | tf_op jit(solution)/shard_map/keys/pallas_call | solution.py:506
  130.3 10.0 %all_to_all.58.refs_3_ = bf16[4,320,128]{2,1,0:T(8,128)(2,1)S(1)} all-to-all(bf16[4,320,128]{2,1,0:T(8,128)(2,1)} %get-tuple-element.38), channel_id=1, replica_groups=mesh['phase'=8,'z'=8,'y'=4] {'y'}, dimensions={0} | all-to-all | bytes 655360 | tf_op jit(solution)/shard_map/all_to_all | solution.py:529
  140.3 1.7 unpack.1
  142.0 16.1 %all_to_all.59.dn_ref = bf16[8,160,128]{2,1,0:T(8,128)(2,1)S(1)} all-to-all(bf16[8,160,128]{2,1,0:T(8,128)(2,1)S(1)} %get-tuple-element.42), channel_id=1, replica_groups=mesh['phase'=8,'z'=8,'y'=4] {'phase'}, dimensions={0} | all-to-all | bytes 655360 | tf_op jit(solution)/shard_map/all_to_all | solution.py:539
  158.2 7.4 %all_to_all.60.refs_1_ = bf16[4,160,128]{2,1,0:T(8,128)(2,1)S(1)} all-to-all(bf16[4,160,128]{2,1,0:T(8,128)(2,1)S(1)} %sum.1), channel_id=1, replica_groups=mesh['phase'=8,'z'=8,'y'=4] {'y'}, dimensions={0} | all-to-all | bytes 327680 | tf_op jit(solution)/shard_map/all_to_all | solution.py:548
  166.2 10.4 %all_to_all.61.refs_1_ = bf16[8,64,128]{2,1,0:T(8,128)(2,1)S(1)} all-to-all(bf16[8,64,128]{2,1,0:T(8,128)(2,1)S(1)} %route.1), channel_id=1, replica_groups=mesh['phase'=8,'z'=8,'y'=4] {'z'}, dimensions={0} | all-to-all | bytes 262144 | tf_op jit(solution)/shard_map/all_to_all | solution.py:558
  176.7 1.2 pick.1
  177.9 6.3 %all-to-all-start.10 = ((bf16[8,64,128]{2,1,0:T(8,128)(2,1)}), bf16[8,64,128]{2,1,0:T(8,128)(2,1)S(1)}, u32[]{:S(2)}, u32[]{:S(2)}) async-start(bf16[8,64,128]{2,1,0:T(8,128)(2,1)} %pick.1), calls=%async_computation.10 | async-start | bytes 262144 | tf_op jit(solution)/shard_map/all_to_all | solution.py:567
  184.2 1.7 copy-done.2
  185.9 1.1 proj_grad.1
  187.0 2.4 %all-to-all-done.10.dn_ref = bf16[8,64,128]{2,1,0:T(8,128)(2,1)S(1)} async-done(((bf16[8,64,128]{2,1,0:T(8,128)(2,1)}), bf16[8,64,128]{2,1,0:T(8,128)(2,1)S(1)}, u32[]{:S(2)}, u32[]{:S(2)}) %all-to-all-start.10) | async-done | bytes 131104 | tf_op jit(solution)/shard_map/all_to_all | solution.py:567
  189.4 3.3 %all-to-all-start.6 = ((bf16[4,64,128]{2,1,0:T(8,128)(2,1)}), bf16[4,64,128]{2,1,0:T(8,128)(2,1)S(1)}, u32[]{:S(2)}, u32[]{:S(2)}) async-start(bf16[4,64,128]{2,1,0:T(8,128)(2,1)} %proj_grad.1), calls=%async_computation.6 | async-start | bytes 131072 | tf_op jit(solution)/shard_map/all_to_all | solution.py:577
  192.7 0.7 unpack_queries.1
  193.5 1.1 norm_grad.1
  194.6 2.6 %all-to-all-done.6.refs_0_ = bf16[4,64,128]{2,1,0:T(8,128)(2,1)S(1)} async-done(((bf16[4,64,128]{2,1,0:T(8,128)(2,1)}), bf16[4,64,128]{2,1,0:T(8,128)(2,1)S(1)}, u32[]{:S(2)}, u32[]{:S(2)}) %all-to-all-start.6) | async-done | bytes 65568 | tf_op jit(solution)/shard_map/all_to_all | solution.py:577
  197.2 0.7 proj_out.1
  (47 shorter events, 2.5 us)
Async XLA Ops:
  7.2 1.9 copy-start.15
  7.2 2.0 copy-start.10
  7.2 2.0 copy-start.3
  7.2 2.0 copy-start.6
  7.2 2.0 copy-start.5
  7.2 2.0 copy-start.13
  7.2 2.0 copy-start.7
  7.2 71.1 %all-gather.5.cloned.1.call-start = ((), (), s32[]{:S(2)}) async-start(), calls=%async_computation.11 | async-start | bytes 4128768 | tf_op jit(solution)/shard_map/all_gather | solution.py:444
  9.1 22.8 %copy-start.14 = (s32[5120]{0:T(1024)S(1)}, s32[5120]{0:T(1024)}, u32[]{:S(2)}) copy-start(s32[5120]{0:T(1024)} %param.21) | copy-start | bytes 61444
  9.3 37.2 %copy-start.11 = (s32[32]{0:T(128)S(1)}, s32[32]{0:T(128)}, u32[]{:S(2)}) copy-start(s32[32]{0:T(128)} %param.19) | copy-start | bytes 388
  9.3 37.2 %copy-start.12 = (s32[32]{0:T(128)S(1)}, s32[32]{0:T(128)}, u32[]{:S(2)}) copy-start(s32[32]{0:T(128)} %param.18) | copy-start | bytes 388
  22.8 97.2 %all-gather.7.cloned.1.call-start = ((), (), s32[]{:S(2)}) async-start(), calls=%async_computation.12 | async-start | bytes 2949120 | tf_op jit(solution)/shard_map/all_gather | solution.py:447
  32.1 17.7 %all-to-all-start.2 = ((bf16[8,64,128]{2,1,0:T(8,128)(2,1)}), bf16[8,64,128]{2,1,0:T(8,128)(2,1)S(1)}, u32[]{:S(2)}, u32[]{:S(2)}) async-start(bf16[8,64,128]{2,1,0:T(8,128)(2,1)} %get-tuple-element.28), calls=%async_computation.2 | async-start | bytes 262144 | tf_op jit(solution)/shard_map/all_to_all | solution.py:450
  46.6 31.7 %copy-start.8 = (s32[71]{0:T(128)}, s32[71]{0:T(128)S(1)}, u32[]{:S(2)}) copy-start(s32[71]{0:T(128)S(1)} %concatenate.3.refs_0_) | copy-start | bytes 856
  64.2 1.1 copy-start
  106.7 33.6 %copy-start.9 = (s32[71]{0:T(128)S(1)}, s32[71]{0:T(128)}, u32[]{:S(2)}) copy-start(s32[71]{0:T(128)} %copy-done.8) | copy-start | bytes 856
  106.7 13.4 %all-to-all-start.4 = ((bf16[4,320,128]{2,1,0:T(8,128)(2,1)}), bf16[4,320,128]{2,1,0:T(8,128)(2,1)S(1)}, u32[]{:S(2)}, u32[]{:S(2)}) async-start(bf16[4,320,128]{2,1,0:T(8,128)(2,1)} %get-tuple-element.32), calls=%async_computation.4 | async-start | bytes 655360 | tf_op jit(solution)/shard_map/all_to_all | solution.py:495
  110.8 73.3 %all-gather.9.cloned.1.call-start = ((), (), s32[]{:S(2)}) async-start(), calls=%async_computation.13 | async-start | bytes 2949120 | tf_op jit(solution)/shard_map/all_gather | solution.py:528
  130.3 53.9 %copy-start.1 = (bf16[128,5120]{1,0:T(8,128)(2,1)S(1)}, bf16[128,5120]{1,0:T(8,128)(2,1)}, u32[]{:S(2)}) copy-start(bf16[128,5120]{1,0:T(8,128)(2,1)} %copy-done) | copy-start | bytes 3932164
  166.2 27.3 %copy-start.4 = (bf16[256,1024]{1,0:T(8,128)(2,1)S(1)}, bf16[256,1024]{1,0:T(8,128)(2,1)}, u32[]{:S(2)}) copy-start(bf16[256,1024]{1,0:T(8,128)(2,1)} %patch_ref.1) | copy-start | bytes 1572868
  177.9 11.6 %all-to-all-start.10 = ((bf16[8,64,128]{2,1,0:T(8,128)(2,1)}), bf16[8,64,128]{2,1,0:T(8,128)(2,1)S(1)}, u32[]{:S(2)}, u32[]{:S(2)}) async-start(bf16[8,64,128]{2,1,0:T(8,128)(2,1)} %pick.1), calls=%async_computation.10 | async-start | bytes 262144 | tf_op jit(solution)/shard_map/all_to_all | solution.py:567
  184.2 1.7 copy-start.2
  189.4 7.7 %all-to-all-start.6 = ((bf16[4,64,128]{2,1,0:T(8,128)(2,1)}), bf16[4,64,128]{2,1,0:T(8,128)(2,1)S(1)}, u32[]{:S(2)}, u32[]{:S(2)}) async-start(bf16[4,64,128]{2,1,0:T(8,128)(2,1)} %proj_grad.1), calls=%async_computation.6 | async-start | bytes 131072 | tf_op jit(solution)/shard_map/all_to_all | solution.py:577
Sparse Core Ops, SparseCore 0:
  22.9 55.3 all-gather.4
  80.1 39.8 all-gather.6
  130.4 37.9 all-gather.8
